TPU v7x, 512 devices: a whole 4x8x8 slice. The times are simulated.
512 devices in a mesh: mem: 16 (over x, y_lo, core), ocn: 32 (over y_hi, z).
Axes of the slice: x: 4, y: 8 (y_hi: 4, y_lo: 2; y = y_hi * 2 + y_lo), z: 8, core: 2. Of those that a mesh axis runs over, the one named last changes fastest.
Arguments:
- panel: bfloat16 [65536, 1024], P('mem', 'ocn'), may hold values from -40 to 40
- ocean: bfloat16 [65536, 8192], P('mem', 'ocn'), may hold values from -100 to 100
- cutoff: int32 [16, 64], P('mem', 'ocn'), may hold values 0 or 1
- factor_index: int32 [16, 64], P('mem', 'ocn'), may hold values from 0 to 7
- factor_table: float32 [8], replicated, may hold values from 0.5 to 2
Outputs:
- inflated: float32 [1024, 8192], P('mem', 'ocn')
All inputs are finite; a program needn't handle non-finite values. No bound on the sum of `cutoff` on one device may be relied on, other than what follows from the above.
Results may differ from a plain program's by a relative error of at most 0.0003.
Values may be sent and summed in bfloat16 or wider, within the bound.
No kernel may reach another device: no remote copies, remote signals or barrier semaphores. Data moves between devices by JAX's collectives and lax.ppermute only.
A program may use at most 64 MiB of HBM per device.

v0:
```python
import jax
import jax.numpy as jnp
from jax import lax
from jax.sharding import PartitionSpec as P

TR = 64
TV = 128
NF = 8


def cross_rows(column_span, ocean):
    return lax.dot_general(
        column_span, ocean, (((0,), (0,)), ((), ())), preferred_element_type=jnp.float32
    )


def per_device(panel, ocean, cutoff, factor_index, factor_table):
    n_mem = lax.axis_size("mem")
    rows_all = panel.shape[1] * lax.axis_size("ocn")
    own_rows = rows_all // n_mem
    member_index = lax.axis_index("mem")
    members = panel.shape[0] * n_mem
    panel_f = panel.astype(jnp.float32)
    ocean_f = ocean.astype(jnp.float32)
    panel_sq = jnp.sum(panel_f * panel_f, axis=0)
    ocean_sq = jnp.sum(ocean_f * ocean_f, axis=0)
    panel_tot, colsq = lax.psum((panel_sq, ocean_sq), "mem")
    rowsq_all = lax.all_gather(panel_tot, "ocn", axis=0, tiled=True)
    rowsq = lax.dynamic_slice_in_dim(rowsq_all, member_index * own_rows, own_rows, 0)
    partial_value = cross_rows(lax.all_gather(panel, "ocn", axis=1, tiled=True), ocean)
    summed = lax.psum(partial_value, "mem")
    covsum = lax.dynamic_slice_in_dim(summed, member_index * own_rows, own_rows, 0)
    vx = rowsq / (members - 1.0) + 1e-06
    vy = colsq / (members - 1.0) + 1e-06
    corr = covsum / (members - 1.0) / jnp.sqrt(vx[:, None] * vy[None, :])
    picks = factor_index[..., None] == jnp.arange(NF, dtype=jnp.int32)
    weight = cutoff.astype(jnp.float32) * jnp.sum(
        jnp.where(picks, factor_table, jnp.float32(0.0)), axis=-1
    )
    row_tiles, col_tiles = weight.shape
    result = corr.reshape(row_tiles, TR, col_tiles, TV) * weight[:, None, :, None]
    return result.reshape(row_tiles * TR, col_tiles * TV)


def solution(mesh):
    in_specs = (P("mem", "ocn"), P("mem", "ocn"), P("mem", "ocn"), P("mem", "ocn"), P())
    out_specs = P("mem", "ocn")
    return jax.shard_map(
        per_device, mesh=mesh, in_specs=in_specs, out_specs=out_specs, check_vma=False
    )
```

profile of v0, /device:TPU:56, one launch (start us, length us, event | category | flops | bytes accessed | tf_op | source)
XLA Modules:
  0.0 293.4 jit_solution(591116939046002467)
XLA Ops:
  6.5 0.0 all-gather.2.cloned.1.call-start
  6.5 0.7 all-gather.2.cloned.1.call-update
  7.3 0.0 copy-start
  7.3 0.0 copy-start.1
  7.3 0.0 copy-start.2
  7.3 0.0 copy-start.3
  7.3 0.0 copy-start.4
  7.3 0.0 all-reduce.4.cloned.1.call-start
  7.4 145.7 %all-gather.2.cloned.1.call-done = bf16[4096,1024]{0,1:T(8,128)(2,1)} async-done(((bf16[4096,32]{0,1:T(8,128)(2,1)}), bf16[4096,1024]{0,1:T(8,128)(2,1)}) %all-gather.2.cloned.1.call-update) | async-done | bytes 8388624 | tf_op jit(solution)/shard_map/all_gather | solution.py:30
  153.1 7.4 %fusion.2 = f32[1024,256]{1,0:T(8,128)} fusion(bf16[4096,1024]{0,1:T(8,128)(2,1)} %all-gather.2.cloned.1.call-done, bf16[4096,256]{1,0:T(8,128)(2,1)} %param.6), kind=kOutput, calls=%fused_computation.10 | convolution fusion | flops 2147483648 | bytes 11534336 | tf_op jit(solution)/shard_map/dot_general | solution.py:12
  160.5 0.0 all-reduce.4.cloned.1.call-update
  160.5 0.0 copy-done
  160.5 0.6 multiply_reduce_fusion
  161.1 1.3 dynamic-slice
  163.0 0.0 copy-done.1
  163.0 0.2 multiply_reduce_fusion.1
  163.2 25.9 %all-reduce.1 = (f32[256]{0:T(256)S(1)}, f32[32]{0:T(128)S(1)}) all-reduce(f32[256]{0:T(256)S(1)} %multiply_reduce_fusion, f32[32]{0:T(128)S(1)} %multiply_reduce_fusion.1), channel_id=1, replica_groups=mesh['mem'=16,'ocn'=32] {'mem'}, use_global_device_ids=true, to_apply=%region_4.0 | all-reduce | flops 288 | bytes 2304 | tf_op jit(solution)/shard_map/psum | solution.py:27
  189.1 0.2 dynamic-update-slice
  189.3 69.7 %all-reduce = f32[1024]{0:T(1024)S(1)} all-reduce(f32[1024]{0:T(1024)S(1)} %dynamic-update-slice), channel_id=1, replica_groups=mesh['mem'=16,'ocn'=32] {'ocn'}, use_global_device_ids=true, to_apply=%add | all-reduce | flops 1024 | bytes 8192
  259.1 0.1 multiply_add_fusion.1
  259.2 0.0 copy-done.2
  259.2 0.0 copy-done.3
  259.2 0.2 fusion
  259.3 0.0 copy-done.4
  259.4 0.1 broadcast_bitcast_fusion
  259.4 25.6 %all-reduce.4.cloned.1.call-done = f32[1024,256]{1,0:T(8,128)} async-done(((f32[1024,256]{1,0:T(8,128)}), f32[1024,256]{1,0:T(8,128)}) %all-reduce.4.cloned.1.call-update) | async-done | bytes 1048592 | tf_op jit(solution)/shard_map/psum | solution.py:31
  285.0 1.6 multiply_multiply_fusion
  (3 shorter events, 0.0 us)
Async XLA Ops:
  6.5 146.6 %all-gather.2.cloned.1.call-start = ((), (), s32[]{:S(2)}) async-start(), calls=%async_computation | async-start | bytes 8650752 | tf_op jit(solution)/shard_map/all_gather | solution.py:30
  7.3 153.2 %copy-start = (bf16[4096,256]{1,0:T(8,128)(2,1)S(1)}, bf16[4096,256]{1,0:T(8,128)(2,1)}, u32[]{:S(2)}) copy-start(bf16[4096,256]{1,0:T(8,128)(2,1)} %param.6) | copy-start | bytes 6291460
  7.3 155.7 %copy-start.1 = (bf16[4096,32]{0,1:T(8,128)(2,1)S(1)}, bf16[4096,32]{0,1:T(8,128)(2,1)}, u32[]{:S(2)}) copy-start(bf16[4096,32]{0,1:T(8,128)(2,1)} %param.5) | copy-start | bytes 786436
  7.3 251.9 %copy-start.2 = (f32[8]{0:T(128)S(1)}, f32[8]{0:T(128)}, u32[]{:S(2)}) copy-start(f32[8]{0:T(128)} %param.9) | copy-start | bytes 100
  7.3 251.9 %copy-start.3 = (s32[1,2]{1,0:T(1,128)S(1)}, s32[1,2]{1,0:T(1,128)}, u32[]{:S(2)}) copy-start(s32[1,2]{1,0:T(1,128)} %param.8) | copy-start | bytes 28
  7.3 252.1 %copy-start.4 = (s32[1,2]{1,0:T(1,128)S(1)}, s32[1,2]{1,0:T(1,128)}, u32[]{:S(2)}) copy-start(s32[1,2]{1,0:T(1,128)} %param.7) | copy-start | bytes 28
  7.3 277.7 %all-reduce.4.cloned.1.call-start = ((), (), s32[]{:S(2)}) async-start(), calls=%async_computation.1 | async-start | bytes 2097152 | tf_op jit(solution)/shard_map/psum | solution.py:31
Sparse Core Ops, SparseCore 0:
  10.5 142.5 all-gather.1
  160.6 124.3 all-reduce.3
where the time goes:
time: 297 us; the launch traced here: 293 us
  waiting for transfers between devices  172 us (58%)
  blocking collectives  95.7 us (32%)
  between operations  14.1 us (5%)
  matrix products  7.38 us (2%)
    all_gather x1, waiting for transfers between devices, per_device(): lax.all_gather(panel, 'ocn', axis=1, tiled=True)  146 us
    unnamed x1, blocking collectives  69.7 us
    psum x1, blocking collectives, per_device(): panel_tot, colsq = lax.psum((panel_sq, ocean_sq), 'mem')  25.9 us
    psum x1, waiting for transfers between devices, per_device(): summed = lax.psum(partial_value, 'mem')  25.6 us
    dot_general x1, matrix products, cross_rows(): lax.dot_general(column_span, ocean, (((0,), (0,)), ((), ())), preferred_e...  7.38 us
  transfers between devices with their start and end apart: 2, of which 2 were waited for; matrix products, arithmetic and copies ran while one was open for 1% of the time, Pallas kernels for 0%

commit v1 on v0

v1 whole, which is shorter than its diff:
```python
import jax
import jax.numpy as jnp
from jax import lax
from jax.experimental import pallas as pl
from jax.experimental.pallas import tpu as pltpu
from jax.sharding import PartitionSpec as P

TR = 64
TV = 128
NZ = 8
NY = 4
EXTRA = 8


def z_shift(x, d):
    perm = [(o, (o // NZ) * NZ + (o % NZ + d) % NZ) for o in range(NY * NZ)]
    return lax.ppermute(x, "ocn", perm)


def y_shift(x, d):
    perm = [(o, ((o // NZ + d) % NY) * NZ + o % NZ) for o in range(NY * NZ)]
    return lax.ppermute(x, "ocn", perm)


def z_ring(x, n_up, n_down):
    got = []
    up = down = x
    for s in range(1, max(n_up, n_down) + 1):
        if s <= n_up:
            up = z_shift(up, 1)
            got.append((up, -s))
        if s <= n_down:
            down = z_shift(down, -1)
            got.append((down, s))
    return got


def cross_kernel(places, *refs):
    n = len(places)
    blocks, ocean_ref, out_ref, rows_ref, sem = refs[:n], refs[n], refs[n + 1], refs[n + 2], refs[n + 3]
    o = lax.axis_index("ocn")
    y, z = o // NZ, lax.rem(o, NZ)
    copies = []
    for ref, (groups, dz) in zip(blocks, places):
        per = ref.shape[0] // len(groups)
        for g, dy in enumerate(groups):
            origin = lax.rem(y + (dy + NY), NY) * NZ + lax.rem(z + (dz + NZ), NZ)
            start = pl.multiple_of(origin * per, per)
            copies.append(
                pltpu.make_async_copy(
                    ref.at[pl.ds(g * per, per)], rows_ref.at[pl.ds(start, per)], sem.at[len(copies)]
                )
            )
    for c in copies:
        c.start()
    ocean = ocean_ref[...]
    ocean_f = ocean.astype(jnp.float32)
    colsq = jnp.sum(ocean_f * ocean_f, axis=0, keepdims=True)
    for c in copies:
        c.wait()
    n_own = out_ref.shape[0]
    own = rows_ref.shape[0] // n_own
    per_tile = 4
    line = lax.broadcasted_iota(jnp.int32, (EXTRA, ocean.shape[1]), 0)
    eye = lax.broadcasted_iota(jnp.int32, (own, 128), 0) == lax.broadcasted_iota(jnp.int32, (own, 128), 1)

    @pl.loop(0, n_own // per_tile)
    def _(t):
        first = pl.multiple_of(t * (per_tile * own), per_tile * own)
        tile = rows_ref[pl.ds(first, per_tile * own), :]
        cov = jnp.dot(tile, ocean_ref[...], preferred_element_type=jnp.float32)
        tile_f = tile.astype(jnp.float32)
        rowsq = jnp.sum(tile_f * tile_f, axis=1, keepdims=True)
        for k in range(per_tile):
            part = slice(k * own, (k + 1) * own)
            across = jnp.sum(jnp.where(eye, rowsq[part], 0.0), axis=0, keepdims=True)
            across = jnp.concatenate([across, jnp.zeros_like(across)], axis=1)
            out_ref[t * per_tile + k, :own, :] = cov[part]
            out_ref[t * per_tile + k, own:, :] = jnp.where(line == 0, across, jnp.where(line == 1, colsq, 0.0))


def cross(pieces, ocean, rows_all, n_mem):
    places = [(groups, dz) for _, groups, dz in pieces]
    n_copies = sum(len(groups) for groups, _ in places)
    members, cols = ocean.shape
    own = rows_all // n_mem
    return pl.pallas_call(
        lambda *refs: cross_kernel(places, *refs),
        out_shape=jax.ShapeDtypeStruct((n_mem, own + EXTRA, cols), jnp.float32),
        in_specs=[pl.BlockSpec(memory_space=pl.ANY)] * len(pieces) + [pl.BlockSpec(memory_space=pltpu.VMEM)],
        out_specs=pl.BlockSpec(memory_space=pltpu.VMEM),
        scratch_shapes=[pltpu.VMEM((rows_all, members), jnp.bfloat16), pltpu.SemaphoreType.DMA((n_copies,))],
        compiler_params=pltpu.CompilerParams(vmem_limit_bytes=32 * 1024 * 1024),
        cost_estimate=pl.CostEstimate(
            flops=2 * rows_all * members * cols, bytes_accessed=2 * members * (rows_all + cols), transcendentals=0
        ),
    )(*[a for a, _, _ in pieces], ocean)


def finish_kernel(members, parts_ref, cutoff_ref, index_ref, table_ref, out_ref):
    own, cols = out_ref.shape
    total = jnp.sum(parts_ref[...], axis=0)
    eye = lax.broadcasted_iota(jnp.int32, (own, 128), 0) == lax.broadcasted_iota(jnp.int32, (own, 128), 1)
    rowsq = jnp.sum(jnp.where(eye, total[own : own + 1, :128], 0.0), axis=1, keepdims=True)
    vx = rowsq / (members - 1.0) + 1e-06
    vy = total[own + 1 : own + 2] / (members - 1.0) + 1e-06
    corr = total[:own] / (members - 1.0) / jnp.sqrt(vx * vy)
    for i in range(own // TR):
        for j in range(cols // TV):
            weight = cutoff_ref[i, j].astype(jnp.float32) * table_ref[index_ref[i, j]]
            tile = (slice(i * TR, (i + 1) * TR), slice(j * TV, (j + 1) * TV))
            out_ref[tile] = corr[tile] * weight


def per_device(panel, ocean, cutoff, factor_index, factor_table):
    n_mem = lax.axis_size("mem")
    rows_all = panel.shape[1] * lax.axis_size("ocn")
    own_rows = rows_all // n_mem
    members = panel.shape[0] * n_mem
    mine = panel.T
    from_below = y_shift(mine, 1)
    from_above = y_shift(mine, -1)
    from_across = y_shift(mine, 2)
    first = jnp.concatenate([mine, from_below], axis=0)
    second = jnp.concatenate([from_above, from_across], axis=0)
    pieces = [(first, (0, -1), 0), (second, (1, 2), 0)]
    pieces += [(a, (0, -1), dz) for a, dz in z_ring(first, 4, 3)]
    pieces += [(a, (1, 2), dz) for a, dz in z_ring(second, 3, 4)]
    parts = cross(pieces, ocean, rows_all, n_mem)
    parts = lax.all_to_all(parts, "mem", split_axis=0, concat_axis=0, tiled=True)
    return pl.pallas_call(
        lambda *refs: finish_kernel(members, *refs),
        out_shape=jax.ShapeDtypeStruct((own_rows, ocean.shape[1]), jnp.float32),
        in_specs=[pl.BlockSpec(memory_space=pltpu.VMEM)] + [pl.BlockSpec(memory_space=pltpu.SMEM)] * 3,
        out_specs=pl.BlockSpec(memory_space=pltpu.VMEM),
        compiler_params=pltpu.CompilerParams(vmem_limit_bytes=16 * 1024 * 1024),
    )(parts, cutoff, factor_index, factor_table)


def solution(mesh):
    in_specs = (P("mem", "ocn"), P("mem", "ocn"), P("mem", "ocn"), P("mem", "ocn"), P())
    out_specs = P("mem", "ocn")
    return jax.shard_map(
        per_device, mesh=mesh, in_specs=in_specs, out_specs=out_specs, check_vma=False
    )
```

time: 297 us -> 153 us (0.52)
  waiting for transfers between devices: 172 us -> 43.1 us
  starting transfers between devices: 0.04 us -> 73 us
  blocking collectives: 95.7 us -> 28.2 us
  between operations: 14.1 us -> 0.23 us
  matrix products: 7.38 us -> 0 us
  Pallas kernels: 0 us -> 5.58 us
    all_gather x1 -> x0, waiting for transfers between devices: 146 us -> none  [per_device(): lax.all_gather(panel, 'ocn', axis=1, tiled=True)]
    ppermute x0 -> x17, starting transfers between devices: none -> 73 us  [the longest x14 61.4 us: z_shift(): return lax.ppermute(x, 'ocn', perm)]
    unnamed x1 -> x0, blocking collectives: 69.7 us -> none
    ppermute x0 -> x17, waiting for transfers between devices: none -> 43.1 us  [the longest x14 35 us: z_shift(): return lax.ppermute(x, 'ocn', perm)]
    all_to_all x0 -> x1, blocking collectives: none -> 28.2 us  [per_device(): lax.all_to_all(parts, 'mem', split_axis=0, concat_axis=0, tiled=True)]
    psum x1 -> x0, blocking collectives: 25.9 us -> none  [per_device(): panel_tot, colsq = lax.psum((panel_sq, ocean_sq), 'mem')]
    psum x1 -> x0, waiting for transfers between devices: 25.6 us -> none  [per_device(): summed = lax.psum(partial_value, 'mem')]
    dot_general x1 -> x0, matrix products: 7.38 us -> none  [cross_rows(): lax.dot_general(column_span, ocean, (((0,), (0,)), ((), ())), preferred_e...]
  transfers between devices with their start and end apart: 2 -> 17, of which waited for: 2 -> 12; matrix products, arithmetic and copies ran while one was open for 1% -> 1% of each run, Pallas kernels for 0% -> 0%
where the time goes in v1:
time: 153 us; the launch traced here: 151 us
  starting transfers between devices  73 us (48%)
  waiting for transfers between devices  43.1 us (28%)
  blocking collectives  28.2 us (18%)
  Pallas kernels  5.58 us (4%)
    ppermute x14, starting transfers between devices, z_shift(): return lax.ppermute(x, 'ocn', perm)  61.4 us
    ppermute x14, waiting for transfers between devices, z_shift(): return lax.ppermute(x, 'ocn', perm)  35 us
    all_to_all x1, blocking collectives, per_device(): lax.all_to_all(parts, 'mem', split_axis=0, concat_axis=0, tiled=True)  28.2 us
    ppermute x3, starting transfers between devices, y_shift(): return lax.ppermute(x, 'ocn', perm)  11.6 us
    ppermute x3, waiting for transfers between devices, y_shift(): return lax.ppermute(x, 'ocn', perm)  8.13 us
    pallas_call x1, Pallas kernels, cross(): pl.pallas_call(lambda *refs: cross_kernel(places, *refs), out_shape=jax.S...  4.27 us
  transfers between devices with their start and end apart: 17, of which 12 were waited for; matrix products, arithmetic and copies ran while one was open for 1% of the time, Pallas kernels for 0%

profile of v1, /device:TPU:56, one launch (start us, length us, event | category | flops | bytes accessed | tf_op | source)
XLA Modules:
  0.0 151.2 jit_solution(10487667756896005414)
XLA Ops:
  0.0 2.8 %collective-permute-start = (bf16[32,4096]{1,0:T(8,128)(2,1)}, bf16[32,4096]{1,0:T(8,128)(2,1)S(1)}, u32[]{:S(2)}, u32[]{:S(2)}) collective-permute-start(bf16[32,4096]{1,0:T(8,128)(2,1)} %bitcast.1), channel_id=1, source_target_pairs={{0,8},{1,9},{2,10},{3,11},{4,12},{5,13},{6,14},{7,15},{8,16},{9,17... | collective-permute-start | bytes 786440 | tf_op jit(solution)/shard_map/ppermute | solution.py:22
  2.8 6.8 %collective-permute-start.2 = (bf16[32,4096]{1,0:T(8,128)(2,1)}, bf16[32,4096]{1,0:T(8,128)(2,1)S(1)}, u32[]{:S(2)}, u32[]{:S(2)}) collective-permute-start(bf16[32,4096]{1,0:T(8,128)(2,1)} %bitcast.2), channel_id=1, source_target_pairs={{0,16},{1,17},{2,18},{3,19},{4,20},{5,21},{6,22},{7,23},{8,24},{9,... | collective-permute-start | bytes 786440 | tf_op jit(solution)/shard_map/ppermute | solution.py:22
  9.7 1.9 %collective-permute-start.1 = (bf16[32,4096]{1,0:T(8,128)(2,1)}, bf16[32,4096]{1,0:T(8,128)(2,1)S(1)}, u32[]{:S(2)}, u32[]{:S(2)}) collective-permute-start(bf16[32,4096]{1,0:T(8,128)(2,1)} %bitcast.3), channel_id=1, source_target_pairs={{0,24},{1,25},{2,26},{3,27},{4,28},{5,29},{6,30},{7,31},{8,0},{9,1... | collective-permute-start | bytes 786440 | tf_op jit(solution)/shard_map/ppermute | solution.py:22
  11.6 5.0 %collective-permute-done = bf16[32,4096]{1,0:T(8,128)(2,1)S(1)} collective-permute-done((bf16[32,4096]{1,0:T(8,128)(2,1)}, bf16[32,4096]{1,0:T(8,128)(2,1)S(1)}, u32[]{:S(2)}, u32[]{:S(2)}) %collective-permute-start) | collective-permute-done | bytes 262176 | tf_op jit(solution)/shard_map/ppermute | solution.py:22
  16.6 1.0 pad_maximum_fusion.refs_0_
  17.5 7.1 %collective-permute-start.3 = (bf16[64,4096]{1,0:T(8,128)(2,1)S(1)}, bf16[64,4096]{1,0:T(8,128)(2,1)S(1)}, u32[]{:S(2)}, u32[]{:S(2)}) collective-permute-start(bf16[64,4096]{1,0:T(8,128)(2,1)S(1)} %pad_maximum_fusion.refs_0_), channel_id=1, source_target_pairs={{0,1},{1,2},{2,3},{3,4},{4,5},{5,6},{6,7},{7,0},{8,9},{9,10},{10,1... | collective-permute-start | bytes 1572872 | tf_op jit(solution)/shard_map/ppermute | solution.py:17
  24.6 3.2 %collective-permute-done.1 = bf16[32,4096]{1,0:T(8,128)(2,1)S(1)} collective-permute-done((bf16[32,4096]{1,0:T(8,128)(2,1)}, bf16[32,4096]{1,0:T(8,128)(2,1)S(1)}, u32[]{:S(2)}, u32[]{:S(2)}) %collective-permute-start.1) | collective-permute-done | bytes 262176 | tf_op jit(solution)/shard_map/ppermute | solution.py:22
  27.9 10.9 %collective-permute-start.11 = (bf16[64,4096]{1,0:T(8,128)(2,1)S(1)}, bf16[64,4096]{1,0:T(8,128)(2,1)S(1)}, u32[]{:S(2)}, u32[]{:S(2)}) collective-permute-start(bf16[64,4096]{1,0:T(8,128)(2,1)S(1)} %constant_dynamic-update-slice_fusion.refs_1_), channel_id=1, source_target_pairs={{0,7},{1,0},{2,1},{3,2},{4,3},{5,4},{6,5},{7,6},{8,15},{9,8},{10,9... | collective-permute-start | bytes 1572872 | tf_op jit(solution)/shard_map/ppermute | solution.py:17
  38.8 2.5 %collective-permute-start.4 = (bf16[64,4096]{1,0:T(8,128)(2,1)S(1)}, bf16[64,4096]{1,0:T(8,128)(2,1)S(1)}, u32[]{:S(2)}, u32[]{:S(2)}) collective-permute-start(bf16[64,4096]{1,0:T(8,128)(2,1)S(1)} %pad_maximum_fusion.refs_0_), channel_id=1, source_target_pairs={{0,7},{1,0},{2,1},{3,2},{4,3},{5,4},{6,5},{7,6},{8,15},{9,8},{10,9... | collective-permute-start | bytes 1572872 | tf_op jit(solution)/shard_map/ppermute | solution.py:17
  41.3 3.4 %collective-permute-start.10 = (bf16[64,4096]{1,0:T(8,128)(2,1)S(1)}, bf16[64,4096]{1,0:T(8,128)(2,1)S(1)}, u32[]{:S(2)}, u32[]{:S(2)}) collective-permute-start(bf16[64,4096]{1,0:T(8,128)(2,1)S(1)} %constant_dynamic-update-slice_fusion.refs_1_), channel_id=1, source_target_pairs={{0,1},{1,2},{2,3},{3,4},{4,5},{5,6},{6,7},{7,0},{8,9},{9,10},{10,1... | collective-permute-start | bytes 1572872 | tf_op jit(solution)/shard_map/ppermute | solution.py:17
  44.7 1.9 %collective-permute-start.5 = (bf16[64,4096]{1,0:T(8,128)(2,1)S(1)}, bf16[64,4096]{1,0:T(8,128)(2,1)S(1)}, u32[]{:S(2)}, u32[]{:S(2)}) collective-permute-start(bf16[64,4096]{1,0:T(8,128)(2,1)S(1)} %collective-permute-done.3.refs_2_), channel_id=1, source_target_pairs={{0,1},{1,2},{2,3},{3,4},{4,5},{5,6},{6,7},{7,0},{8,9},{9,10},{10,1... | collective-permute-start | bytes 1572872 | tf_op jit(solution)/shard_map/ppermute | solution.py:17
  46.6 4.5 %collective-permute-done.11.refs_10_ = bf16[64,4096]{1,0:T(8,128)(2,1)S(1)} collective-permute-done((bf16[64,4096]{1,0:T(8,128)(2,1)S(1)}, bf16[64,4096]{1,0:T(8,128)(2,1)S(1)}, u32[]{:S(2)}, u32[]{:S(2)}) %collective-permute-start.11) | collective-permute-done | bytes 524320 | tf_op jit(solution)/shard_map/ppermute | solution.py:17
  51.2 5.6 %collective-permute-start.13 = (bf16[64,4096]{1,0:T(8,128)(2,1)S(1)}, bf16[64,4096]{1,0:T(8,128)(2,1)S(1)}, u32[]{:S(2)}, u32[]{:S(2)}) collective-permute-start(bf16[64,4096]{1,0:T(8,128)(2,1)S(1)} %collective-permute-done.11.refs_10_), channel_id=1, source_target_pairs={{0,7},{1,0},{2,1},{3,2},{4,3},{5,4},{6,5},{7,6},{8,15},{9,8},{10,9... | collective-permute-start | bytes 1572872 | tf_op jit(solution)/shard_map/ppermute | solution.py:17
  56.7 5.6 %collective-permute-done.4.refs_3_ = bf16[64,4096]{1,0:T(8,128)(2,1)S(1)} collective-permute-done((bf16[64,4096]{1,0:T(8,128)(2,1)S(1)}, bf16[64,4096]{1,0:T(8,128)(2,1)S(1)}, u32[]{:S(2)}, u32[]{:S(2)}) %collective-permute-start.4) | collective-permute-done | bytes 524320 | tf_op jit(solution)/shard_map/ppermute | solution.py:17
  62.4 5.6 %collective-permute-start.6 = (bf16[64,4096]{1,0:T(8,128)(2,1)S(1)}, bf16[64,4096]{1,0:T(8,128)(2,1)S(1)}, u32[]{:S(2)}, u32[]{:S(2)}) collective-permute-start(bf16[64,4096]{1,0:T(8,128)(2,1)S(1)} %collective-permute-done.4.refs_3_), channel_id=1, source_target_pairs={{0,7},{1,0},{2,1},{3,2},{4,3},{5,4},{6,5},{7,6},{8,15},{9,8},{10,9... | collective-permute-start | bytes 1572872 | tf_op jit(solution)/shard_map/ppermute | solution.py:17
  68.0 1.9 %collective-permute-start.12 = (bf16[64,4096]{1,0:T(8,128)(2,1)S(1)}, bf16[64,4096]{1,0:T(8,128)(2,1)S(1)}, u32[]{:S(2)}, u32[]{:S(2)}) collective-permute-start(bf16[64,4096]{1,0:T(8,128)(2,1)S(1)} %collective-permute-done.10.refs_9_), channel_id=1, source_target_pairs={{0,1},{1,2},{2,3},{3,4},{4,5},{5,6},{6,7},{7,0},{8,9},{9,10},{10,1... | collective-permute-start | bytes 1572872 | tf_op jit(solution)/shard_map/ppermute | solution.py:17
  69.9 1.9 %collective-permute-start.7 = (bf16[64,4096]{1,0:T(8,128)(2,1)S(1)}, bf16[64,4096]{1,0:T(8,128)(2,1)S(1)}, u32[]{:S(2)}, u32[]{:S(2)}) collective-permute-start(bf16[64,4096]{1,0:T(8,128)(2,1)S(1)} %collective-permute-done.5.refs_4_), channel_id=1, source_target_pairs={{0,1},{1,2},{2,3},{3,4},{4,5},{5,6},{6,7},{7,0},{8,9},{9,10},{10,1... | collective-permute-start | bytes 1572872 | tf_op jit(solution)/shard_map/ppermute | solution.py:17
  71.9 1.8 %collective-permute-done.13.refs_12_ = bf16[64,4096]{1,0:T(8,128)(2,1)S(1)} collective-permute-done((bf16[64,4096]{1,0:T(8,128)(2,1)S(1)}, bf16[64,4096]{1,0:T(8,128)(2,1)S(1)}, u32[]{:S(2)}, u32[]{:S(2)}) %collective-permute-start.13) | collective-permute-done | bytes 524320 | tf_op jit(solution)/shard_map/ppermute | solution.py:17
  73.6 5.6 %collective-permute-start.15 = (bf16[64,4096]{1,0:T(8,128)(2,1)S(1)}, bf16[64,4096]{1,0:T(8,128)(2,1)S(1)}, u32[]{:S(2)}, u32[]{:S(2)}) collective-permute-start(bf16[64,4096]{1,0:T(8,128)(2,1)S(1)} %collective-permute-done.13.refs_12_), channel_id=1, source_target_pairs={{0,7},{1,0},{2,1},{3,2},{4,3},{5,4},{6,5},{7,6},{8,15},{9,8},{10,9... | collective-permute-start | bytes 1572872 | tf_op jit(solution)/shard_map/ppermute | solution.py:17
  79.2 5.6 %collective-permute-done.6.refs_5_ = bf16[64,4096]{1,0:T(8,128)(2,1)S(1)} collective-permute-done((bf16[64,4096]{1,0:T(8,128)(2,1)S(1)}, bf16[64,4096]{1,0:T(8,128)(2,1)S(1)}, u32[]{:S(2)}, u32[]{:S(2)}) %collective-permute-start.6) | collective-permute-done | bytes 524320 | tf_op jit(solution)/shard_map/ppermute | solution.py:17
  84.9 5.6 %collective-permute-start.8 = (bf16[64,4096]{1,0:T(8,128)(2,1)S(1)}, bf16[64,4096]{1,0:T(8,128)(2,1)S(1)}, u32[]{:S(2)}, u32[]{:S(2)}) collective-permute-start(bf16[64,4096]{1,0:T(8,128)(2,1)S(1)} %collective-permute-done.6.refs_5_), channel_id=1, source_target_pairs={{0,7},{1,0},{2,1},{3,2},{4,3},{5,4},{6,5},{7,6},{8,15},{9,8},{10,9... | collective-permute-start | bytes 1572872 | tf_op jit(solution)/shard_map/ppermute | solution.py:17
  90.5 1.9 %collective-permute-start.14 = (bf16[64,4096]{1,0:T(8,128)(2,1)S(1)}, bf16[64,4096]{1,0:T(8,128)(2,1)S(1)}, u32[]{:S(2)}, u32[]{:S(2)}) collective-permute-start(bf16[64,4096]{1,0:T(8,128)(2,1)S(1)} %collective-permute-done.12.refs_11_), channel_id=1, source_target_pairs={{0,1},{1,2},{2,3},{3,4},{4,5},{5,6},{6,7},{7,0},{8,9},{9,10},{10,1... | collective-permute-start | bytes 1572872 | tf_op jit(solution)/shard_map/ppermute | solution.py:17
  92.4 1.1 collective-permute-done.7.refs_6_
  93.5 1.9 %collective-permute-start.9 = (bf16[64,4096]{1,0:T(8,128)(2,1)S(1)}, bf16[64,4096]{1,0:T(8,128)(2,1)S(1)}, u32[]{:S(2)}, u32[]{:S(2)}) collective-permute-start(bf16[64,4096]{1,0:T(8,128)(2,1)S(1)} %collective-permute-done.7.refs_6_), channel_id=1, source_target_pairs={{0,1},{1,2},{2,3},{3,4},{4,5},{5,6},{6,7},{7,0},{8,9},{9,10},{10,1... | collective-permute-start | bytes 1572872 | tf_op jit(solution)/shard_map/ppermute | solution.py:17
  96.1 5.6 %collective-permute-start.16 = (bf16[64,4096]{1,0:T(8,128)(2,1)S(1)}, bf16[64,4096]{1,0:T(8,128)(2,1)S(1)}, u32[]{:S(2)}, u32[]{:S(2)}) collective-permute-start(bf16[64,4096]{1,0:T(8,128)(2,1)S(1)} %collective-permute-done.15.refs_14_), channel_id=1, source_target_pairs={{0,7},{1,0},{2,1},{3,2},{4,3},{5,4},{6,5},{7,6},{8,15},{9,8},{10,9... | collective-permute-start | bytes 1572872 | tf_op jit(solution)/shard_map/ppermute | solution.py:17
  101.7 5.6 %collective-permute-done.8.refs_7_ = bf16[64,4096]{1,0:T(8,128)(2,1)S(1)} collective-permute-done((bf16[64,4096]{1,0:T(8,128)(2,1)S(1)}, bf16[64,4096]{1,0:T(8,128)(2,1)S(1)}, u32[]{:S(2)}, u32[]{:S(2)}) %collective-permute-start.8) | collective-permute-done | bytes 524320 | tf_op jit(solution)/shard_map/ppermute | solution.py:17
  107.3 1.1 collective-permute-done.14.refs_13_
  108.4 7.5 %collective-permute-done.9.refs_8_ = bf16[64,4096]{1,0:T(8,128)(2,1)S(1)} collective-permute-done((bf16[64,4096]{1,0:T(8,128)(2,1)S(1)}, bf16[64,4096]{1,0:T(8,128)(2,1)S(1)}, u32[]{:S(2)}, u32[]{:S(2)}) %collective-permute-start.9) | collective-permute-done | bytes 524320 | tf_op jit(solution)/shard_map/ppermute | solution.py:17
  115.9 1.4 collective-permute-done.16.refs_15_
  117.3 4.3 %shard_map.55 = f32[16,72,256]{2,1,0:T(8,128)S(1)} custom-call(bf16[64,4096]{1,0:T(8,128)(2,1)S(1)} %pad_maximum_fusion.refs_0_, bf16[64,4096]{1,0:T(8,128)(2,1)S(1)} %constant_dynamic-update-slice_fusion.refs_1_, bf16[64,4096]{1,0:T(8,128)(2,1)S(1)} %collective-permute-done.3.refs_2_, bf16[64,4096]{1,0:T(8,128)(2,1)S(1)} %collective-permute-done.4.refs_3_, ...), custom_call_target="tpu_custom_call" | custom-call | flops 2147483648 | bytes 10485760 | tf_op jit(solution)/shard_map/pallas_call | solution.py:87
  121.6 28.2 %all_to_all.5.refs_0_ = f32[16,72,256]{2,1,0:T(8,128)S(1)} all-to-all(f32[16,72,256]{2,1,0:T(8,128)S(1)} %shard_map.55), channel_id=1, replica_groups=mesh['mem'=16,'ocn'=32] {'mem'}, dimensions={0} | all-to-all | bytes 2359296 | tf_op jit(solution)/shard_map/all_to_all | solution.py:130
  149.9 1.3 shard_map.56
  (16 shorter events, 0.8 us)
Async XLA Ops:
  0.0 117.3 %copy-start = (bf16[4096,256]{1,0:T(8,128)(2,1)S(1)}, bf16[4096,256]{1,0:T(8,128)(2,1)}, u32[]{:S(2)}) copy-start(bf16[4096,256]{1,0:T(8,128)(2,1)} %refs_16_.1) | copy-start | bytes 6291460
  0.0 16.6 %collective-permute-start = (bf16[32,4096]{1,0:T(8,128)(2,1)}, bf16[32,4096]{1,0:T(8,128)(2,1)S(1)}, u32[]{:S(2)}, u32[]{:S(2)}) collective-permute-start(bf16[32,4096]{1,0:T(8,128)(2,1)} %bitcast.1), channel_id=1, source_target_pairs={{0,8},{1,9},{2,10},{3,11},{4,12},{5,13},{6,14},{7,15},{8,16},{9,17... | collective-permute-start | bytes 786440 | tf_op jit(solution)/shard_map/ppermute | solution.py:22
  2.8 25.0 %collective-permute-start.2 = (bf16[32,4096]{1,0:T(8,128)(2,1)}, bf16[32,4096]{1,0:T(8,128)(2,1)S(1)}, u32[]{:S(2)}, u32[]{:S(2)}) collective-permute-start(bf16[32,4096]{1,0:T(8,128)(2,1)} %bitcast.2), channel_id=1, source_target_pairs={{0,16},{1,17},{2,18},{3,19},{4,20},{5,21},{6,22},{7,23},{8,24},{9,... | collective-permute-start | bytes 786440 | tf_op jit(solution)/shard_map/ppermute | solution.py:22
  9.7 18.2 %collective-permute-start.1 = (bf16[32,4096]{1,0:T(8,128)(2,1)}, bf16[32,4096]{1,0:T(8,128)(2,1)S(1)}, u32[]{:S(2)}, u32[]{:S(2)}) collective-permute-start(bf16[32,4096]{1,0:T(8,128)(2,1)} %bitcast.3), channel_id=1, source_target_pairs={{0,24},{1,25},{2,26},{3,27},{4,28},{5,29},{6,30},{7,31},{8,0},{9,1... | collective-permute-start | bytes 786440 | tf_op jit(solution)/shard_map/ppermute | solution.py:22
  17.5 27.1 %collective-permute-start.3 = (bf16[64,4096]{1,0:T(8,128)(2,1)S(1)}, bf16[64,4096]{1,0:T(8,128)(2,1)S(1)}, u32[]{:S(2)}, u32[]{:S(2)}) collective-permute-start(bf16[64,4096]{1,0:T(8,128)(2,1)S(1)} %pad_maximum_fusion.refs_0_), channel_id=1, source_target_pairs={{0,1},{1,2},{2,3},{3,4},{4,5},{5,6},{6,7},{7,0},{8,9},{9,10},{10,1... | collective-permute-start | bytes 1572872 | tf_op jit(solution)/shard_map/ppermute | solution.py:17
  27.9 23.3 %collective-permute-start.11 = (bf16[64,4096]{1,0:T(8,128)(2,1)S(1)}, bf16[64,4096]{1,0:T(8,128)(2,1)S(1)}, u32[]{:S(2)}, u32[]{:S(2)}) collective-permute-start(bf16[64,4096]{1,0:T(8,128)(2,1)S(1)} %constant_dynamic-update-slice_fusion.refs_1_), channel_id=1, source_target_pairs={{0,7},{1,0},{2,1},{3,2},{4,3},{5,4},{6,5},{7,6},{8,15},{9,8},{10,9... | collective-permute-start | bytes 1572872 | tf_op jit(solution)/shard_map/ppermute | solution.py:17
  38.8 23.6 %collective-permute-start.4 = (bf16[64,4096]{1,0:T(8,128)(2,1)S(1)}, bf16[64,4096]{1,0:T(8,128)(2,1)S(1)}, u32[]{:S(2)}, u32[]{:S(2)}) collective-permute-start(bf16[64,4096]{1,0:T(8,128)(2,1)S(1)} %pad_maximum_fusion.refs_0_), channel_id=1, source_target_pairs={{0,7},{1,0},{2,1},{3,2},{4,3},{5,4},{6,5},{7,6},{8,15},{9,8},{10,9... | collective-permute-start | bytes 1572872 | tf_op jit(solution)/shard_map/ppermute | solution.py:17
  41.3 26.7 %collective-permute-start.10 = (bf16[64,4096]{1,0:T(8,128)(2,1)S(1)}, bf16[64,4096]{1,0:T(8,128)(2,1)S(1)}, u32[]{:S(2)}, u32[]{:S(2)}) collective-permute-start(bf16[64,4096]{1,0:T(8,128)(2,1)S(1)} %constant_dynamic-update-slice_fusion.refs_1_), channel_id=1, source_target_pairs={{0,1},{1,2},{2,3},{3,4},{4,5},{5,6},{6,7},{7,0},{8,9},{9,10},{10,1... | collective-permute-start | bytes 1572872 | tf_op jit(solution)/shard_map/ppermute | solution.py:17
  44.7 25.2 %collective-permute-start.5 = (bf16[64,4096]{1,0:T(8,128)(2,1)S(1)}, bf16[64,4096]{1,0:T(8,128)(2,1)S(1)}, u32[]{:S(2)}, u32[]{:S(2)}) collective-permute-start(bf16[64,4096]{1,0:T(8,128)(2,1)S(1)} %collective-permute-done.3.refs_2_), channel_id=1, source_target_pairs={{0,1},{1,2},{2,3},{3,4},{4,5},{5,6},{6,7},{7,0},{8,9},{9,10},{10,1... | collective-permute-start | bytes 1572872 | tf_op jit(solution)/shard_map/ppermute | solution.py:17
  51.2 22.5 %collective-permute-start.13 = (bf16[64,4096]{1,0:T(8,128)(2,1)S(1)}, bf16[64,4096]{1,0:T(8,128)(2,1)S(1)}, u32[]{:S(2)}, u32[]{:S(2)}) collective-permute-start(bf16[64,4096]{1,0:T(8,128)(2,1)S(1)} %collective-permute-done.11.refs_10_), channel_id=1, source_target_pairs={{0,7},{1,0},{2,1},{3,2},{4,3},{5,4},{6,5},{7,6},{8,15},{9,8},{10,9... | collective-permute-start | bytes 1572872 | tf_op jit(solution)/shard_map/ppermute | solution.py:17
  62.4 22.5 %collective-permute-start.6 = (bf16[64,4096]{1,0:T(8,128)(2,1)S(1)}, bf16[64,4096]{1,0:T(8,128)(2,1)S(1)}, u32[]{:S(2)}, u32[]{:S(2)}) collective-permute-start(bf16[64,4096]{1,0:T(8,128)(2,1)S(1)} %collective-permute-done.4.refs_3_), channel_id=1, source_target_pairs={{0,7},{1,0},{2,1},{3,2},{4,3},{5,4},{6,5},{7,6},{8,15},{9,8},{10,9... | collective-permute-start | bytes 1572872 | tf_op jit(solution)/shard_map/ppermute | solution.py:17
  68.0 22.5 %collective-permute-start.12 = (bf16[64,4096]{1,0:T(8,128)(2,1)S(1)}, bf16[64,4096]{1,0:T(8,128)(2,1)S(1)}, u32[]{:S(2)}, u32[]{:S(2)}) collective-permute-start(bf16[64,4096]{1,0:T(8,128)(2,1)S(1)} %collective-permute-done.10.refs_9_), channel_id=1, source_target_pairs={{0,1},{1,2},{2,3},{3,4},{4,5},{5,6},{6,7},{7,0},{8,9},{9,10},{10,1... | collective-permute-start | bytes 1572872 | tf_op jit(solution)/shard_map/ppermute | solution.py:17
  69.9 23.5 %collective-permute-start.7 = (bf16[64,4096]{1,0:T(8,128)(2,1)S(1)}, bf16[64,4096]{1,0:T(8,128)(2,1)S(1)}, u32[]{:S(2)}, u32[]{:S(2)}) collective-permute-start(bf16[64,4096]{1,0:T(8,128)(2,1)S(1)} %collective-permute-done.5.refs_4_), channel_id=1, source_target_pairs={{0,1},{1,2},{2,3},{3,4},{4,5},{5,6},{6,7},{7,0},{8,9},{9,10},{10,1... | collective-permute-start | bytes 1572872 | tf_op jit(solution)/shard_map/ppermute | solution.py:17
  73.6 22.5 %collective-permute-start.15 = (bf16[64,4096]{1,0:T(8,128)(2,1)S(1)}, bf16[64,4096]{1,0:T(8,128)(2,1)S(1)}, u32[]{:S(2)}, u32[]{:S(2)}) collective-permute-start(bf16[64,4096]{1,0:T(8,128)(2,1)S(1)} %collective-permute-done.13.refs_12_), channel_id=1, source_target_pairs={{0,7},{1,0},{2,1},{3,2},{4,3},{5,4},{6,5},{7,6},{8,15},{9,8},{10,9... | collective-permute-start | bytes 1572872 | tf_op jit(solution)/shard_map/ppermute | solution.py:17
  84.9 22.5 %collective-permute-start.8 = (bf16[64,4096]{1,0:T(8,128)(2,1)S(1)}, bf16[64,4096]{1,0:T(8,128)(2,1)S(1)}, u32[]{:S(2)}, u32[]{:S(2)}) collective-permute-start(bf16[64,4096]{1,0:T(8,128)(2,1)S(1)} %collective-permute-done.6.refs_5_), channel_id=1, source_target_pairs={{0,7},{1,0},{2,1},{3,2},{4,3},{5,4},{6,5},{7,6},{8,15},{9,8},{10,9... | collective-permute-start | bytes 1572872 | tf_op jit(solution)/shard_map/ppermute | solution.py:17
  90.5 18.0 %collective-permute-start.14 = (bf16[64,4096]{1,0:T(8,128)(2,1)S(1)}, bf16[64,4096]{1,0:T(8,128)(2,1)S(1)}, u32[]{:S(2)}, u32[]{:S(2)}) collective-permute-start(bf16[64,4096]{1,0:T(8,128)(2,1)S(1)} %collective-permute-done.12.refs_11_), channel_id=1, source_target_pairs={{0,1},{1,2},{2,3},{3,4},{4,5},{5,6},{6,7},{7,0},{8,9},{9,10},{10,1... | collective-permute-start | bytes 1572872 | tf_op jit(solution)/shard_map/ppermute | solution.py:17
  93.5 22.5 %collective-permute-start.9 = (bf16[64,4096]{1,0:T(8,128)(2,1)S(1)}, bf16[64,4096]{1,0:T(8,128)(2,1)S(1)}, u32[]{:S(2)}, u32[]{:S(2)}) collective-permute-start(bf16[64,4096]{1,0:T(8,128)(2,1)S(1)} %collective-permute-done.7.refs_6_), channel_id=1, source_target_pairs={{0,1},{1,2},{2,3},{3,4},{4,5},{5,6},{6,7},{7,0},{8,9},{9,10},{10,1... | collective-permute-start | bytes 1572872 | tf_op jit(solution)/shard_map/ppermute | solution.py:17
  96.1 21.2 %collective-permute-start.16 = (bf16[64,4096]{1,0:T(8,128)(2,1)S(1)}, bf16[64,4096]{1,0:T(8,128)(2,1)S(1)}, u32[]{:S(2)}, u32[]{:S(2)}) collective-permute-start(bf16[64,4096]{1,0:T(8,128)(2,1)S(1)} %collective-permute-done.15.refs_14_), channel_id=1, source_target_pairs={{0,7},{1,0},{2,1},{3,2},{4,3},{5,4},{6,5},{7,6},{8,15},{9,8},{10,9... | collective-permute-start | bytes 1572872 | tf_op jit(solution)/shard_map/ppermute | solution.py:17
  121.6 28.3 %copy-start.1 = (s32[1,2]{1,0:T(1,128)S(1)}, s32[1,2]{1,0:T(1,128)}, u32[]{:S(2)}) copy-start(s32[1,2]{1,0:T(1,128)} %refs_1_.1) | copy-start | bytes 28
  121.6 28.3 %copy-start.2 = (s32[1,2]{1,0:T(1,128)S(1)}, s32[1,2]{1,0:T(1,128)}, u32[]{:S(2)}) copy-start(s32[1,2]{1,0:T(1,128)} %refs_2_.1) | copy-start | bytes 28
  121.6 28.3 %copy-start.3 = (f32[8]{0:T(128)S(1)}, f32[8]{0:T(128)}, u32[]{:S(2)}) copy-start(f32[8]{0:T(128)} %refs_3_.1) | copy-start | bytes 100

commit v2 on v0

v2 whole, which is shorter than its diff:
```python
import jax
import jax.numpy as jnp
from jax import lax
from jax.experimental import pallas as pl
from jax.experimental.pallas import tpu as pltpu
from jax.sharding import PartitionSpec as P

TR = 64
TV = 128
NZ = 8
NY = 4
EXTRA = 8


def z_shift(x, d):
    perm = [(o, (o // NZ) * NZ + (o % NZ + d) % NZ) for o in range(NY * NZ)]
    return lax.ppermute(x, "ocn", perm)


def y_shift(x, d):
    perm = [(o, ((o // NZ + d) % NY) * NZ + o % NZ) for o in range(NY * NZ)]
    return lax.ppermute(x, "ocn", perm)


def cross_kernel(groups, early, *refs):
    n = len(groups)
    blocks, ocean_ref = refs[:n], refs[n]
    out_ref, rows_ref, cov_ref, sq_ref, sem = refs[-5:]
    copies, placed, at = [], [], 0
    for ref, parts in zip(blocks, groups):
        copies.append(pltpu.make_async_copy(ref, rows_ref.at[pl.ds(at, ref.shape[0])], sem.at[len(copies)]))
        for dy, dz, first, count in parts:
            placed.append((at, dy, dz, first, count))
            at += count
    for c in copies:
        c.start()
    n_own, own = out_ref.shape[0], out_ref.shape[1] - EXTRA
    per = n_own * own // (NY * NZ)
    if early:
        ocean_f = ocean_ref[...].astype(jnp.float32)
        colsq = jnp.sum(ocean_f * ocean_f, axis=0, keepdims=True)
        line = lax.broadcasted_iota(jnp.int32, (EXTRA, colsq.shape[1]), 0)
        for m in range(n_own):
            out_ref[m, :own, :] = jnp.zeros((own, colsq.shape[1]), jnp.float32)
            out_ref[m, own:, :] = jnp.where(line == 2, colsq, 0.0)
    for c in copies:
        c.wait()
    tile = at // 2

    @pl.loop(0, 2)
    def _(t):
        part = pl.ds(pl.multiple_of(t * tile, 16), tile)
        rows = rows_ref[part, :]
        cov_ref[part, :] = jnp.dot(rows, ocean_ref[...], preferred_element_type=jnp.float32)
        rows_f = rows.astype(jnp.float32)
        sq_ref[part, :] = jnp.broadcast_to(jnp.sum(rows_f * rows_f, axis=1, keepdims=True), (tile, 128))

    o = lax.axis_index("ocn")
    y, z = o // NZ, lax.rem(o, NZ)
    for at, dy, dz, first, count in placed:
        origin = lax.rem(y + (dy + NY), NY) * NZ + lax.rem(z + (dz + NZ), NZ)
        owner, side = origin // 2, lax.rem(origin, 2)
        to = pl.ds(pl.multiple_of(side * per + first, 16), count)
        out_ref[owner, to, :] = cov_ref[at : at + count, :]
        row = lax.broadcasted_iota(jnp.int32, (count, 128), 0) + first
        lane = lax.broadcasted_iota(jnp.int32, (count, 128), 1)
        across = jnp.sum(jnp.where(row == lane, sq_ref[at : at + count, :], 0.0), axis=0, keepdims=True)
        line = lax.broadcasted_iota(jnp.int32, (EXTRA, 128), 0)
        out_ref[owner, own:, :128] += jnp.where(line == side, across, 0.0)


def cross(pieces, ocean, rows_all, n_mem, before=None):
    members, cols = ocean.shape
    rows = sum(a.shape[0] for a, _ in pieces)
    vmem = pl.BlockSpec(memory_space=pltpu.VMEM)
    args = [a for a, _ in pieces] + [ocean]
    specs = [pl.BlockSpec(memory_space=pl.ANY)] * len(pieces) + [vmem]
    if before is not None:
        args.append(before)
        specs.append(vmem)
    return pl.pallas_call(
        lambda *refs: cross_kernel([parts for _, parts in pieces], before is None, *refs),
        out_shape=jax.ShapeDtypeStruct((n_mem, rows_all // n_mem + EXTRA, cols), jnp.float32),
        in_specs=specs,
        out_specs=vmem,
        scratch_shapes=[
            pltpu.VMEM((rows, members), jnp.bfloat16),
            pltpu.VMEM((rows, cols), jnp.float32),
            pltpu.VMEM((rows, 128), jnp.float32),
            pltpu.SemaphoreType.DMA((len(pieces),)),
        ],
        input_output_aliases={} if before is None else {len(args) - 1: 0},
        compiler_params=pltpu.CompilerParams(vmem_limit_bytes=24 * 1024 * 1024),
        cost_estimate=pl.CostEstimate(
            flops=2 * rows * members * cols, bytes_accessed=2 * members * (rows + cols), transcendentals=0
        ),
    )(*args)


def finish_kernel(members, parts_ref, cutoff_ref, index_ref, table_ref, out_ref):
    own, cols = out_ref.shape
    total = jnp.sum(parts_ref[...], axis=0)
    eye = lax.broadcasted_iota(jnp.int32, (own, own), 0) == lax.broadcasted_iota(jnp.int32, (own, own), 1)
    half = own // 2
    across = jnp.concatenate([total[own : own + 1, :half], total[own + 1 : own + 2, :half]], axis=1)
    rowsq = jnp.sum(jnp.where(eye, across, 0.0), axis=1, keepdims=True)
    vx = rowsq / (members - 1.0) + 1e-06
    vy = total[own + 2 : own + 3] / (members - 1.0) + 1e-06
    corr = total[:own] / (members - 1.0) / jnp.sqrt(vx * vy)
    for i in range(own // TR):
        for j in range(cols // TV):
            weight = cutoff_ref[i, j].astype(jnp.float32) * table_ref[index_ref[i, j]]
            tile = (slice(i * TR, (i + 1) * TR), slice(j * TV, (j + 1) * TV))
            out_ref[tile] = corr[tile] * weight


def per_device(panel, ocean, cutoff, factor_index, factor_table):
    n_mem = lax.axis_size("mem")
    rows_all = panel.shape[1] * lax.axis_size("ocn")
    own_rows = rows_all // n_mem
    members = panel.shape[0] * n_mem
    mine = panel.T
    per = mine.shape[0]
    half = per // 2
    lo, hi = (0, half), (half, half)
    from_below = y_shift(mine, 1)
    from_above = y_shift(mine, -1)
    from_across = y_shift(mine, 2)
    own_up = z_shift(mine, 1)
    own_down = z_shift(mine, -1)

    first = [from_below, from_across[:half]]
    second = [from_above, from_across[half:]]
    up_1 = jnp.concatenate(first + [own_up[:half]], axis=0)
    up_2 = jnp.concatenate(second + [own_up[half:]], axis=0)
    down_1 = jnp.concatenate(first + [own_down[:half]], axis=0)
    down_2 = jnp.concatenate(second + [own_down[half:]], axis=0)
    both = per + half

    def parts_1(dz, own_dz=None):
        parts = [(-1, dz, 0, per), (2, dz, *lo)]
        return parts if own_dz is None else parts + [(0, own_dz, *lo)]

    def parts_2(dz, own_dz=None):
        parts = [(1, dz, 0, per), (2, dz, *hi)]
        return parts if own_dz is None else parts + [(0, own_dz, *hi)]

    early = [(mine, [(0, 0, 0, per)]), (up_1, parts_1(0, -1)), (up_2, parts_2(0, -1)), (own_down, [(0, 1, 0, per)])]
    for s in (1, 2):
        up_1, down_1 = z_shift(up_1, 1), z_shift(down_1, -1)
        up_2, down_2 = z_shift(up_2, 1), z_shift(down_2, -1)
        early += [(up_1, parts_1(-s, -s - 1)), (down_1, parts_1(s, s + 1))]
        early += [(up_2, parts_2(-s, -s - 1)), (down_2, parts_2(s, s + 1))]
    up_1, down_1 = z_shift(up_1, 1), z_shift(down_1[:both], -1)
    up_2, down_2 = z_shift(up_2[:both], 1), z_shift(down_2, -1)
    late = [(up_1, parts_1(-3, -4)), (down_1, parts_1(3)), (up_2, parts_2(-3)), (down_2, parts_2(3, 4))]
    late += [(z_shift(down_1, -1), parts_1(4)), (z_shift(up_2, 1), parts_2(4))]

    parts = cross(early, ocean, rows_all, n_mem)
    parts = cross(late, ocean, rows_all, n_mem, parts)
    parts = lax.all_to_all(parts, "mem", split_axis=0, concat_axis=0, tiled=True)
    return pl.pallas_call(
        lambda *refs: finish_kernel(members, *refs),
        out_shape=jax.ShapeDtypeStruct((own_rows, ocean.shape[1]), jnp.float32),
        in_specs=[pl.BlockSpec(memory_space=pltpu.VMEM)] + [pl.BlockSpec(memory_space=pltpu.SMEM)] * 3,
        out_specs=pl.BlockSpec(memory_space=pltpu.VMEM),
        compiler_params=pltpu.CompilerParams(vmem_limit_bytes=16 * 1024 * 1024),
    )(parts, cutoff, factor_index, factor_table)


def solution(mesh):
    in_specs = (P("mem", "ocn"), P("mem", "ocn"), P("mem", "ocn"), P("mem", "ocn"), P())
    out_specs = P("mem", "ocn")
    return jax.shard_map(
        per_device, mesh=mesh, in_specs=in_specs, out_specs=out_specs, check_vma=False
    )
```

time: 297 us -> 150 us (0.51)
  waiting for transfers between devices: 172 us -> 44.6 us
  starting transfers between devices: 0.04 us -> 69.8 us
  blocking collectives: 95.7 us -> 26.1 us
  between operations: 14.1 us -> 0.29 us
  matrix products: 7.38 us -> 0 us
  Pallas kernels: 0 us -> 6.46 us
    all_gather x1 -> x0, waiting for transfers between devices: 146 us -> none  [per_device(): lax.all_gather(panel, 'ocn', axis=1, tiled=True)]
    ppermute x0 -> x19, starting transfers between devices: none -> 69.8 us  [the longest x16 57.1 us: z_shift(): return lax.ppermute(x, 'ocn', perm)]
    unnamed x1 -> x0, blocking collectives: 69.7 us -> none
    ppermute x0 -> x19, waiting for transfers between devices: none -> 44.6 us  [the longest x16 32.1 us: z_shift(): return lax.ppermute(x, 'ocn', perm)]
    all_to_all x0 -> x1, blocking collectives: none -> 26.1 us  [per_device(): lax.all_to_all(parts, 'mem', split_axis=0, concat_axis=0, tiled=True)]
    psum x1 -> x0, blocking collectives: 25.9 us -> none  [per_device(): panel_tot, colsq = lax.psum((panel_sq, ocean_sq), 'mem')]
    psum x1 -> x0, waiting for transfers between devices: 25.6 us -> none  [per_device(): summed = lax.psum(partial_value, 'mem')]
    dot_general x1 -> x0, matrix products: 7.38 us -> none  [cross_rows(): lax.dot_general(column_span, ocean, (((0,), (0,)), ((), ())), preferred_e...]
  transfers between devices with their start and end apart: 2 -> 19, of which waited for: 2 -> 17; matrix products, arithmetic and copies ran while one was open for 1% -> 0% of each run, Pallas kernels for 0% -> 2%
where the time goes in v2:
time: 150 us; the launch traced here: 148 us
  starting transfers between devices  69.8 us (47%)
  waiting for transfers between devices  44.6 us (30%)
  blocking collectives  26.1 us (17%)
  Pallas kernels  6.46 us (4%)
    ppermute x16, starting transfers between devices, z_shift(): return lax.ppermute(x, 'ocn', perm)  57.1 us
    ppermute x16, waiting for transfers between devices, z_shift(): return lax.ppermute(x, 'ocn', perm)  32.1 us
    all_to_all x1, blocking collectives, per_device(): lax.all_to_all(parts, 'mem', split_axis=0, concat_axis=0, tiled=True)  26.1 us
    ppermute x3, starting transfers between devices, y_shift(): return lax.ppermute(x, 'ocn', perm)  12.7 us
    ppermute x3, waiting for transfers between devices, y_shift(): return lax.ppermute(x, 'ocn', perm)  12.5 us
    pallas_call x2, Pallas kernels, cross(): pl.pallas_call(lambda *refs: cross_kernel([parts for _, parts in pieces],...  5.08 us
  transfers between devices with their start and end apart: 19, of which 17 were waited for; matrix products, arithmetic and copies ran while one was open for 0% of the time, Pallas kernels for 2%

profile of v2, /device:TPU:56, one launch (start us, length us, event | category | flops | bytes accessed | tf_op | source)
XLA Modules:
  0.0 147.6 jit_solution(16143138684865729757)
XLA Ops:
  0.0 10.9 %collective-permute-start.6 = (bf16[32,4096]{1,0:T(8,128)(2,1)}, bf16[32,4096]{1,0:T(8,128)(2,1)S(1)}, u32[]{:S(2)}, u32[]{:S(2)}) collective-permute-start(bf16[32,4096]{1,0:T(8,128)(2,1)} %bitcast.1), channel_id=1, source_target_pairs={{0,7},{1,0},{2,1},{3,2},{4,3},{5,4},{6,5},{7,6},{8,15},{9,8},{10,9... | collective-permute-start | bytes 786440 | tf_op jit(solution)/shard_map/ppermute | solution.py:17
  10.9 4.7 %collective-permute-start.1 = (bf16[32,4096]{1,0:T(8,128)(2,1)}, bf16[32,4096]{1,0:T(8,128)(2,1)S(1)}, u32[]{:S(2)}, u32[]{:S(2)}) collective-permute-start(bf16[32,4096]{1,0:T(8,128)(2,1)} %bitcast.2), channel_id=1, source_target_pairs={{0,16},{1,17},{2,18},{3,19},{4,20},{5,21},{6,22},{7,23},{8,24},{9,... | collective-permute-start | bytes 786440 | tf_op jit(solution)/shard_map/ppermute | solution.py:22
  15.7 1.9 %collective-permute-start.2 = (bf16[32,4096]{1,0:T(8,128)(2,1)}, bf16[32,4096]{1,0:T(8,128)(2,1)S(1)}, u32[]{:S(2)}, u32[]{:S(2)}) collective-permute-start(bf16[32,4096]{1,0:T(8,128)(2,1)} %bitcast.3), channel_id=1, source_target_pairs={{0,1},{1,2},{2,3},{3,4},{4,5},{5,6},{6,7},{7,0},{8,9},{9,10},{10,1... | collective-permute-start | bytes 786440 | tf_op jit(solution)/shard_map/ppermute | solution.py:17
  17.6 2.2 %collective-permute-start.10 = (bf16[32,4096]{1,0:T(8,128)(2,1)}, bf16[32,4096]{1,0:T(8,128)(2,1)S(1)}, u32[]{:S(2)}, u32[]{:S(2)}) collective-permute-start(bf16[32,4096]{1,0:T(8,128)(2,1)} %bitcast.4), channel_id=1, source_target_pairs={{0,24},{1,25},{2,26},{3,27},{4,28},{5,29},{6,30},{7,31},{8,0},{9,1... | collective-permute-start | bytes 786440 | tf_op jit(solution)/shard_map/ppermute | solution.py:22
  19.9 5.7 %collective-permute-start = (bf16[32,4096]{1,0:T(8,128)(2,1)}, bf16[32,4096]{1,0:T(8,128)(2,1)S(1)}, u32[]{:S(2)}, u32[]{:S(2)}) collective-permute-start(bf16[32,4096]{1,0:T(8,128)(2,1)} %bitcast.5), channel_id=1, source_target_pairs={{0,8},{1,9},{2,10},{3,11},{4,12},{5,13},{6,14},{7,15},{8,16},{9,17... | collective-permute-start | bytes 786440 | tf_op jit(solution)/shard_map/ppermute | solution.py:22
  25.6 4.8 %collective-permute-done.1 = bf16[32,4096]{1,0:T(8,128)(2,1)S(1)} collective-permute-done((bf16[32,4096]{1,0:T(8,128)(2,1)}, bf16[32,4096]{1,0:T(8,128)(2,1)S(1)}, u32[]{:S(2)}, u32[]{:S(2)}) %collective-permute-start.1) | collective-permute-done | bytes 262176 | tf_op jit(solution)/shard_map/ppermute | solution.py:22
  30.4 5.4 %collective-permute-done.10 = bf16[32,4096]{1,0:T(8,128)(2,1)S(1)} collective-permute-done((bf16[32,4096]{1,0:T(8,128)(2,1)}, bf16[32,4096]{1,0:T(8,128)(2,1)S(1)}, u32[]{:S(2)}, u32[]{:S(2)}) %collective-permute-start.10) | collective-permute-done | bytes 262176 | tf_op jit(solution)/shard_map/ppermute | solution.py:22
  36.0 1.9 %collective-permute-start.11 = (bf16[64,4096]{1,0:T(8,128)(2,1)S(1)}, bf16[64,4096]{1,0:T(8,128)(2,1)S(1)}, u32[]{:S(2)}, u32[]{:S(2)}) collective-permute-start(bf16[64,4096]{1,0:T(8,128)(2,1)S(1)} %get-tuple-element.6.refs_2_), channel_id=1, source_target_pairs={{0,1},{1,2},{2,3},{3,4},{4,5},{5,6},{6,7},{7,0},{8,9},{9,10},{10,1... | collective-permute-start | bytes 1572872 | tf_op jit(solution)/shard_map/ppermute | solution.py:17
  37.9 2.3 %collective-permute-done = bf16[32,4096]{1,0:T(8,128)(2,1)S(1)} collective-permute-done((bf16[32,4096]{1,0:T(8,128)(2,1)}, bf16[32,4096]{1,0:T(8,128)(2,1)S(1)}, u32[]{:S(2)}, u32[]{:S(2)}) %collective-permute-start) | collective-permute-done | bytes 262176 | tf_op jit(solution)/shard_map/ppermute | solution.py:22
  40.3 3.3 %collective-permute-start.7 = (bf16[64,4096]{1,0:T(8,128)(2,1)S(1)}, bf16[64,4096]{1,0:T(8,128)(2,1)S(1)}, u32[]{:S(2)}, u32[]{:S(2)}) collective-permute-start(bf16[64,4096]{1,0:T(8,128)(2,1)S(1)} %get-tuple-element.7), channel_id=1, source_target_pairs={{0,7},{1,0},{2,1},{3,2},{4,3},{5,4},{6,5},{7,6},{8,15},{9,8},{10,9... | collective-permute-start | bytes 1572872 | tf_op jit(solution)/shard_map/ppermute | solution.py:17
  43.7 2.6 %collective-permute-start.3 = (bf16[64,4096]{1,0:T(8,128)(2,1)S(1)}, bf16[64,4096]{1,0:T(8,128)(2,1)S(1)}, u32[]{:S(2)}, u32[]{:S(2)}) collective-permute-start(bf16[64,4096]{1,0:T(8,128)(2,1)S(1)} %get-tuple-element.8.refs_1_), channel_id=1, source_target_pairs={{0,1},{1,2},{2,3},{3,4},{4,5},{5,6},{6,7},{7,0},{8,9},{9,10},{10,1... | collective-permute-start | bytes 1572872 | tf_op jit(solution)/shard_map/ppermute | solution.py:17
  46.3 4.4 %collective-permute-start.14 = (bf16[64,4096]{1,0:T(8,128)(2,1)S(1)}, bf16[64,4096]{1,0:T(8,128)(2,1)S(1)}, u32[]{:S(2)}, u32[]{:S(2)}) collective-permute-start(bf16[64,4096]{1,0:T(8,128)(2,1)S(1)} %get-tuple-element.5), channel_id=1, source_target_pairs={{0,7},{1,0},{2,1},{3,2},{4,3},{5,4},{6,5},{7,6},{8,15},{9,8},{10,9... | collective-permute-start | bytes 1572872 | tf_op jit(solution)/shard_map/ppermute | solution.py:17
  50.7 3.2 %collective-permute-done.11.refs_6_ = bf16[64,4096]{1,0:T(8,128)(2,1)S(1)} collective-permute-done((bf16[64,4096]{1,0:T(8,128)(2,1)S(1)}, bf16[64,4096]{1,0:T(8,128)(2,1)S(1)}, u32[]{:S(2)}, u32[]{:S(2)}) %collective-permute-start.11) | collective-permute-done | bytes 524320 | tf_op jit(solution)/shard_map/ppermute | solution.py:17
  53.9 1.9 %collective-permute-start.12 = (bf16[64,4096]{1,0:T(8,128)(2,1)S(1)}, bf16[64,4096]{1,0:T(8,128)(2,1)S(1)}, u32[]{:S(2)}, u32[]{:S(2)}) collective-permute-start(bf16[64,4096]{1,0:T(8,128)(2,1)S(1)} %collective-permute-done.11.refs_6_), channel_id=1, source_target_pairs={{0,1},{1,2},{2,3},{3,4},{4,5},{5,6},{6,7},{7,0},{8,9},{9,10},{10,1... | collective-permute-start | bytes 1572872 | tf_op jit(solution)/shard_map/ppermute | solution.py:17
  57.1 4.5 %collective-permute-start.8 = (bf16[64,4096]{1,0:T(8,128)(2,1)S(1)}, bf16[64,4096]{1,0:T(8,128)(2,1)S(1)}, u32[]{:S(2)}, u32[]{:S(2)}) collective-permute-start(bf16[64,4096]{1,0:T(8,128)(2,1)S(1)} %collective-permute-done.7.refs_5_), channel_id=1, source_target_pairs={{0,7},{1,0},{2,1},{3,2},{4,3},{5,4},{6,5},{7,6},{8,15},{9,8},{10,9... | collective-permute-start | bytes 1572872 | tf_op jit(solution)/shard_map/ppermute | solution.py:17
  61.6 3.6 %collective-permute-done.3.refs_4_ = bf16[64,4096]{1,0:T(8,128)(2,1)S(1)} collective-permute-done((bf16[64,4096]{1,0:T(8,128)(2,1)S(1)}, bf16[64,4096]{1,0:T(8,128)(2,1)S(1)}, u32[]{:S(2)}, u32[]{:S(2)}) %collective-permute-start.3) | collective-permute-done | bytes 524320 | tf_op jit(solution)/shard_map/ppermute | solution.py:17
  65.2 1.9 %collective-permute-start.4 = (bf16[64,4096]{1,0:T(8,128)(2,1)S(1)}, bf16[64,4096]{1,0:T(8,128)(2,1)S(1)}, u32[]{:S(2)}, u32[]{:S(2)}) collective-permute-start(bf16[64,4096]{1,0:T(8,128)(2,1)S(1)} %collective-permute-done.3.refs_4_), channel_id=1, source_target_pairs={{0,1},{1,2},{2,3},{3,4},{4,5},{5,6},{6,7},{7,0},{8,9},{9,10},{10,1... | collective-permute-start | bytes 1572872 | tf_op jit(solution)/shard_map/ppermute | solution.py:17
  68.4 4.5 %collective-permute-start.15 = (bf16[64,4096]{1,0:T(8,128)(2,1)S(1)}, bf16[64,4096]{1,0:T(8,128)(2,1)S(1)}, u32[]{:S(2)}, u32[]{:S(2)}) collective-permute-start(bf16[64,4096]{1,0:T(8,128)(2,1)S(1)} %collective-permute-done.14.refs_7_), channel_id=1, source_target_pairs={{0,7},{1,0},{2,1},{3,2},{4,3},{5,4},{6,5},{7,6},{8,15},{9,8},{10,9... | collective-permute-start | bytes 1572872 | tf_op jit(solution)/shard_map/ppermute | solution.py:17
  72.9 3.6 %collective-permute-done.12.refs_10_ = bf16[64,4096]{1,0:T(8,128)(2,1)S(1)} collective-permute-done((bf16[64,4096]{1,0:T(8,128)(2,1)S(1)}, bf16[64,4096]{1,0:T(8,128)(2,1)S(1)}, u32[]{:S(2)}, u32[]{:S(2)}) %collective-permute-start.12) | collective-permute-done | bytes 524320 | tf_op jit(solution)/shard_map/ppermute | solution.py:17
  76.4 1.9 %collective-permute-start.13 = (bf16[48,4096]{1,0:T(8,128)(2,1)S(1)}, bf16[48,4096]{1,0:T(8,128)(2,1)S(1)}, u32[]{:S(2)}, u32[]{:S(2)}) collective-permute-start(bf16[48,4096]{1,0:T(8,128)(2,1)S(1)} %slice.38), channel_id=1, source_target_pairs={{0,1},{1,2},{2,3},{3,4},{4,5},{5,6},{6,7},{7,0},{8,9},{9,10},{10,1... | collective-permute-start | bytes 1179656 | tf_op jit(solution)/shard_map/ppermute | solution.py:17
  79.6 4.5 %collective-permute-start.9 = (bf16[48,4096]{1,0:T(8,128)(2,1)S(1)}, bf16[48,4096]{1,0:T(8,128)(2,1)S(1)}, u32[]{:S(2)}, u32[]{:S(2)}) collective-permute-start(bf16[48,4096]{1,0:T(8,128)(2,1)S(1)} %slice.35), channel_id=1, source_target_pairs={{0,7},{1,0},{2,1},{3,2},{4,3},{5,4},{6,5},{7,6},{8,15},{9,8},{10,9... | collective-permute-start | bytes 1179656 | tf_op jit(solution)/shard_map/ppermute | solution.py:17
  84.1 3.5 %collective-permute-done.4.refs_8_ = bf16[64,4096]{1,0:T(8,128)(2,1)S(1)} collective-permute-done((bf16[64,4096]{1,0:T(8,128)(2,1)S(1)}, bf16[64,4096]{1,0:T(8,128)(2,1)S(1)}, u32[]{:S(2)}, u32[]{:S(2)}) %collective-permute-start.4) | collective-permute-done | bytes 524320 | tf_op jit(solution)/shard_map/ppermute | solution.py:17
  87.7 1.9 %collective-permute-start.5 = (bf16[64,4096]{1,0:T(8,128)(2,1)S(1)}, bf16[64,4096]{1,0:T(8,128)(2,1)S(1)}, u32[]{:S(2)}, u32[]{:S(2)}) collective-permute-start(bf16[64,4096]{1,0:T(8,128)(2,1)S(1)} %collective-permute-done.4.refs_8_), channel_id=1, source_target_pairs={{0,1},{1,2},{2,3},{3,4},{4,5},{5,6},{6,7},{7,0},{8,9},{9,10},{10,1... | collective-permute-start | bytes 1572872 | tf_op jit(solution)/shard_map/ppermute | solution.py:17
  90.8 4.5 %collective-permute-start.16 = (bf16[64,4096]{1,0:T(8,128)(2,1)S(1)}, bf16[64,4096]{1,0:T(8,128)(2,1)S(1)}, u32[]{:S(2)}, u32[]{:S(2)}) collective-permute-start(bf16[64,4096]{1,0:T(8,128)(2,1)S(1)} %collective-permute-done.15.refs_11_), channel_id=1, source_target_pairs={{0,7},{1,0},{2,1},{3,2},{4,3},{5,4},{6,5},{7,6},{8,15},{9,8},{10,9... | collective-permute-start | bytes 1572872 | tf_op jit(solution)/shard_map/ppermute | solution.py:17
  96.1 1.9 %collective-permute-start.18 = (bf16[48,4096]{1,0:T(8,128)(2,1)S(1)}, bf16[48,4096]{1,0:T(8,128)(2,1)S(1)}, u32[]{:S(2)}, u32[]{:S(2)}) collective-permute-start(bf16[48,4096]{1,0:T(8,128)(2,1)S(1)} %collective-permute-done.13.refs_2_), channel_id=1, source_target_pairs={{0,1},{1,2},{2,3},{3,4},{4,5},{5,6},{6,7},{7,0},{8,9},{9,10},{10,1... | collective-permute-start | bytes 1179656 | tf_op jit(solution)/shard_map/ppermute | solution.py:17
  99.3 4.5 %collective-permute-start.17 = (bf16[48,4096]{1,0:T(8,128)(2,1)S(1)}, bf16[48,4096]{1,0:T(8,128)(2,1)S(1)}, u32[]{:S(2)}, u32[]{:S(2)}) collective-permute-start(bf16[48,4096]{1,0:T(8,128)(2,1)S(1)} %collective-permute-done.9.refs_1_), channel_id=1, source_target_pairs={{0,7},{1,0},{2,1},{3,2},{4,3},{5,4},{6,5},{7,6},{8,15},{9,8},{10,9... | collective-permute-start | bytes 1179656 | tf_op jit(solution)/shard_map/ppermute | solution.py:17
  103.8 3.0 %shard_map.55.refs_7_ = f32[16,72,256]{2,1,0:T(8,128)S(1)} custom-call(bf16[32,4096]{1,0:T(8,128)(2,1)S(1)} %bitcast.6, bf16[64,4096]{1,0:T(8,128)(2,1)S(1)} %get-tuple-element.8.refs_1_, bf16[64,4096]{1,0:T(8,128)(2,1)S(1)} %get-tuple-element.6.refs_2_, bf16[32,4096]{1,0:T(8,128)(2,1)S(1)} %collective-permute-done.6.refs_3_, ...), custom_call_target="tpu_custom_call" | custom-call | flops 1476395008 | bytes 7864320 | tf_op jit(solution)/shard_map/pallas_call | solution.py:81
  107.3 3.2 %collective-permute-done.16.refs_3_ = bf16[64,4096]{1,0:T(8,128)(2,1)S(1)} collective-permute-done((bf16[64,4096]{1,0:T(8,128)(2,1)S(1)}, bf16[64,4096]{1,0:T(8,128)(2,1)S(1)}, u32[]{:S(2)}, u32[]{:S(2)}) %collective-permute-start.16) | collective-permute-done | bytes 524320 | tf_op jit(solution)/shard_map/ppermute | solution.py:17
  110.5 3.2 %collective-permute-done.18.refs_5_ = bf16[48,4096]{1,0:T(8,128)(2,1)S(1)} collective-permute-done((bf16[48,4096]{1,0:T(8,128)(2,1)S(1)}, bf16[48,4096]{1,0:T(8,128)(2,1)S(1)}, u32[]{:S(2)}, u32[]{:S(2)}) %collective-permute-start.18) | collective-permute-done | bytes 393248 | tf_op jit(solution)/shard_map/ppermute | solution.py:17
  113.7 4.3 %collective-permute-done.17.refs_4_ = bf16[48,4096]{1,0:T(8,128)(2,1)S(1)} collective-permute-done((bf16[48,4096]{1,0:T(8,128)(2,1)S(1)}, bf16[48,4096]{1,0:T(8,128)(2,1)S(1)}, u32[]{:S(2)}, u32[]{:S(2)}) %collective-permute-start.17) | collective-permute-done | bytes 393248 | tf_op jit(solution)/shard_map/ppermute | solution.py:17
  118.0 2.1 %shard_map.56 = f32[16,72,256]{2,1,0:T(8,128)S(1)} custom-call(bf16[64,4096]{1,0:T(8,128)(2,1)S(1)} %collective-permute-done.5.refs_0_, bf16[48,4096]{1,0:T(8,128)(2,1)S(1)} %collective-permute-done.9.refs_1_, bf16[48,4096]{1,0:T(8,128)(2,1)S(1)} %collective-permute-done.13.refs_2_, ...), custom_call_target="tpu_custom_call", output_to_operand_aliasing={{}: (7, {})} | custom-call | flops 671088640 | bytes 4718592 | tf_op jit(solution)/shard_map/pallas_call | solution.py:81
  120.1 26.1 %all_to_all.5.refs_0_ = f32[16,72,256]{2,1,0:T(8,128)S(1)} all-to-all(f32[16,72,256]{2,1,0:T(8,128)S(1)} %shard_map.56), channel_id=1, replica_groups=mesh['mem'=16,'ocn'=32] {'mem'}, dimensions={0} | all-to-all | bytes 2359296 | tf_op jit(solution)/shard_map/all_to_all | solution.py:161
  (27 shorter events, 9.3 us)
Async XLA Ops:
  0.0 25.6 %collective-permute-start.6 = (bf16[32,4096]{1,0:T(8,128)(2,1)}, bf16[32,4096]{1,0:T(8,128)(2,1)S(1)}, u32[]{:S(2)}, u32[]{:S(2)}) collective-permute-start(bf16[32,4096]{1,0:T(8,128)(2,1)} %bitcast.1), channel_id=1, source_target_pairs={{0,7},{1,0},{2,1},{3,2},{4,3},{5,4},{6,5},{7,6},{8,15},{9,8},{10,9... | collective-permute-start | bytes 786440 | tf_op jit(solution)/shard_map/ppermute | solution.py:17
  10.9 19.4 %collective-permute-start.1 = (bf16[32,4096]{1,0:T(8,128)(2,1)}, bf16[32,4096]{1,0:T(8,128)(2,1)S(1)}, u32[]{:S(2)}, u32[]{:S(2)}) collective-permute-start(bf16[32,4096]{1,0:T(8,128)(2,1)} %bitcast.2), channel_id=1, source_target_pairs={{0,16},{1,17},{2,18},{3,19},{4,20},{5,21},{6,22},{7,23},{8,24},{9,... | collective-permute-start | bytes 786440 | tf_op jit(solution)/shard_map/ppermute | solution.py:22
  15.7 14.7 %collective-permute-start.2 = (bf16[32,4096]{1,0:T(8,128)(2,1)}, bf16[32,4096]{1,0:T(8,128)(2,1)S(1)}, u32[]{:S(2)}, u32[]{:S(2)}) collective-permute-start(bf16[32,4096]{1,0:T(8,128)(2,1)} %bitcast.3), channel_id=1, source_target_pairs={{0,1},{1,2},{2,3},{3,4},{4,5},{5,6},{6,7},{7,0},{8,9},{9,10},{10,1... | collective-permute-start | bytes 786440 | tf_op jit(solution)/shard_map/ppermute | solution.py:17
  17.6 18.3 %collective-permute-start.10 = (bf16[32,4096]{1,0:T(8,128)(2,1)}, bf16[32,4096]{1,0:T(8,128)(2,1)S(1)}, u32[]{:S(2)}, u32[]{:S(2)}) collective-permute-start(bf16[32,4096]{1,0:T(8,128)(2,1)} %bitcast.4), channel_id=1, source_target_pairs={{0,24},{1,25},{2,26},{3,27},{4,28},{5,29},{6,30},{7,31},{8,0},{9,1... | collective-permute-start | bytes 786440 | tf_op jit(solution)/shard_map/ppermute | solution.py:22
  19.9 20.4 %collective-permute-start = (bf16[32,4096]{1,0:T(8,128)(2,1)}, bf16[32,4096]{1,0:T(8,128)(2,1)S(1)}, u32[]{:S(2)}, u32[]{:S(2)}) collective-permute-start(bf16[32,4096]{1,0:T(8,128)(2,1)} %bitcast.5), channel_id=1, source_target_pairs={{0,8},{1,9},{2,10},{3,11},{4,12},{5,13},{6,14},{7,15},{8,16},{9,17... | collective-permute-start | bytes 786440 | tf_op jit(solution)/shard_map/ppermute | solution.py:22
  36.0 18.0 %collective-permute-start.11 = (bf16[64,4096]{1,0:T(8,128)(2,1)S(1)}, bf16[64,4096]{1,0:T(8,128)(2,1)S(1)}, u32[]{:S(2)}, u32[]{:S(2)}) collective-permute-start(bf16[64,4096]{1,0:T(8,128)(2,1)S(1)} %get-tuple-element.6.refs_2_), channel_id=1, source_target_pairs={{0,1},{1,2},{2,3},{3,4},{4,5},{5,6},{6,7},{7,0},{8,9},{9,10},{10,1... | collective-permute-start | bytes 1572872 | tf_op jit(solution)/shard_map/ppermute | solution.py:17
  40.2 63.5 %copy-start = (bf16[4096,256]{1,0:T(8,128)(2,1)S(1)}, bf16[4096,256]{1,0:T(8,128)(2,1)}, u32[]{:S(2)}) copy-start(bf16[4096,256]{1,0:T(8,128)(2,1)} %refs_6_.1) | copy-start | bytes 6291460
  40.3 63.5 %copy-start.1 = (bf16[4096,32]{0,1:T(8,128)(2,1)S(1)}, bf16[4096,32]{0,1:T(8,128)(2,1)}, u32[]{:S(2)}) copy-start(bf16[4096,32]{0,1:T(8,128)(2,1)} %param.5) | copy-start | bytes 786436
  40.3 16.8 %collective-permute-start.7 = (bf16[64,4096]{1,0:T(8,128)(2,1)S(1)}, bf16[64,4096]{1,0:T(8,128)(2,1)S(1)}, u32[]{:S(2)}, u32[]{:S(2)}) collective-permute-start(bf16[64,4096]{1,0:T(8,128)(2,1)S(1)} %get-tuple-element.7), channel_id=1, source_target_pairs={{0,7},{1,0},{2,1},{3,2},{4,3},{5,4},{6,5},{7,6},{8,15},{9,8},{10,9... | collective-permute-start | bytes 1572872 | tf_op jit(solution)/shard_map/ppermute | solution.py:17
  43.7 21.5 %collective-permute-start.3 = (bf16[64,4096]{1,0:T(8,128)(2,1)S(1)}, bf16[64,4096]{1,0:T(8,128)(2,1)S(1)}, u32[]{:S(2)}, u32[]{:S(2)}) collective-permute-start(bf16[64,4096]{1,0:T(8,128)(2,1)S(1)} %get-tuple-element.8.refs_1_), channel_id=1, source_target_pairs={{0,1},{1,2},{2,3},{3,4},{4,5},{5,6},{6,7},{7,0},{8,9},{9,10},{10,1... | collective-permute-start | bytes 1572872 | tf_op jit(solution)/shard_map/ppermute | solution.py:17
  46.3 22.1 %collective-permute-start.14 = (bf16[64,4096]{1,0:T(8,128)(2,1)S(1)}, bf16[64,4096]{1,0:T(8,128)(2,1)S(1)}, u32[]{:S(2)}, u32[]{:S(2)}) collective-permute-start(bf16[64,4096]{1,0:T(8,128)(2,1)S(1)} %get-tuple-element.5), channel_id=1, source_target_pairs={{0,7},{1,0},{2,1},{3,2},{4,3},{5,4},{6,5},{7,6},{8,15},{9,8},{10,9... | collective-permute-start | bytes 1572872 | tf_op jit(solution)/shard_map/ppermute | solution.py:17
  53.9 22.5 %collective-permute-start.12 = (bf16[64,4096]{1,0:T(8,128)(2,1)S(1)}, bf16[64,4096]{1,0:T(8,128)(2,1)S(1)}, u32[]{:S(2)}, u32[]{:S(2)}) collective-permute-start(bf16[64,4096]{1,0:T(8,128)(2,1)S(1)} %collective-permute-done.11.refs_6_), channel_id=1, source_target_pairs={{0,1},{1,2},{2,3},{3,4},{4,5},{5,6},{6,7},{7,0},{8,9},{9,10},{10,1... | collective-permute-start | bytes 1572872 | tf_op jit(solution)/shard_map/ppermute | solution.py:17
  57.1 22.5 %collective-permute-start.8 = (bf16[64,4096]{1,0:T(8,128)(2,1)S(1)}, bf16[64,4096]{1,0:T(8,128)(2,1)S(1)}, u32[]{:S(2)}, u32[]{:S(2)}) collective-permute-start(bf16[64,4096]{1,0:T(8,128)(2,1)S(1)} %collective-permute-done.7.refs_5_), channel_id=1, source_target_pairs={{0,7},{1,0},{2,1},{3,2},{4,3},{5,4},{6,5},{7,6},{8,15},{9,8},{10,9... | collective-permute-start | bytes 1572872 | tf_op jit(solution)/shard_map/ppermute | solution.py:17
  65.2 22.5 %collective-permute-start.4 = (bf16[64,4096]{1,0:T(8,128)(2,1)S(1)}, bf16[64,4096]{1,0:T(8,128)(2,1)S(1)}, u32[]{:S(2)}, u32[]{:S(2)}) collective-permute-start(bf16[64,4096]{1,0:T(8,128)(2,1)S(1)} %collective-permute-done.3.refs_4_), channel_id=1, source_target_pairs={{0,1},{1,2},{2,3},{3,4},{4,5},{5,6},{6,7},{7,0},{8,9},{9,10},{10,1... | collective-permute-start | bytes 1572872 | tf_op jit(solution)/shard_map/ppermute | solution.py:17
  68.4 22.5 %collective-permute-start.15 = (bf16[64,4096]{1,0:T(8,128)(2,1)S(1)}, bf16[64,4096]{1,0:T(8,128)(2,1)S(1)}, u32[]{:S(2)}, u32[]{:S(2)}) collective-permute-start(bf16[64,4096]{1,0:T(8,128)(2,1)S(1)} %collective-permute-done.14.refs_7_), channel_id=1, source_target_pairs={{0,7},{1,0},{2,1},{3,2},{4,3},{5,4},{6,5},{7,6},{8,15},{9,8},{10,9... | collective-permute-start | bytes 1572872 | tf_op jit(solution)/shard_map/ppermute | solution.py:17
  76.4 19.6 %collective-permute-start.13 = (bf16[48,4096]{1,0:T(8,128)(2,1)S(1)}, bf16[48,4096]{1,0:T(8,128)(2,1)S(1)}, u32[]{:S(2)}, u32[]{:S(2)}) collective-permute-start(bf16[48,4096]{1,0:T(8,128)(2,1)S(1)} %slice.38), channel_id=1, source_target_pairs={{0,1},{1,2},{2,3},{3,4},{4,5},{5,6},{6,7},{7,0},{8,9},{9,10},{10,1... | collective-permute-start | bytes 1179656 | tf_op jit(solution)/shard_map/ppermute | solution.py:17
  79.6 19.6 %collective-permute-start.9 = (bf16[48,4096]{1,0:T(8,128)(2,1)S(1)}, bf16[48,4096]{1,0:T(8,128)(2,1)S(1)}, u32[]{:S(2)}, u32[]{:S(2)}) collective-permute-start(bf16[48,4096]{1,0:T(8,128)(2,1)S(1)} %slice.35), channel_id=1, source_target_pairs={{0,7},{1,0},{2,1},{3,2},{4,3},{5,4},{6,5},{7,6},{8,15},{9,8},{10,9... | collective-permute-start | bytes 1179656 | tf_op jit(solution)/shard_map/ppermute | solution.py:17
  87.7 19.7 %collective-permute-start.5 = (bf16[64,4096]{1,0:T(8,128)(2,1)S(1)}, bf16[64,4096]{1,0:T(8,128)(2,1)S(1)}, u32[]{:S(2)}, u32[]{:S(2)}) collective-permute-start(bf16[64,4096]{1,0:T(8,128)(2,1)S(1)} %collective-permute-done.4.refs_8_), channel_id=1, source_target_pairs={{0,1},{1,2},{2,3},{3,4},{4,5},{5,6},{6,7},{7,0},{8,9},{9,10},{10,1... | collective-permute-start | bytes 1572872 | tf_op jit(solution)/shard_map/ppermute | solution.py:17
  90.8 19.7 %collective-permute-start.16 = (bf16[64,4096]{1,0:T(8,128)(2,1)S(1)}, bf16[64,4096]{1,0:T(8,128)(2,1)S(1)}, u32[]{:S(2)}, u32[]{:S(2)}) collective-permute-start(bf16[64,4096]{1,0:T(8,128)(2,1)S(1)} %collective-permute-done.15.refs_11_), channel_id=1, source_target_pairs={{0,7},{1,0},{2,1},{3,2},{4,3},{5,4},{6,5},{7,6},{8,15},{9,8},{10,9... | collective-permute-start | bytes 1572872 | tf_op jit(solution)/shard_map/ppermute | solution.py:17
  96.1 17.6 %collective-permute-start.18 = (bf16[48,4096]{1,0:T(8,128)(2,1)S(1)}, bf16[48,4096]{1,0:T(8,128)(2,1)S(1)}, u32[]{:S(2)}, u32[]{:S(2)}) collective-permute-start(bf16[48,4096]{1,0:T(8,128)(2,1)S(1)} %collective-permute-done.13.refs_2_), channel_id=1, source_target_pairs={{0,1},{1,2},{2,3},{3,4},{4,5},{5,6},{6,7},{7,0},{8,9},{9,10},{10,1... | collective-permute-start | bytes 1179656 | tf_op jit(solution)/shard_map/ppermute | solution.py:17
  99.3 18.7 %collective-permute-start.17 = (bf16[48,4096]{1,0:T(8,128)(2,1)S(1)}, bf16[48,4096]{1,0:T(8,128)(2,1)S(1)}, u32[]{:S(2)}, u32[]{:S(2)}) collective-permute-start(bf16[48,4096]{1,0:T(8,128)(2,1)S(1)} %collective-permute-done.9.refs_1_), channel_id=1, source_target_pairs={{0,7},{1,0},{2,1},{3,2},{4,3},{5,4},{6,5},{7,6},{8,15},{9,8},{10,9... | collective-permute-start | bytes 1179656 | tf_op jit(solution)/shard_map/ppermute | solution.py:17
  120.1 26.2 %copy-start.2 = (s32[1,2]{1,0:T(1,128)S(1)}, s32[1,2]{1,0:T(1,128)}, u32[]{:S(2)}) copy-start(s32[1,2]{1,0:T(1,128)} %refs_1_.1) | copy-start | bytes 28
  120.1 26.1 %copy-start.3 = (s32[1,2]{1,0:T(1,128)S(1)}, s32[1,2]{1,0:T(1,128)}, u32[]{:S(2)}) copy-start(s32[1,2]{1,0:T(1,128)} %refs_2_.1) | copy-start | bytes 28
  120.1 26.1 %copy-start.4 = (f32[8]{0:T(128)S(1)}, f32[8]{0:T(128)}, u32[]{:S(2)}) copy-start(f32[8]{0:T(128)} %refs_3_.1) | copy-start | bytes 100

commit v3 on v2

v3 whole, which is shorter than its diff:
```python
import functools

import jax
import jax.numpy as jnp
from jax import lax
from jax.experimental import pallas as pl
from jax.experimental.pallas import tpu as pltpu
from jax.sharding import PartitionSpec as P

TR = 64
TV = 128
NZ = 8
NY = 4
EXTRA = 8
TAIL = 768


def z_shift(x, d):
    perm = [(o, (o // NZ) * NZ + (o % NZ + d) % NZ) for o in range(NY * NZ)]
    return lax.ppermute(x, "ocn", perm)


def y_shift(x, d):
    perm = [(o, ((o // NZ + d) % NY) * NZ + o % NZ) for o in range(NY * NZ)]
    return lax.ppermute(x, "ocn", perm)


def z_spread(x):
    groups = [[y * NZ + z for z in range(NZ)] for y in range(NY)]
    copies = jnp.broadcast_to(x[None], (NZ,) + x.shape).reshape(NZ * x.shape[0], x.shape[1])
    return lax.all_to_all(copies, "ocn", split_axis=0, concat_axis=0, axis_index_groups=groups, tiled=True)


def own_sums(rows):
    rows_f = rows.astype(jnp.float32)
    return jnp.sum(rows_f * rows_f, axis=1, keepdims=True)


def along_lanes(column, first):
    shape = (column.shape[0], 128)
    here = lax.broadcasted_iota(jnp.int32, shape, 0) + first == lax.broadcasted_iota(jnp.int32, shape, 1)
    return jnp.sum(jnp.where(here, column, 0.0), axis=0, keepdims=True)


def tail_kernel(*refs):
    blocks, ocean_ref = refs[:NY], refs[NY]
    out_ref, rows_ref, sem = refs[-3:]
    y = lax.axis_index("ocn") // NZ
    rows_y = blocks[0].shape[0]
    copies = []
    for ref, dy in zip(blocks, (0, -1, 1, 2)):
        start = pl.multiple_of(lax.rem(y + (dy + NY), NY) * rows_y, rows_y)
        copies.append(pltpu.make_async_copy(ref, rows_ref.at[pl.ds(start, rows_y)], sem.at[len(copies)]))
    for c in copies:
        c.start()
    members, cols = ocean_ref.shape
    tail = rows_ref.shape[1]
    ocean_f = ocean_ref[...].astype(jnp.float32)
    colsq = jnp.sum(ocean_f * ocean_f, axis=0, keepdims=True)
    line = lax.broadcasted_iota(jnp.int32, (EXTRA, cols), 0)
    own = out_ref.shape[1] - EXTRA
    per_y = rows_y // own
    for c in copies:
        c.wait()

    @pl.loop(0, NY)
    def _(t):
        rows = rows_ref[pl.ds(pl.multiple_of(t * rows_y, rows_y), rows_y), :]
        cov = jnp.dot(rows, ocean_ref[members - tail :, :], preferred_element_type=jnp.float32)
        sq = own_sums(rows)
        for k in range(per_y):
            owner = t * per_y + k
            out_ref[owner, :own, :] = cov[k * own : (k + 1) * own]
            lines = jnp.where(line == 2, colsq, 0.0)
            for side in range(2):
                at = k * own + side * (own // 2)
                across = along_lanes(sq[at : at + own // 2], 0)
                across = jnp.concatenate([across, jnp.zeros((1, cols - 128), jnp.float32)], axis=1)
                lines = jnp.where(line == side, across, lines)
            out_ref[owner, own:, :] = lines


def head_kernel(groups, *refs):
    n = len(groups)
    blocks, ocean_ref = refs[:n], refs[n]
    out_ref, rows_ref, cov_ref, sq_ref, sem = refs[-5:]
    own = out_ref.shape[1] - EXTRA
    per = own // 2
    copies, placed = [], []
    for ref, parts in zip(blocks, groups):
        to = pl.ds(len(placed) * per, ref.shape[0])
        copies.append(pltpu.make_async_copy(ref, rows_ref.at[to], sem.at[len(copies)]))
        placed.extend(parts)
    for c in copies:
        c.start()
    for c in copies:
        c.wait()
    n_rows, head = rows_ref.shape
    tile = n_rows // 2

    @pl.loop(0, 2)
    def _(t):
        part = pl.ds(pl.multiple_of(t * tile, 16), tile)
        rows = rows_ref[part, :]
        cov_ref[part, :] = jnp.dot(rows, ocean_ref[:head, :], preferred_element_type=jnp.float32)
        sq_ref[part, :] = jnp.broadcast_to(own_sums(rows), (tile, 128))

    o = lax.axis_index("ocn")
    y, z = o // NZ, lax.rem(o, NZ)
    line = lax.broadcasted_iota(jnp.int32, (EXTRA, 128), 0)
    for i, (dy, dz) in enumerate(placed):
        origin = lax.rem(y + (dy + NY), NY) * NZ + lax.rem(z + (dz + NZ), NZ)
        owner, side = origin // 2, lax.rem(origin, 2)
        at = slice(i * per, (i + 1) * per)
        out_ref[owner, pl.ds(pl.multiple_of(side * per, per), per), :] += cov_ref[at, :]
        out_ref[owner, own:, :128] += jnp.where(line == side, along_lanes(sq_ref[at, :], 0), 0.0)


def cross(kernel, blocks, ocean, sums_shape, scratch, before=None):
    rows = sum(a.shape[0] for a in blocks)
    depth, cols = blocks[0].shape[1], ocean.shape[1]
    vmem = pl.BlockSpec(memory_space=pltpu.VMEM)
    args = list(blocks) + [ocean]
    specs = [pl.BlockSpec(memory_space=pl.ANY)] * len(blocks) + [vmem]
    if before is not None:
        args.append(before)
        specs.append(vmem)
    return pl.pallas_call(
        kernel,
        out_shape=jax.ShapeDtypeStruct(sums_shape, jnp.float32),
        in_specs=specs,
        out_specs=vmem,
        scratch_shapes=[pltpu.VMEM((rows, depth), jnp.bfloat16)]
        + [pltpu.VMEM((rows, width), jnp.float32) for width in scratch]
        + [pltpu.SemaphoreType.DMA((len(blocks),))],
        input_output_aliases={} if before is None else {len(args) - 1: 0},
        compiler_params=pltpu.CompilerParams(vmem_limit_bytes=24 * 1024 * 1024),
        cost_estimate=pl.CostEstimate(
            flops=2 * rows * depth * cols, bytes_accessed=2 * depth * (rows + cols), transcendentals=0
        ),
    )(*args)


def finish_kernel(members, parts_ref, cutoff_ref, index_ref, table_ref, out_ref):
    own, cols = out_ref.shape
    total = jnp.sum(parts_ref[...], axis=0)
    eye = lax.broadcasted_iota(jnp.int32, (own, own), 0) == lax.broadcasted_iota(jnp.int32, (own, own), 1)
    half = own // 2
    across = jnp.concatenate([total[own : own + 1, :half], total[own + 1 : own + 2, :half]], axis=1)
    rowsq = jnp.sum(jnp.where(eye, across, 0.0), axis=1, keepdims=True)
    vx = rowsq / (members - 1.0) + 1e-06
    vy = total[own + 2 : own + 3] / (members - 1.0) + 1e-06
    corr = total[:own] / (members - 1.0) / jnp.sqrt(vx * vy)
    for i in range(own // TR):
        for j in range(cols // TV):
            weight = cutoff_ref[i, j].astype(jnp.float32) * table_ref[index_ref[i, j]]
            tile = (slice(i * TR, (i + 1) * TR), slice(j * TV, (j + 1) * TV))
            out_ref[tile] = corr[tile] * weight


def per_device(panel, ocean, cutoff, factor_index, factor_table):
    n_mem = lax.axis_size("mem")
    rows_all = panel.shape[1] * lax.axis_size("ocn")
    own_rows = rows_all // n_mem
    members = panel.shape[0] * n_mem
    mine = panel.T
    per = mine.shape[0]
    half = per // 2
    lo, hi = (0, half), (half, half)
    head, tail = mine[:, :-TAIL], mine[:, -TAIL:]
    first = jnp.concatenate([head, y_shift(head, 1)], axis=0)
    second = jnp.concatenate([y_shift(head, -1), y_shift(head, 2)], axis=0)
    tail = z_spread(tail)
    first, second, tail = lax.optimization_barrier((first, second, tail))
    tails = [tail, y_shift(tail, 1), y_shift(tail, -1), y_shift(tail, 2)]

    def parts_1(dz):
        return ((0, dz), (-1, dz))

    def parts_2(dz):
        return ((1, dz), (2, dz))

    early = [(first, parts_1(0)), (second, parts_2(0))]
    late = []
    up_1 = down_1 = first
    up_2 = down_2 = second
    for s in (1, 2, 3):
        up_1, down_1 = z_shift(up_1, 1), z_shift(down_1, -1)
        up_2, down_2 = z_shift(up_2, 1), z_shift(down_2, -1)
        (early if s < 3 else late).extend(
            [(up_1, parts_1(-s)), (down_1, parts_1(s)), (up_2, parts_2(-s)), (down_2, parts_2(s))]
        )
    late += [(z_shift(up_1, 1), parts_1(-4)), (z_shift(down_2, -1), parts_2(4))]

    cols = ocean.shape[1]
    sums_shape = (n_mem, own_rows + EXTRA, cols)
    parts = cross(tail_kernel, tails, ocean, sums_shape, ())
    for pieces in (early, late):
        kernel = functools.partial(head_kernel, [g for _, g in pieces])
        parts = cross(kernel, [a for a, _ in pieces], ocean, sums_shape, (cols, 128), parts)
    parts = lax.all_to_all(parts, "mem", split_axis=0, concat_axis=0, tiled=True)
    return pl.pallas_call(
        lambda *refs: finish_kernel(members, *refs),
        out_shape=jax.ShapeDtypeStruct((own_rows, ocean.shape[1]), jnp.float32),
        in_specs=[pl.BlockSpec(memory_space=pltpu.VMEM)] + [pl.BlockSpec(memory_space=pltpu.SMEM)] * 3,
        out_specs=pl.BlockSpec(memory_space=pltpu.VMEM),
        compiler_params=pltpu.CompilerParams(vmem_limit_bytes=16 * 1024 * 1024),
    )(parts, cutoff, factor_index, factor_table)


def solution(mesh):
    in_specs = (P("mem", "ocn"), P("mem", "ocn"), P("mem", "ocn"), P("mem", "ocn"), P())
    out_specs = P("mem", "ocn")
    return jax.shard_map(
        per_device, mesh=mesh, in_specs=in_specs, out_specs=out_specs, check_vma=False
    )
```

time: 150 us -> 142 us (0.947)
  waiting for transfers between devices: 44.6 us -> 15.7 us
  starting transfers between devices: 69.8 us -> 87.2 us
  Pallas kernels: 6.46 us -> 10.2 us
  blocking collectives: 26.1 us -> 22.5 us
  local copies, waits for them, and re-layouts: 0.14 us -> 2.54 us
    ppermute x16 -> x14, waiting for transfers between devices: 32.1 us -> 0.04 us  [z_shift(): return lax.ppermute(x, 'ocn', perm)]
    ppermute x3 -> x6, starting transfers between devices: 12.7 us -> 27.4 us  [y_shift(): return lax.ppermute(x, 'ocn', perm)]
    all_to_all x0 -> x1, waiting for transfers between devices: none -> 13.1 us  [z_spread(): lax.all_to_all(copies, 'ocn', split_axis=0, concat_axis=0, axis_index_gro...]
    all_to_all x0 -> x1, starting transfers between devices: none -> 10.4 us  [z_spread(): lax.all_to_all(copies, 'ocn', split_axis=0, concat_axis=0, axis_index_gro...]
    ppermute x3 -> x6, waiting for transfers between devices: 12.5 us -> 2.56 us  [y_shift(): return lax.ppermute(x, 'ocn', perm)]
    ppermute x16 -> x14, starting transfers between devices: 57.1 us -> 49.4 us  [z_shift(): return lax.ppermute(x, 'ocn', perm)]
    pallas_call x2 -> x3, Pallas kernels: 5.08 us -> 8.87 us  [cross(): pl.pallas_call(kernel, out_shape=jax.ShapeDtypeStruct(sums_shape, jnp.flo...]
    all_to_all x1, blocking collectives: 26.1 us -> 22.5 us  [per_device(): lax.all_to_all(parts, 'mem', split_axis=0, concat_axis=0, tiled=True)]
  transfers between devices with their start and end apart: 19 -> 21, of which waited for: 17 -> 2; matrix products, arithmetic and copies ran while one was open for 0% -> 2% of each run, Pallas kernels for 2% -> 4%
where the time goes in v3:
time: 142 us; the launch traced here: 140 us
  starting transfers between devices  87.2 us (61%)
  blocking collectives  22.5 us (16%)
  waiting for transfers between devices  15.7 us (11%)
  Pallas kernels  10.2 us (7%)
  local copies, waits for them, and re-layouts  2.54 us (2%)
    ppermute x14, starting transfers between devices, z_shift(): return lax.ppermute(x, 'ocn', perm)  49.4 us
    ppermute x6, starting transfers between devices, y_shift(): return lax.ppermute(x, 'ocn', perm)  27.4 us
    all_to_all x1, blocking collectives, per_device(): lax.all_to_all(parts, 'mem', split_axis=0, concat_axis=0, tiled=True)  22.5 us
    all_to_all x1, waiting for transfers between devices, z_spread(): lax.all_to_all(copies, 'ocn', split_axis=0, concat_axis=0, axis_index_gro...  13.1 us
    all_to_all x1, starting transfers between devices, z_spread(): lax.all_to_all(copies, 'ocn', split_axis=0, concat_axis=0, axis_index_gro...  10.4 us
    pallas_call x3, Pallas kernels, cross(): pl.pallas_call(kernel, out_shape=jax.ShapeDtypeStruct(sums_shape, jnp.flo...  8.87 us
  transfers between devices with their start and end apart: 21, of which 2 were waited for; matrix products, arithmetic and copies ran while one was open for 2% of the time, Pallas kernels for 4%

profile of v3, /device:TPU:56, one launch (start us, length us, event | category | flops | bytes accessed | tf_op | source)
XLA Modules:
  0.0 139.5 jit_solution(8315770087144386611)
XLA Ops:
  0.0 0.9 slice.8
  0.9 2.7 %collective-permute-start = (bf16[32,3328]{1,0:T(8,128)(2,1)S(1)}, bf16[32,3328]{1,0:T(8,128)(2,1)S(1)}, u32[]{:S(2)}, u32[]{:S(2)}) collective-permute-start(bf16[32,3328]{1,0:T(8,128)(2,1)S(1)} %slice.8), channel_id=1, source_target_pairs={{0,8},{1,9},{2,10},{3,11},{4,12},{5,13},{6,14},{7,15},{8,16},{9,17... | collective-permute-start | bytes 638984 | tf_op jit(solution)/shard_map/ppermute | solution.py:25
  3.6 4.1 %collective-permute-start.1 = (bf16[32,3328]{1,0:T(8,128)(2,1)S(1)}, bf16[32,3328]{1,0:T(8,128)(2,1)S(1)}, u32[]{:S(2)}, u32[]{:S(2)}) collective-permute-start(bf16[32,3328]{1,0:T(8,128)(2,1)S(1)} %slice.8), channel_id=1, source_target_pairs={{0,24},{1,25},{2,26},{3,27},{4,28},{5,29},{6,30},{7,31},{8,0},{9,1... | collective-permute-start | bytes 638984 | tf_op jit(solution)/shard_map/ppermute | solution.py:25
  7.7 4.7 %collective-permute-start.2 = (bf16[32,3328]{1,0:T(8,128)(2,1)S(1)}, bf16[32,3328]{1,0:T(8,128)(2,1)}, u32[]{:S(2)}, u32[]{:S(2)}) collective-permute-start(bf16[32,3328]{1,0:T(8,128)(2,1)S(1)} %slice.8), channel_id=1, source_target_pairs={{0,16},{1,17},{2,18},{3,19},{4,20},{5,21},{6,22},{7,23},{8,24},{9,... | collective-permute-start | bytes 638984 | tf_op jit(solution)/shard_map/ppermute | solution.py:25
  12.4 0.8 slice.9
  13.2 0.8 broadcast_in_dim.2
  14.0 10.4 %all-to-all-start = ((bf16[8,32,768]{2,1,0:T(8,128)(2,1)}), bf16[8,32,768]{2,1,0:T(8,128)(2,1)S(1)}, u32[]{:S(2)}, u32[]{:S(2)}) async-start(bf16[8,32,768]{2,1,0:T(8,128)(2,1)} %broadcast_in_dim.2), calls=%async_computation | async-start | bytes 786432 | tf_op jit(solution)/shard_map/all_to_all | solution.py:31
  24.5 1.0 pad_maximum_fusion.1.refs_1_
  25.5 13.1 %all-to-all-done = bf16[8,32,768]{2,1,0:T(8,128)(2,1)S(1)} async-done(((bf16[8,32,768]{2,1,0:T(8,128)(2,1)}), bf16[8,32,768]{2,1,0:T(8,128)(2,1)S(1)}, u32[]{:S(2)}, u32[]{:S(2)}) %all-to-all-start) | async-done | bytes 393248 | tf_op jit(solution)/shard_map/all_to_all | solution.py:31
  38.6 2.5 %collective-permute-start.3 = (bf16[64,3328]{1,0:T(8,128)(2,1)S(1)}, bf16[64,3328]{1,0:T(8,128)(2,1)S(1)}, u32[]{:S(2)}, u32[]{:S(2)}) collective-permute-start(bf16[64,3328]{1,0:T(8,128)(2,1)S(1)} %pad_maximum_fusion.refs_0_), channel_id=1, source_target_pairs={{0,1},{1,2},{2,3},{3,4},{4,5},{5,6},{6,7},{7,0},{8,9},{9,10},{10,1... | collective-permute-start | bytes 1277960 | tf_op jit(solution)/shard_map/ppermute | solution.py:20
  41.0 4.6 %collective-permute-start.12 = (bf16[64,3328]{1,0:T(8,128)(2,1)S(1)}, bf16[64,3328]{1,0:T(8,128)(2,1)S(1)}, u32[]{:S(2)}, u32[]{:S(2)}) collective-permute-start(bf16[64,3328]{1,0:T(8,128)(2,1)S(1)} %pad_maximum_fusion.1.refs_1_), channel_id=1, source_target_pairs={{0,7},{1,0},{2,1},{3,2},{4,3},{5,4},{6,5},{7,6},{8,15},{9,8},{10,9... | collective-permute-start | bytes 1277960 | tf_op jit(solution)/shard_map/ppermute | solution.py:20
  45.6 5.8 %collective-permute-start.17 = (bf16[256,768]{1,0:T(8,128)(2,1)S(1)}, bf16[256,768]{1,0:T(8,128)(2,1)S(1)}, u32[]{:S(2)}, u32[]{:S(2)}) collective-permute-start(bf16[256,768]{1,0:T(8,128)(2,1)S(1)} %bitcast.2), channel_id=1, source_target_pairs={{0,8},{1,9},{2,10},{3,11},{4,12},{5,13},{6,14},{7,15},{8,16},{9,17... | collective-permute-start | bytes 1179656 | tf_op jit(solution)/shard_map/ppermute | solution.py:25
  51.4 1.9 %collective-permute-start.9 = (bf16[64,3328]{1,0:T(8,128)(2,1)S(1)}, bf16[64,3328]{1,0:T(8,128)(2,1)S(1)}, u32[]{:S(2)}, u32[]{:S(2)}) collective-permute-start(bf16[64,3328]{1,0:T(8,128)(2,1)S(1)} %pad_maximum_fusion.1.refs_1_), channel_id=1, source_target_pairs={{0,1},{1,2},{2,3},{3,4},{4,5},{5,6},{6,7},{7,0},{8,9},{9,10},{10,1... | collective-permute-start | bytes 1277960 | tf_op jit(solution)/shard_map/ppermute | solution.py:20
  53.3 5.1 %collective-permute-start.6 = (bf16[64,3328]{1,0:T(8,128)(2,1)S(1)}, bf16[64,3328]{1,0:T(8,128)(2,1)S(1)}, u32[]{:S(2)}, u32[]{:S(2)}) collective-permute-start(bf16[64,3328]{1,0:T(8,128)(2,1)S(1)} %pad_maximum_fusion.refs_0_), channel_id=1, source_target_pairs={{0,7},{1,0},{2,1},{3,2},{4,3},{5,4},{6,5},{7,6},{8,15},{9,8},{10,9... | collective-permute-start | bytes 1277960 | tf_op jit(solution)/shard_map/ppermute | solution.py:20
  58.5 1.9 %collective-permute-start.4 = (bf16[64,3328]{1,0:T(8,128)(2,1)S(1)}, bf16[64,3328]{1,0:T(8,128)(2,1)S(1)}, u32[]{:S(2)}, u32[]{:S(2)}) collective-permute-start(bf16[64,3328]{1,0:T(8,128)(2,1)S(1)} %collective-permute-done.3.refs_2_), channel_id=1, source_target_pairs={{0,1},{1,2},{2,3},{3,4},{4,5},{5,6},{6,7},{7,0},{8,9},{9,10},{10,1... | collective-permute-start | bytes 1277960 | tf_op jit(solution)/shard_map/ppermute | solution.py:20
  60.4 5.1 %collective-permute-start.13 = (bf16[64,3328]{1,0:T(8,128)(2,1)S(1)}, bf16[64,3328]{1,0:T(8,128)(2,1)S(1)}, u32[]{:S(2)}, u32[]{:S(2)}) collective-permute-start(bf16[64,3328]{1,0:T(8,128)(2,1)S(1)} %collective-permute-done.12.refs_5_), channel_id=1, source_target_pairs={{0,7},{1,0},{2,1},{3,2},{4,3},{5,4},{6,5},{7,6},{8,15},{9,8},{10,9... | collective-permute-start | bytes 1277960 | tf_op jit(solution)/shard_map/ppermute | solution.py:20
  65.6 4.0 %collective-permute-start.18 = (bf16[256,768]{1,0:T(8,128)(2,1)S(1)}, bf16[256,768]{1,0:T(8,128)(2,1)S(1)}, u32[]{:S(2)}, u32[]{:S(2)}) collective-permute-start(bf16[256,768]{1,0:T(8,128)(2,1)S(1)} %bitcast.3), channel_id=1, source_target_pairs={{0,24},{1,25},{2,26},{3,27},{4,28},{5,29},{6,30},{7,31},{8,0},{9,1... | collective-permute-start | bytes 1179656 | tf_op jit(solution)/shard_map/ppermute | solution.py:25
  69.6 1.9 %collective-permute-start.10 = (bf16[64,3328]{1,0:T(8,128)(2,1)S(1)}, bf16[64,3328]{1,0:T(8,128)(2,1)S(1)}, u32[]{:S(2)}, u32[]{:S(2)}) collective-permute-start(bf16[64,3328]{1,0:T(8,128)(2,1)S(1)} %collective-permute-done.9.refs_4_), channel_id=1, source_target_pairs={{0,1},{1,2},{2,3},{3,4},{4,5},{5,6},{6,7},{7,0},{8,9},{9,10},{10,1... | collective-permute-start | bytes 1277960 | tf_op jit(solution)/shard_map/ppermute | solution.py:20
  71.5 5.1 %collective-permute-start.7 = (bf16[64,3328]{1,0:T(8,128)(2,1)S(1)}, bf16[64,3328]{1,0:T(8,128)(2,1)S(1)}, u32[]{:S(2)}, u32[]{:S(2)}) collective-permute-start(bf16[64,3328]{1,0:T(8,128)(2,1)S(1)} %collective-permute-done.6.refs_3_), channel_id=1, source_target_pairs={{0,7},{1,0},{2,1},{3,2},{4,3},{5,4},{6,5},{7,6},{8,15},{9,8},{10,9... | collective-permute-start | bytes 1277960 | tf_op jit(solution)/shard_map/ppermute | solution.py:20
  76.7 1.9 %collective-permute-start.5 = (bf16[64,3328]{1,0:T(8,128)(2,1)S(1)}, bf16[64,3328]{1,0:T(8,128)(2,1)S(1)}, u32[]{:S(2)}, u32[]{:S(2)}) collective-permute-start(bf16[64,3328]{1,0:T(8,128)(2,1)S(1)} %collective-permute-done.4.refs_6_), channel_id=1, source_target_pairs={{0,1},{1,2},{2,3},{3,4},{4,5},{5,6},{6,7},{7,0},{8,9},{9,10},{10,1... | collective-permute-start | bytes 1277960 | tf_op jit(solution)/shard_map/ppermute | solution.py:20
  78.6 5.1 %collective-permute-start.14 = (bf16[64,3328]{1,0:T(8,128)(2,1)S(1)}, bf16[64,3328]{1,0:T(8,128)(2,1)S(1)}, u32[]{:S(2)}, u32[]{:S(2)}) collective-permute-start(bf16[64,3328]{1,0:T(8,128)(2,1)S(1)} %collective-permute-done.13.refs_9_), channel_id=1, source_target_pairs={{0,7},{1,0},{2,1},{3,2},{4,3},{5,4},{6,5},{7,6},{8,15},{9,8},{10,9... | collective-permute-start | bytes 1277960 | tf_op jit(solution)/shard_map/ppermute | solution.py:20
  83.8 6.2 %collective-permute-start.19 = (bf16[256,768]{1,0:T(8,128)(2,1)S(1)}, bf16[256,768]{1,0:T(8,128)(2,1)S(1)}, u32[]{:S(2)}, u32[]{:S(2)}) collective-permute-start(bf16[256,768]{1,0:T(8,128)(2,1)S(1)} %bitcast.4), channel_id=1, source_target_pairs={{0,16},{1,17},{2,18},{3,19},{4,20},{5,21},{6,22},{7,23},{8,24},{9,... | collective-permute-start | bytes 1179656 | tf_op jit(solution)/shard_map/ppermute | solution.py:25
  90.0 1.9 %collective-permute-start.11 = (bf16[64,3328]{1,0:T(8,128)(2,1)S(1)}, bf16[64,3328]{1,0:T(8,128)(2,1)S(1)}, u32[]{:S(2)}, u32[]{:S(2)}) collective-permute-start(bf16[64,3328]{1,0:T(8,128)(2,1)S(1)} %collective-permute-done.10.refs_8_), channel_id=1, source_target_pairs={{0,1},{1,2},{2,3},{3,4},{4,5},{5,6},{6,7},{7,0},{8,9},{9,10},{10,1... | collective-permute-start | bytes 1277960 | tf_op jit(solution)/shard_map/ppermute | solution.py:20
  91.9 5.1 %collective-permute-start.8 = (bf16[64,3328]{1,0:T(8,128)(2,1)S(1)}, bf16[64,3328]{1,0:T(8,128)(2,1)S(1)}, u32[]{:S(2)}, u32[]{:S(2)}) collective-permute-start(bf16[64,3328]{1,0:T(8,128)(2,1)S(1)} %collective-permute-done.7.refs_7_), channel_id=1, source_target_pairs={{0,7},{1,0},{2,1},{3,2},{4,3},{5,4},{6,5},{7,6},{8,15},{9,8},{10,9... | collective-permute-start | bytes 1277960 | tf_op jit(solution)/shard_map/ppermute | solution.py:20
  97.1 1.9 %collective-permute-start.15 = (bf16[64,3328]{1,0:T(8,128)(2,1)S(1)}, bf16[64,3328]{1,0:T(8,128)(2,1)S(1)}, u32[]{:S(2)}, u32[]{:S(2)}) collective-permute-start(bf16[64,3328]{1,0:T(8,128)(2,1)S(1)} %collective-permute-done.5.refs_0_), channel_id=1, source_target_pairs={{0,1},{1,2},{2,3},{3,4},{4,5},{5,6},{6,7},{7,0},{8,9},{9,10},{10,1... | collective-permute-start | bytes 1277960 | tf_op jit(solution)/shard_map/ppermute | solution.py:20
  99.0 5.1 %collective-permute-start.16 = (bf16[64,3328]{1,0:T(8,128)(2,1)S(1)}, bf16[64,3328]{1,0:T(8,128)(2,1)S(1)}, u32[]{:S(2)}, u32[]{:S(2)}) collective-permute-start(bf16[64,3328]{1,0:T(8,128)(2,1)S(1)} %collective-permute-done.14.refs_3_), channel_id=1, source_target_pairs={{0,7},{1,0},{2,1},{3,2},{4,3},{5,4},{6,5},{7,6},{8,15},{9,8},{10,9... | collective-permute-start | bytes 1277960 | tf_op jit(solution)/shard_map/ppermute | solution.py:20
  104.2 2.5 %collective-permute-done.19.refs_3_ = bf16[256,768]{1,0:T(8,128)(2,1)S(1)} collective-permute-done((bf16[256,768]{1,0:T(8,128)(2,1)S(1)}, bf16[256,768]{1,0:T(8,128)(2,1)S(1)}, u32[]{:S(2)}, u32[]{:S(2)}) %collective-permute-start.19) | collective-permute-done | bytes 393248 | tf_op jit(solution)/shard_map/ppermute | solution.py:25
  106.7 2.2 %shard_map.55.refs_11_ = f32[16,72,256]{2,1,0:T(8,128)S(1)} custom-call(bf16[256,768]{1,0:T(8,128)(2,1)S(1)} %bitcast.5, bf16[256,768]{1,0:T(8,128)(2,1)S(1)} %collective-permute-done.17.refs_1_, bf16[256,768]{1,0:T(8,128)(2,1)S(1)} %collective-permute-done.18.refs_2_, bf16[256,768]{1,0:T(8,128)(2,1)S(1)} %collective-permute-done.19.refs_3_, ...), custom_call_target="tpu_custom_call" | custom-call | flops 402653184 | bytes 1966080 | tf_op jit(solution)/shard_map/pallas_call | solution.py:128
  108.9 4.1 %shard_map.56.refs_7_ = f32[16,72,256]{2,1,0:T(8,128)S(1)} custom-call(bf16[64,3328]{1,0:T(8,128)(2,1)S(1)} %pad_maximum_fusion.refs_0_, bf16[64,3328]{1,0:T(8,128)(2,1)S(1)} %pad_maximum_fusion.1.refs_1_, bf16[64,3328]{1,0:T(8,128)(2,1)S(1)} %collective-permute-done.3.refs_2_, ...), custom_call_target="tpu_custom_call", output_to_operand_aliasing={{}: (11, {})} | custom-call | flops 1090519040 | bytes 5963776 | tf_op jit(solution)/shard_map/pallas_call | solution.py:128
  113.0 2.6 %shard_map.57 = f32[16,72,256]{2,1,0:T(8,128)S(1)} custom-call(bf16[64,3328]{1,0:T(8,128)(2,1)S(1)} %collective-permute-done.5.refs_0_, bf16[64,3328]{1,0:T(8,128)(2,1)S(1)} %collective-permute-done.8.refs_1_, bf16[64,3328]{1,0:T(8,128)(2,1)S(1)} %collective-permute-done.11.refs_2_, ...), custom_call_target="tpu_custom_call", output_to_operand_aliasing={{}: (7, {})} | custom-call | flops 654311424 | bytes 4259840 | tf_op jit(solution)/shard_map/pallas_call | solution.py:128
  115.7 22.5 %all_to_all.14.refs_0_ = f32[16,72,256]{2,1,0:T(8,128)S(1)} all-to-all(f32[16,72,256]{2,1,0:T(8,128)S(1)} %shard_map.57), channel_id=1, replica_groups=mesh['mem'=16,'ocn'=32] {'mem'}, dimensions={0} | all-to-all | bytes 2359296 | tf_op jit(solution)/shard_map/all_to_all | solution.py:201
  138.2 1.4 shard_map.58
  (28 shorter events, 0.1 us)
Async XLA Ops:
  0.9 23.5 %collective-permute-start = (bf16[32,3328]{1,0:T(8,128)(2,1)S(1)}, bf16[32,3328]{1,0:T(8,128)(2,1)S(1)}, u32[]{:S(2)}, u32[]{:S(2)}) collective-permute-start(bf16[32,3328]{1,0:T(8,128)(2,1)S(1)} %slice.8), channel_id=1, source_target_pairs={{0,8},{1,9},{2,10},{3,11},{4,12},{5,13},{6,14},{7,15},{8,16},{9,17... | collective-permute-start | bytes 638984 | tf_op jit(solution)/shard_map/ppermute | solution.py:25
  3.6 20.9 %collective-permute-start.1 = (bf16[32,3328]{1,0:T(8,128)(2,1)S(1)}, bf16[32,3328]{1,0:T(8,128)(2,1)S(1)}, u32[]{:S(2)}, u32[]{:S(2)}) collective-permute-start(bf16[32,3328]{1,0:T(8,128)(2,1)S(1)} %slice.8), channel_id=1, source_target_pairs={{0,24},{1,25},{2,26},{3,27},{4,28},{5,29},{6,30},{7,31},{8,0},{9,1... | collective-permute-start | bytes 638984 | tf_op jit(solution)/shard_map/ppermute | solution.py:25
  7.7 16.8 %collective-permute-start.2 = (bf16[32,3328]{1,0:T(8,128)(2,1)S(1)}, bf16[32,3328]{1,0:T(8,128)(2,1)}, u32[]{:S(2)}, u32[]{:S(2)}) collective-permute-start(bf16[32,3328]{1,0:T(8,128)(2,1)S(1)} %slice.8), channel_id=1, source_target_pairs={{0,16},{1,17},{2,18},{3,19},{4,20},{5,21},{6,22},{7,23},{8,24},{9,... | collective-permute-start | bytes 638984 | tf_op jit(solution)/shard_map/ppermute | solution.py:25
  14.0 92.7 %copy-start = (bf16[4096,256]{1,0:T(8,128)(2,1)S(1)}, bf16[4096,256]{1,0:T(8,128)(2,1)}, u32[]{:S(2)}) copy-start(bf16[4096,256]{1,0:T(8,128)(2,1)} %refs_6_.1) | copy-start | bytes 6291460
  14.0 24.6 %all-to-all-start = ((bf16[8,32,768]{2,1,0:T(8,128)(2,1)}), bf16[8,32,768]{2,1,0:T(8,128)(2,1)S(1)}, u32[]{:S(2)}, u32[]{:S(2)}) async-start(bf16[8,32,768]{2,1,0:T(8,128)(2,1)} %broadcast_in_dim.2), calls=%async_computation | async-start | bytes 786432 | tf_op jit(solution)/shard_map/all_to_all | solution.py:31
  38.6 19.9 %collective-permute-start.3 = (bf16[64,3328]{1,0:T(8,128)(2,1)S(1)}, bf16[64,3328]{1,0:T(8,128)(2,1)S(1)}, u32[]{:S(2)}, u32[]{:S(2)}) collective-permute-start(bf16[64,3328]{1,0:T(8,128)(2,1)S(1)} %pad_maximum_fusion.refs_0_), channel_id=1, source_target_pairs={{0,1},{1,2},{2,3},{3,4},{4,5},{5,6},{6,7},{7,0},{8,9},{9,10},{10,1... | collective-permute-start | bytes 1277960 | tf_op jit(solution)/shard_map/ppermute | solution.py:20
  41.0 19.4 %collective-permute-start.12 = (bf16[64,3328]{1,0:T(8,128)(2,1)S(1)}, bf16[64,3328]{1,0:T(8,128)(2,1)S(1)}, u32[]{:S(2)}, u32[]{:S(2)}) collective-permute-start(bf16[64,3328]{1,0:T(8,128)(2,1)S(1)} %pad_maximum_fusion.1.refs_1_), channel_id=1, source_target_pairs={{0,7},{1,0},{2,1},{3,2},{4,3},{5,4},{6,5},{7,6},{8,15},{9,8},{10,9... | collective-permute-start | bytes 1277960 | tf_op jit(solution)/shard_map/ppermute | solution.py:20
  45.6 19.9 %collective-permute-start.17 = (bf16[256,768]{1,0:T(8,128)(2,1)S(1)}, bf16[256,768]{1,0:T(8,128)(2,1)S(1)}, u32[]{:S(2)}, u32[]{:S(2)}) collective-permute-start(bf16[256,768]{1,0:T(8,128)(2,1)S(1)} %bitcast.2), channel_id=1, source_target_pairs={{0,8},{1,9},{2,10},{3,11},{4,12},{5,13},{6,14},{7,15},{8,16},{9,17... | collective-permute-start | bytes 1179656 | tf_op jit(solution)/shard_map/ppermute | solution.py:25
  51.4 18.2 %collective-permute-start.9 = (bf16[64,3328]{1,0:T(8,128)(2,1)S(1)}, bf16[64,3328]{1,0:T(8,128)(2,1)S(1)}, u32[]{:S(2)}, u32[]{:S(2)}) collective-permute-start(bf16[64,3328]{1,0:T(8,128)(2,1)S(1)} %pad_maximum_fusion.1.refs_1_), channel_id=1, source_target_pairs={{0,1},{1,2},{2,3},{3,4},{4,5},{5,6},{6,7},{7,0},{8,9},{9,10},{10,1... | collective-permute-start | bytes 1277960 | tf_op jit(solution)/shard_map/ppermute | solution.py:20
  53.3 18.2 %collective-permute-start.6 = (bf16[64,3328]{1,0:T(8,128)(2,1)S(1)}, bf16[64,3328]{1,0:T(8,128)(2,1)S(1)}, u32[]{:S(2)}, u32[]{:S(2)}) collective-permute-start(bf16[64,3328]{1,0:T(8,128)(2,1)S(1)} %pad_maximum_fusion.refs_0_), channel_id=1, source_target_pairs={{0,7},{1,0},{2,1},{3,2},{4,3},{5,4},{6,5},{7,6},{8,15},{9,8},{10,9... | collective-permute-start | bytes 1277960 | tf_op jit(solution)/shard_map/ppermute | solution.py:20
  58.5 18.2 %collective-permute-start.4 = (bf16[64,3328]{1,0:T(8,128)(2,1)S(1)}, bf16[64,3328]{1,0:T(8,128)(2,1)S(1)}, u32[]{:S(2)}, u32[]{:S(2)}) collective-permute-start(bf16[64,3328]{1,0:T(8,128)(2,1)S(1)} %collective-permute-done.3.refs_2_), channel_id=1, source_target_pairs={{0,1},{1,2},{2,3},{3,4},{4,5},{5,6},{6,7},{7,0},{8,9},{9,10},{10,1... | collective-permute-start | bytes 1277960 | tf_op jit(solution)/shard_map/ppermute | solution.py:20
  60.4 18.2 %collective-permute-start.13 = (bf16[64,3328]{1,0:T(8,128)(2,1)S(1)}, bf16[64,3328]{1,0:T(8,128)(2,1)S(1)}, u32[]{:S(2)}, u32[]{:S(2)}) collective-permute-start(bf16[64,3328]{1,0:T(8,128)(2,1)S(1)} %collective-permute-done.12.refs_5_), channel_id=1, source_target_pairs={{0,7},{1,0},{2,1},{3,2},{4,3},{5,4},{6,5},{7,6},{8,15},{9,8},{10,9... | collective-permute-start | bytes 1277960 | tf_op jit(solution)/shard_map/ppermute | solution.py:20
  65.6 18.2 %collective-permute-start.18 = (bf16[256,768]{1,0:T(8,128)(2,1)S(1)}, bf16[256,768]{1,0:T(8,128)(2,1)S(1)}, u32[]{:S(2)}, u32[]{:S(2)}) collective-permute-start(bf16[256,768]{1,0:T(8,128)(2,1)S(1)} %bitcast.3), channel_id=1, source_target_pairs={{0,24},{1,25},{2,26},{3,27},{4,28},{5,29},{6,30},{7,31},{8,0},{9,1... | collective-permute-start | bytes 1179656 | tf_op jit(solution)/shard_map/ppermute | solution.py:25
  69.6 20.4 %collective-permute-start.10 = (bf16[64,3328]{1,0:T(8,128)(2,1)S(1)}, bf16[64,3328]{1,0:T(8,128)(2,1)S(1)}, u32[]{:S(2)}, u32[]{:S(2)}) collective-permute-start(bf16[64,3328]{1,0:T(8,128)(2,1)S(1)} %collective-permute-done.9.refs_4_), channel_id=1, source_target_pairs={{0,1},{1,2},{2,3},{3,4},{4,5},{5,6},{6,7},{7,0},{8,9},{9,10},{10,1... | collective-permute-start | bytes 1277960 | tf_op jit(solution)/shard_map/ppermute | solution.py:20
  71.5 20.4 %collective-permute-start.7 = (bf16[64,3328]{1,0:T(8,128)(2,1)S(1)}, bf16[64,3328]{1,0:T(8,128)(2,1)S(1)}, u32[]{:S(2)}, u32[]{:S(2)}) collective-permute-start(bf16[64,3328]{1,0:T(8,128)(2,1)S(1)} %collective-permute-done.6.refs_3_), channel_id=1, source_target_pairs={{0,7},{1,0},{2,1},{3,2},{4,3},{5,4},{6,5},{7,6},{8,15},{9,8},{10,9... | collective-permute-start | bytes 1277960 | tf_op jit(solution)/shard_map/ppermute | solution.py:20
  76.7 20.4 %collective-permute-start.5 = (bf16[64,3328]{1,0:T(8,128)(2,1)S(1)}, bf16[64,3328]{1,0:T(8,128)(2,1)S(1)}, u32[]{:S(2)}, u32[]{:S(2)}) collective-permute-start(bf16[64,3328]{1,0:T(8,128)(2,1)S(1)} %collective-permute-done.4.refs_6_), channel_id=1, source_target_pairs={{0,1},{1,2},{2,3},{3,4},{4,5},{5,6},{6,7},{7,0},{8,9},{9,10},{10,1... | collective-permute-start | bytes 1277960 | tf_op jit(solution)/shard_map/ppermute | solution.py:20
  78.6 20.4 %collective-permute-start.14 = (bf16[64,3328]{1,0:T(8,128)(2,1)S(1)}, bf16[64,3328]{1,0:T(8,128)(2,1)S(1)}, u32[]{:S(2)}, u32[]{:S(2)}) collective-permute-start(bf16[64,3328]{1,0:T(8,128)(2,1)S(1)} %collective-permute-done.13.refs_9_), channel_id=1, source_target_pairs={{0,7},{1,0},{2,1},{3,2},{4,3},{5,4},{6,5},{7,6},{8,15},{9,8},{10,9... | collective-permute-start | bytes 1277960 | tf_op jit(solution)/shard_map/ppermute | solution.py:20
  83.8 23.0 %collective-permute-start.19 = (bf16[256,768]{1,0:T(8,128)(2,1)S(1)}, bf16[256,768]{1,0:T(8,128)(2,1)S(1)}, u32[]{:S(2)}, u32[]{:S(2)}) collective-permute-start(bf16[256,768]{1,0:T(8,128)(2,1)S(1)} %bitcast.4), channel_id=1, source_target_pairs={{0,16},{1,17},{2,18},{3,19},{4,20},{5,21},{6,22},{7,23},{8,24},{9,... | collective-permute-start | bytes 1179656 | tf_op jit(solution)/shard_map/ppermute | solution.py:25
  90.0 23.0 %collective-permute-start.11 = (bf16[64,3328]{1,0:T(8,128)(2,1)S(1)}, bf16[64,3328]{1,0:T(8,128)(2,1)S(1)}, u32[]{:S(2)}, u32[]{:S(2)}) collective-permute-start(bf16[64,3328]{1,0:T(8,128)(2,1)S(1)} %collective-permute-done.10.refs_8_), channel_id=1, source_target_pairs={{0,1},{1,2},{2,3},{3,4},{4,5},{5,6},{6,7},{7,0},{8,9},{9,10},{10,1... | collective-permute-start | bytes 1277960 | tf_op jit(solution)/shard_map/ppermute | solution.py:20
  91.9 21.1 %collective-permute-start.8 = (bf16[64,3328]{1,0:T(8,128)(2,1)S(1)}, bf16[64,3328]{1,0:T(8,128)(2,1)S(1)}, u32[]{:S(2)}, u32[]{:S(2)}) collective-permute-start(bf16[64,3328]{1,0:T(8,128)(2,1)S(1)} %collective-permute-done.7.refs_7_), channel_id=1, source_target_pairs={{0,7},{1,0},{2,1},{3,2},{4,3},{5,4},{6,5},{7,6},{8,15},{9,8},{10,9... | collective-permute-start | bytes 1277960 | tf_op jit(solution)/shard_map/ppermute | solution.py:20
  97.1 15.9 %collective-permute-start.15 = (bf16[64,3328]{1,0:T(8,128)(2,1)S(1)}, bf16[64,3328]{1,0:T(8,128)(2,1)S(1)}, u32[]{:S(2)}, u32[]{:S(2)}) collective-permute-start(bf16[64,3328]{1,0:T(8,128)(2,1)S(1)} %collective-permute-done.5.refs_0_), channel_id=1, source_target_pairs={{0,1},{1,2},{2,3},{3,4},{4,5},{5,6},{6,7},{7,0},{8,9},{9,10},{10,1... | collective-permute-start | bytes 1277960 | tf_op jit(solution)/shard_map/ppermute | solution.py:20
  99.0 14.0 %collective-permute-start.16 = (bf16[64,3328]{1,0:T(8,128)(2,1)S(1)}, bf16[64,3328]{1,0:T(8,128)(2,1)S(1)}, u32[]{:S(2)}, u32[]{:S(2)}) collective-permute-start(bf16[64,3328]{1,0:T(8,128)(2,1)S(1)} %collective-permute-done.14.refs_3_), channel_id=1, source_target_pairs={{0,7},{1,0},{2,1},{3,2},{4,3},{5,4},{6,5},{7,6},{8,15},{9,8},{10,9... | collective-permute-start | bytes 1277960 | tf_op jit(solution)/shard_map/ppermute | solution.py:20
  115.6 22.5 %copy-start.1 = (s32[1,2]{1,0:T(1,128)S(1)}, s32[1,2]{1,0:T(1,128)}, u32[]{:S(2)}) copy-start(s32[1,2]{1,0:T(1,128)} %refs_1_.1) | copy-start | bytes 28
  115.7 22.5 %copy-start.2 = (s32[1,2]{1,0:T(1,128)S(1)}, s32[1,2]{1,0:T(1,128)}, u32[]{:S(2)}) copy-start(s32[1,2]{1,0:T(1,128)} %refs_2_.1) | copy-start | bytes 28
  115.7 22.5 %copy-start.3 = (f32[8]{0:T(128)S(1)}, f32[8]{0:T(128)}, u32[]{:S(2)}) copy-start(f32[8]{0:T(128)} %refs_3_.1) | copy-start | bytes 100

commit v4 on v3

v4 whole, which is shorter than its diff:
```python
import functools

import jax
import jax.numpy as jnp
from jax import lax
from jax.experimental import pallas as pl
from jax.experimental.pallas import tpu as pltpu
from jax.sharding import PartitionSpec as P

TR = 64
TV = 128
NZ = 8
NY = 4
EXTRA = 8


def z_shift(x, d):
    perm = [(o, (o // NZ) * NZ + (o % NZ + d) % NZ) for o in range(NY * NZ)]
    return lax.ppermute(x, "ocn", perm)


def y_shift(x, d):
    perm = [(o, ((o // NZ + d) % NY) * NZ + o % NZ) for o in range(NY * NZ)]
    return lax.ppermute(x, "ocn", perm)


def square_sums(rows):
    rows_f = rows.astype(jnp.float32)
    return jnp.sum(rows_f * rows_f, axis=1, keepdims=True)


def along_lanes(column):
    shape = (column.shape[0], 128)
    here = lax.broadcasted_iota(jnp.int32, shape, 0) == lax.broadcasted_iota(jnp.int32, shape, 1)
    return jnp.sum(jnp.where(here, column, 0.0), axis=0, keepdims=True)


def cross_kernel(groups, starts, *refs):
    n = len(groups)
    blocks, near_ref, side_ref = refs[:n], refs[n], refs[n + 1]
    out_ref, rows_ref, cov_ref, sq_ref, sem = refs[-5:]
    own = out_ref.shape[2] - EXTRA
    per = own // 2
    cols = near_ref.shape[1]
    copies, placed = [], []
    for ref, parts in zip(blocks, groups):
        to = pl.ds(len(placed) * per, ref.shape[0])
        copies.append(pltpu.make_async_copy(ref, rows_ref.at[to], sem.at[len(copies)]))
        placed.extend(parts)
    for c in copies:
        c.start()
    if starts:
        line = lax.broadcasted_iota(jnp.int32, (EXTRA, cols), 0)
        for i, ref in enumerate((near_ref, side_ref)):
            ocean_f = ref[...].astype(jnp.float32)
            lines = jnp.where(line == 2, jnp.sum(ocean_f * ocean_f, axis=0, keepdims=True), 0.0)
            for m in range(2 * out_ref.shape[1]):
                out_ref[m % 2, m // 2, own:, i * cols : (i + 1) * cols] = lines
    for c in copies:
        c.wait()
    tile = rows_ref.shape[0] // 2

    @pl.loop(0, 2)
    def _(t):
        part = pl.ds(pl.multiple_of(t * tile, 16), tile)
        rows = rows_ref[part, :]
        cov_ref[part, :cols] = jnp.dot(rows, near_ref[...], preferred_element_type=jnp.float32)
        cov_ref[part, cols:] = jnp.dot(rows, side_ref[...], preferred_element_type=jnp.float32)
        sq_ref[part, :] = jnp.broadcast_to(square_sums(rows), (tile, 128))

    o = lax.axis_index("ocn")
    y, z = o // NZ, lax.rem(o, NZ)
    line = lax.broadcasted_iota(jnp.int32, (EXTRA, 128), 0)
    core = lax.rem(lax.axis_index("mem"), 2)
    for i, (dy, dz) in enumerate(placed):
        origin = lax.rem(y + (dy + NY), NY) * NZ + lax.rem(z + (dz + NZ), NZ)
        owner, side = origin // 2, lax.rem(origin, 2)
        to = (lax.rem(owner + core, 2), owner // 2)
        at = slice(i * per, (i + 1) * per)
        out_ref[(*to, pl.ds(pl.multiple_of(side * per, per), per))] = cov_ref[at, :]
        lines = jnp.where(line == side, along_lanes(sq_ref[at, :]), 0.0)
        out_ref[(*to, slice(own, None), slice(0, 128))] += lines
        out_ref[(*to, slice(own, None), slice(cols, cols + 128))] += lines


def cross(pieces, near, side, sums_shape, before=None):
    blocks, groups = [a for a, _ in pieces], [g for _, g in pieces]
    rows = sum(a.shape[0] for a in blocks)
    depth, cols = blocks[0].shape[1], near.shape[1] + side.shape[1]
    vmem = pl.BlockSpec(memory_space=pltpu.VMEM)
    args = blocks + [near, side]
    specs = [pl.BlockSpec(memory_space=pl.ANY)] * len(blocks) + [vmem, vmem]
    if before is not None:
        args.append(before)
        specs.append(vmem)
    return pl.pallas_call(
        functools.partial(cross_kernel, groups, before is None),
        out_shape=jax.ShapeDtypeStruct(sums_shape, jnp.float32),
        in_specs=specs,
        out_specs=vmem,
        scratch_shapes=[
            pltpu.VMEM((rows, depth), jnp.bfloat16),
            pltpu.VMEM((rows, cols), jnp.float32),
            pltpu.VMEM((rows, 128), jnp.float32),
            pltpu.SemaphoreType.DMA((len(blocks),)),
        ],
        input_output_aliases={} if before is None else {len(args) - 1: 0},
        compiler_params=pltpu.CompilerParams(vmem_limit_bytes=24 * 1024 * 1024),
        cost_estimate=pl.CostEstimate(
            flops=2 * rows * depth * cols, bytes_accessed=2 * depth * (rows + cols), transcendentals=0
        ),
    )(*args)


def sum_kernel(parts_ref, near_ref, left_ref, right_ref):
    total = jnp.sum(parts_ref[...], axis=0)
    cols = near_ref.shape[1]
    near_ref[...] = total[:, :cols]
    left_ref[...] = total[:, cols : cols + cols // 2]
    right_ref[...] = total[:, cols + cols // 2 :]


def finish_kernel(members, near_ref, low_ref, high_ref, cutoff_ref, index_ref, table_ref, out_ref):
    own, cols = out_ref.shape
    half = own // 2
    total = near_ref[...] + jnp.concatenate([low_ref[...], high_ref[...]], axis=1)
    squares = near_ref[own:, :128] + high_ref[own:, :]
    eye = lax.broadcasted_iota(jnp.int32, (own, own), 0) == lax.broadcasted_iota(jnp.int32, (own, own), 1)
    across = jnp.concatenate([squares[:1, :half], squares[1:2, :half]], axis=1)
    rowsq = jnp.sum(jnp.where(eye, across, 0.0), axis=1, keepdims=True)
    vx = rowsq / (members - 1.0) + 1e-06
    vy = total[own + 2 : own + 3] / (members - 1.0) + 1e-06
    corr = total[:own] / (members - 1.0) / jnp.sqrt(vx * vy)
    for i in range(own // TR):
        for j in range(cols // TV):
            weight = cutoff_ref[i, j].astype(jnp.float32) * table_ref[index_ref[i, j]]
            tile = (slice(i * TR, (i + 1) * TR), slice(j * TV, (j + 1) * TV))
            out_ref[tile] = corr[tile] * weight


def per_device(panel, ocean, cutoff, factor_index, factor_table):
    n_mem = lax.axis_size("mem")
    own_rows = panel.shape[1] * lax.axis_size("ocn") // n_mem
    members = panel.shape[0] * n_mem
    half, cols = panel.shape[0] // 2, ocean.shape[1]
    parity = lax.rem(lax.axis_index("ocn") // NZ, 2)
    mine = panel.T
    kept = lax.dynamic_slice_in_dim(mine, parity * half, half, 1)
    other = lax.dynamic_slice_in_dim(mine, (1 - parity) * half, half, 1)
    below, above, across = y_shift(other, 1), y_shift(other, -1), y_shift(kept, 2)
    first = jnp.concatenate([kept, below], axis=0)
    second = jnp.concatenate([above, across], axis=0)

    near = lax.dynamic_slice_in_dim(ocean, parity * half, half, 0)
    away = lax.dynamic_slice_in_dim(ocean, (1 - parity) * half, half, 0)
    below, away = lax.optimization_barrier((below, away))
    left, right = y_shift(away[:, cols // 2 :], 1), y_shift(away[:, : cols // 2], -1)
    side = jnp.concatenate([left, right], axis=1)

    def parts_1(dz):
        return ((0, dz), (-1, dz))

    def parts_2(dz):
        return ((1, dz), (2, dz))

    early = [(first, parts_1(0)), (second, parts_2(0))]
    late = []
    up_1 = down_1 = first
    up_2 = down_2 = second
    for s in (1, 2, 3):
        up_1, down_1 = z_shift(up_1, 1), z_shift(down_1, -1)
        up_2, down_2 = z_shift(up_2, 1), z_shift(down_2, -1)
        if s == 2:
            up_1, side = lax.optimization_barrier((up_1, side))
        (early if s < 3 else late).extend(
            [(up_1, parts_1(-s)), (down_1, parts_1(s)), (up_2, parts_2(-s)), (down_2, parts_2(s))]
        )
    late += [(z_shift(up_1, 1), parts_1(-4)), (z_shift(down_2, -1), parts_2(4))]

    sums_shape = (2, n_mem // 2, own_rows + EXTRA, 2 * cols)
    parts = cross(early, near, side, sums_shape)
    parts = cross(late, near, side, sums_shape, parts)
    parts = parts[0] + lax.ppermute(parts[1], "mem", [(m, m ^ 1) for m in range(n_mem)])
    groups = [list(range(c, n_mem, 2)) for c in range(2)]
    parts = lax.all_to_all(parts, "mem", split_axis=0, concat_axis=0, axis_index_groups=groups, tiled=True)
    vmem, smem = pl.BlockSpec(memory_space=pltpu.VMEM), pl.BlockSpec(memory_space=pltpu.SMEM)
    compiler_params = pltpu.CompilerParams(vmem_limit_bytes=16 * 1024 * 1024)
    here, to_left, to_right = pl.pallas_call(
        sum_kernel,
        out_shape=[jax.ShapeDtypeStruct((own_rows + EXTRA, n), jnp.float32) for n in (cols, cols // 2, cols // 2)],
        in_specs=[vmem],
        out_specs=[vmem] * 3,
        compiler_params=compiler_params,
    )(parts)
    low, high = y_shift(to_right, 1), y_shift(to_left, -1)
    return pl.pallas_call(
        functools.partial(finish_kernel, members),
        out_shape=jax.ShapeDtypeStruct((own_rows, cols), jnp.float32),
        in_specs=[vmem] * 3 + [smem] * 3,
        out_specs=vmem,
        compiler_params=compiler_params,
    )(here, low, high, cutoff, factor_index, factor_table)


def solution(mesh):
    in_specs = (P("mem", "ocn"), P("mem", "ocn"), P("mem", "ocn"), P("mem", "ocn"), P())
    out_specs = P("mem", "ocn")
    return jax.shard_map(
        per_device, mesh=mesh, in_specs=in_specs, out_specs=out_specs, check_vma=False
    )
```

time: 142 us -> 132 us (0.930)
  Pallas kernels: 10.2 us -> 5.44 us
  starting transfers between devices: 87.2 us -> 83.5 us
    all_to_all x1 -> x0, waiting for transfers between devices: 13.1 us -> none  [z_spread(): lax.all_to_all(copies, 'ocn', split_axis=0, concat_axis=0, axis_index_gro...]
    all_to_all x1 -> x0, starting transfers between devices: 10.4 us -> none  [z_spread(): lax.all_to_all(copies, 'ocn', split_axis=0, concat_axis=0, axis_index_gro...]
    ppermute x14, waiting for transfers between devices: 0.04 us -> 7.34 us  [z_shift(): return lax.ppermute(x, 'ocn', perm)]
    ppermute x14, starting transfers between devices: 49.4 us -> 55.2 us  [z_shift(): return lax.ppermute(x, 'ocn', perm)]
    pallas_call x4, Pallas kernels: 10.2 us -> 5.44 us  [the longest x2 3.98 us: cross(): pl.pallas_call(functools.partial(cross_kernel, groups, before is None), o...]
    ppermute x6 -> x7, waiting for transfers between devices: 2.56 us -> 5.78 us  [y_shift(): return lax.ppermute(x, 'ocn', perm)]
    ppermute x0 -> x1, waiting for transfers between devices: none -> 2.81 us  [per_device(): lax.ppermute(parts[1], 'mem', [(m, m ^ 1) for m in range(n_mem)])]
    dynamic_slice x0 -> x2, local copies, waits for them, and re-layouts: none -> 2.67 us  [the longest x1 1.68 us: per_device(): near = lax.dynamic_slice_in_dim(ocean, parity * half, half, 0)]
  transfers between devices with their start and end apart: 21 -> 22, of which waited for: 2 -> 5; matrix products, arithmetic and copies ran while one was open for 2% -> 1% of each run, Pallas kernels for 4% -> 2%
where the time goes in v4:
time: 132 us; the launch traced here: 130 us
  starting transfers between devices  83.5 us (63%)
  blocking collectives  21.9 us (17%)
  waiting for transfers between devices  15.9 us (12%)
  Pallas kernels  5.44 us (4%)
  local copies, waits for them, and re-layouts  2.86 us (2%)
    ppermute x14, starting transfers between devices, z_shift(): return lax.ppermute(x, 'ocn', perm)  55.2 us
    ppermute x7, starting transfers between devices, y_shift(): return lax.ppermute(x, 'ocn', perm)  26.3 us
    all_to_all x1, blocking collectives, per_device(): lax.all_to_all(parts, 'mem', split_axis=0, concat_axis=0, axis_index_grou...  21.9 us
    ppermute x14, waiting for transfers between devices, z_shift(): return lax.ppermute(x, 'ocn', perm)  7.34 us
    ppermute x7, waiting for transfers between devices, y_shift(): return lax.ppermute(x, 'ocn', perm)  5.78 us
    pallas_call x2, Pallas kernels, cross(): pl.pallas_call(functools.partial(cross_kernel, groups, before is None), o...  3.98 us
    ppermute x1, waiting for transfers between devices, per_device(): lax.ppermute(parts[1], 'mem', [(m, m ^ 1) for m in range(n_mem)])  2.81 us
  transfers between devices with their start and end apart: 22, of which 5 were waited for; matrix products, arithmetic and copies ran while one was open for 1% of the time, Pallas kernels for 2%

profile of v4, /device:TPU:56, one launch (start us, length us, event | category | flops | bytes accessed | tf_op | source)
XLA Modules:
  0.0 130.4 jit_solution(17894710662644963159)
XLA Ops:
  0.0 1.0 dynamic-slice_bitcast_fusion.1
  1.0 4.0 %collective-permute-start.9 = (bf16[32,2048]{1,0:T(8,128)(2,1)S(1)}, bf16[32,2048]{1,0:T(8,128)(2,1)S(1)}, u32[]{:S(2)}, u32[]{:S(2)}) collective-permute-start(bf16[32,2048]{1,0:T(8,128)(2,1)S(1)} %get-tuple-element.22), channel_id=1, source_target_pairs={{0,24},{1,25},{2,26},{3,27},{4,28},{5,29},{6,30},{7,31},{8,0},{9,1... | collective-permute-start | bytes 393224 | tf_op jit(solution)/shard_map/ppermute | solution.py:24
  5.0 3.9 %collective-permute-start = (bf16[32,2048]{1,0:T(8,128)(2,1)S(1)}, bf16[32,2048]{1,0:T(8,128)(2,1)S(1)}, u32[]{:S(2)}, u32[]{:S(2)}) collective-permute-start(bf16[32,2048]{1,0:T(8,128)(2,1)S(1)} %get-tuple-element.22), channel_id=1, source_target_pairs={{0,8},{1,9},{2,10},{3,11},{4,12},{5,13},{6,14},{7,15},{8,16},{9,17... | collective-permute-start | bytes 393224 | tf_op jit(solution)/shard_map/ppermute | solution.py:24
  9.0 4.7 %collective-permute-start.10 = (bf16[32,2048]{1,0:T(8,128)(2,1)S(1)}, bf16[32,2048]{1,0:T(8,128)(2,1)S(1)}, u32[]{:S(2)}, u32[]{:S(2)}) collective-permute-start(bf16[32,2048]{1,0:T(8,128)(2,1)S(1)} %get-tuple-element.21), channel_id=1, source_target_pairs={{0,16},{1,17},{2,18},{3,19},{4,20},{5,21},{6,22},{7,23},{8,24},{9,... | collective-permute-start | bytes 393224 | tf_op jit(solution)/shard_map/ppermute | solution.py:24
  13.7 1.7 %constant_dynamic-slice_fusion = (bf16[2048,256]{1,0:T(8,128)(2,1)S(1)}, bf16[2048,256]{1,0:T(8,128)(2,1)S(1)}) fusion(bf16[4096,256]{1,0:T(8,128)(2,1)} %param.6, s32[]{:T(128)S(6)} %select_n.14, s32[]{:T(128)S(6)} %select_n.15), kind=kLoop, calls=%fused_computation.9 | loop fusion | bytes 4194312 | tf_op jit(solution)/shard_map/dynamic_slice | solution.py:154
  15.4 12.1 %collective-permute-start.6 = (bf16[64,2048]{1,0:T(8,128)(2,1)S(1)}, bf16[64,2048]{1,0:T(8,128)(2,1)S(1)}, u32[]{:S(2)}, u32[]{:S(2)}) collective-permute-start(bf16[64,2048]{1,0:T(8,128)(2,1)S(1)} %pad_maximum_fusion.1.refs_0_), channel_id=1, source_target_pairs={{0,7},{1,0},{2,1},{3,2},{4,3},{5,4},{6,5},{7,6},{8,15},{9,8},{10,9... | collective-permute-start | bytes 786440 | tf_op jit(solution)/shard_map/ppermute | solution.py:19
  27.5 1.9 %collective-permute-start.1 = (bf16[64,2048]{1,0:T(8,128)(2,1)S(1)}, bf16[64,2048]{1,0:T(8,128)(2,1)S(1)}, u32[]{:S(2)}, u32[]{:S(2)}) collective-permute-start(bf16[64,2048]{1,0:T(8,128)(2,1)S(1)} %pad_maximum_fusion.1.refs_0_), channel_id=1, source_target_pairs={{0,1},{1,2},{2,3},{3,4},{4,5},{5,6},{6,7},{7,0},{8,9},{9,10},{10,1... | collective-permute-start | bytes 786440 | tf_op jit(solution)/shard_map/ppermute | solution.py:19
  29.5 5.0 %collective-permute-start.3 = (bf16[2048,128]{1,0:T(8,128)(2,1)S(1)}, bf16[2048,128]{1,0:T(8,128)(2,1)S(1)}, u32[]{:S(2)}, u32[]{:S(2)}) collective-permute-start(bf16[2048,128]{1,0:T(8,128)(2,1)S(1)} %get-tuple-element.19), channel_id=1, source_target_pairs={{0,8},{1,9},{2,10},{3,11},{4,12},{5,13},{6,14},{7,15},{8,16},{9,17... | collective-permute-start | bytes 1572872 | tf_op jit(solution)/shard_map/ppermute | solution.py:24
  34.5 1.9 %collective-permute-start.4 = (bf16[2048,128]{1,0:T(8,128)(2,1)S(1)}, bf16[2048,128]{1,0:T(8,128)(2,1)S(1)}, u32[]{:S(2)}, u32[]{:S(2)}) collective-permute-start(bf16[2048,128]{1,0:T(8,128)(2,1)S(1)} %get-tuple-element.20), channel_id=1, source_target_pairs={{0,24},{1,25},{2,26},{3,27},{4,28},{5,29},{6,30},{7,31},{8,0},{9,1... | collective-permute-start | bytes 1572872 | tf_op jit(solution)/shard_map/ppermute | solution.py:24
  36.5 5.1 %collective-permute-start.14 = (bf16[64,2048]{1,0:T(8,128)(2,1)S(1)}, bf16[64,2048]{1,0:T(8,128)(2,1)S(1)}, u32[]{:S(2)}, u32[]{:S(2)}) collective-permute-start(bf16[64,2048]{1,0:T(8,128)(2,1)S(1)} %constant_dynamic-update-slice_fusion.refs_1_), channel_id=1, source_target_pairs={{0,7},{1,0},{2,1},{3,2},{4,3},{5,4},{6,5},{7,6},{8,15},{9,8},{10,9... | collective-permute-start | bytes 786440 | tf_op jit(solution)/shard_map/ppermute | solution.py:19
  41.6 1.9 %collective-permute-start.11 = (bf16[64,2048]{1,0:T(8,128)(2,1)S(1)}, bf16[64,2048]{1,0:T(8,128)(2,1)S(1)}, u32[]{:S(2)}, u32[]{:S(2)}) collective-permute-start(bf16[64,2048]{1,0:T(8,128)(2,1)S(1)} %constant_dynamic-update-slice_fusion.refs_1_), channel_id=1, source_target_pairs={{0,1},{1,2},{2,3},{3,4},{4,5},{5,6},{6,7},{7,0},{8,9},{9,10},{10,1... | collective-permute-start | bytes 786440 | tf_op jit(solution)/shard_map/ppermute | solution.py:19
  43.6 1.9 %collective-permute-start.2 = (bf16[64,2048]{1,0:T(8,128)(2,1)S(1)}, bf16[64,2048]{1,0:T(8,128)(2,1)S(1)}, u32[]{:S(2)}, u32[]{:S(2)}) collective-permute-start(bf16[64,2048]{1,0:T(8,128)(2,1)S(1)} %collective-permute-done.1.refs_2_), channel_id=1, source_target_pairs={{0,1},{1,2},{2,3},{3,4},{4,5},{5,6},{6,7},{7,0},{8,9},{9,10},{10,1... | collective-permute-start | bytes 786440 | tf_op jit(solution)/shard_map/ppermute | solution.py:19
  45.5 5.6 %collective-permute-start.15 = (bf16[64,2048]{1,0:T(8,128)(2,1)S(1)}, bf16[64,2048]{1,0:T(8,128)(2,1)S(1)}, u32[]{:S(2)}, u32[]{:S(2)}) collective-permute-start(bf16[64,2048]{1,0:T(8,128)(2,1)S(1)} %collective-permute-done.14.refs_5_), channel_id=1, source_target_pairs={{0,7},{1,0},{2,1},{3,2},{4,3},{5,4},{6,5},{7,6},{8,15},{9,8},{10,9... | collective-permute-start | bytes 786440 | tf_op jit(solution)/shard_map/ppermute | solution.py:19
  51.1 2.1 %collective-permute-done.11.refs_4_ = bf16[64,2048]{1,0:T(8,128)(2,1)S(1)} collective-permute-done((bf16[64,2048]{1,0:T(8,128)(2,1)S(1)}, bf16[64,2048]{1,0:T(8,128)(2,1)S(1)}, u32[]{:S(2)}, u32[]{:S(2)}) %collective-permute-start.11) | collective-permute-done | bytes 262176 | tf_op jit(solution)/shard_map/ppermute | solution.py:19
  53.2 1.9 %collective-permute-start.7 = (bf16[64,2048]{1,0:T(8,128)(2,1)S(1)}, bf16[64,2048]{1,0:T(8,128)(2,1)S(1)}, u32[]{:S(2)}, u32[]{:S(2)}) collective-permute-start(bf16[64,2048]{1,0:T(8,128)(2,1)S(1)} %collective-permute-done.6.refs_3_), channel_id=1, source_target_pairs={{0,7},{1,0},{2,1},{3,2},{4,3},{5,4},{6,5},{7,6},{8,15},{9,8},{10,9... | collective-permute-start | bytes 786440 | tf_op jit(solution)/shard_map/ppermute | solution.py:19
  55.1 3.9 %collective-permute-start.12 = (bf16[64,2048]{1,0:T(8,128)(2,1)S(1)}, bf16[64,2048]{1,0:T(8,128)(2,1)S(1)}, u32[]{:S(2)}, u32[]{:S(2)}) collective-permute-start(bf16[64,2048]{1,0:T(8,128)(2,1)S(1)} %collective-permute-done.11.refs_4_), channel_id=1, source_target_pairs={{0,1},{1,2},{2,3},{3,4},{4,5},{5,6},{6,7},{7,0},{8,9},{9,10},{10,1... | collective-permute-start | bytes 786440 | tf_op jit(solution)/shard_map/ppermute | solution.py:19
  59.6 4.9 %collective-permute-start.16 = (bf16[64,2048]{1,0:T(8,128)(2,1)S(1)}, bf16[64,2048]{1,0:T(8,128)(2,1)S(1)}, u32[]{:S(2)}, u32[]{:S(2)}) collective-permute-start(bf16[64,2048]{1,0:T(8,128)(2,1)S(1)} %collective-permute-done.15.refs_9_), channel_id=1, source_target_pairs={{0,7},{1,0},{2,1},{3,2},{4,3},{5,4},{6,5},{7,6},{8,15},{9,8},{10,9... | collective-permute-start | bytes 786440 | tf_op jit(solution)/shard_map/ppermute | solution.py:19
  64.5 1.9 %collective-permute-start.5 = (bf16[64,2048]{1,0:T(8,128)(2,1)S(1)}, bf16[64,2048]{1,0:T(8,128)(2,1)S(1)}, u32[]{:S(2)}, u32[]{:S(2)}) collective-permute-start(bf16[64,2048]{1,0:T(8,128)(2,1)S(1)} %collective-permute-done.2.refs_6_), channel_id=1, source_target_pairs={{0,1},{1,2},{2,3},{3,4},{4,5},{5,6},{6,7},{7,0},{8,9},{9,10},{10,1... | collective-permute-start | bytes 786440 | tf_op jit(solution)/shard_map/ppermute | solution.py:19
  66.4 5.1 %collective-permute-start.8 = (bf16[64,2048]{1,0:T(8,128)(2,1)S(1)}, bf16[64,2048]{1,0:T(8,128)(2,1)S(1)}, u32[]{:S(2)}, u32[]{:S(2)}) collective-permute-start(bf16[64,2048]{1,0:T(8,128)(2,1)S(1)} %collective-permute-done.7.refs_7_), channel_id=1, source_target_pairs={{0,7},{1,0},{2,1},{3,2},{4,3},{5,4},{6,5},{7,6},{8,15},{9,8},{10,9... | collective-permute-start | bytes 786440 | tf_op jit(solution)/shard_map/ppermute | solution.py:19
  71.6 1.9 %collective-permute-start.13 = (bf16[64,2048]{1,0:T(8,128)(2,1)S(1)}, bf16[64,2048]{1,0:T(8,128)(2,1)S(1)}, u32[]{:S(2)}, u32[]{:S(2)}) collective-permute-start(bf16[64,2048]{1,0:T(8,128)(2,1)S(1)} %collective-permute-done.12.refs_8_), channel_id=1, source_target_pairs={{0,1},{1,2},{2,3},{3,4},{4,5},{5,6},{6,7},{7,0},{8,9},{9,10},{10,1... | collective-permute-start | bytes 786440 | tf_op jit(solution)/shard_map/ppermute | solution.py:19
  73.5 5.1 %collective-permute-start.18 = (bf16[64,2048]{1,0:T(8,128)(2,1)S(1)}, bf16[64,2048]{1,0:T(8,128)(2,1)S(1)}, u32[]{:S(2)}, u32[]{:S(2)}) collective-permute-start(bf16[64,2048]{1,0:T(8,128)(2,1)S(1)} %collective-permute-done.16.refs_3_), channel_id=1, source_target_pairs={{0,7},{1,0},{2,1},{3,2},{4,3},{5,4},{6,5},{7,6},{8,15},{9,8},{10,9... | collective-permute-start | bytes 786440 | tf_op jit(solution)/shard_map/ppermute | solution.py:19
  78.7 1.9 %collective-permute-start.17 = (bf16[64,2048]{1,0:T(8,128)(2,1)S(1)}, bf16[64,2048]{1,0:T(8,128)(2,1)S(1)}, u32[]{:S(2)}, u32[]{:S(2)}) collective-permute-start(bf16[64,2048]{1,0:T(8,128)(2,1)S(1)} %collective-permute-done.5.refs_0_), channel_id=1, source_target_pairs={{0,1},{1,2},{2,3},{3,4},{4,5},{5,6},{6,7},{7,0},{8,9},{9,10},{10,1... | collective-permute-start | bytes 786440 | tf_op jit(solution)/shard_map/ppermute | solution.py:19
  80.6 2.5 %shard_map.55.refs_8_ = f32[2,8,72,512]{3,2,1,0:T(8,128)S(1)} custom-call(bf16[64,2048]{1,0:T(8,128)(2,1)S(1)} %pad_maximum_fusion.1.refs_0_, bf16[64,2048]{1,0:T(8,128)(2,1)S(1)} %constant_dynamic-update-slice_fusion.refs_1_, bf16[64,2048]{1,0:T(8,128)(2,1)S(1)} %collective-permute-done.1.refs_2_, bf16[64,2048]{1,0:T(8,128)(2,1)S(1)} %collective-permute-done.6.refs_3_, ...), custom_call_target="tpu_custom_call" | custom-call | flops 1342177280 | bytes 4718592 | tf_op jit(solution)/shard_map/pallas_call | solution.py:96
  83.1 5.2 %collective-permute-done.17.refs_4_ = bf16[64,2048]{1,0:T(8,128)(2,1)S(1)} collective-permute-done((bf16[64,2048]{1,0:T(8,128)(2,1)S(1)}, bf16[64,2048]{1,0:T(8,128)(2,1)S(1)}, u32[]{:S(2)}, u32[]{:S(2)}) %collective-permute-start.17) | collective-permute-done | bytes 262176 | tf_op jit(solution)/shard_map/ppermute | solution.py:19
  88.3 1.5 %shard_map.56 = f32[2,8,72,512]{3,2,1,0:T(8,128)S(1)} custom-call(bf16[64,2048]{1,0:T(8,128)(2,1)S(1)} %collective-permute-done.5.refs_0_, bf16[64,2048]{1,0:T(8,128)(2,1)S(1)} %collective-permute-done.8.refs_1_, bf16[64,2048]{1,0:T(8,128)(2,1)S(1)} %collective-permute-done.13.refs_2_, ...), custom_call_target="tpu_custom_call", output_to_operand_aliasing={{}: (8, {})} | custom-call | flops 805306368 | bytes 3670016 | tf_op jit(solution)/shard_map/pallas_call | solution.py:96
  89.9 1.9 %collective-permute-start.19 = (f32[8,72,512]{2,1,0:T(8,128)S(1)}, f32[8,72,512]{2,1,0:T(8,128)S(1)}, u32[]{:S(2)}, u32[]{:S(2)}) collective-permute-start(f32[8,72,512]{2,1,0:T(8,128)S(1)} %slice_bitcast_fusion), channel_id=1, source_target_pairs={{0,32},{32,0},{64,96},{96,64},{128,160},{160,128},{192,224},{224,1... | collective-permute-start | bytes 3538952 | tf_op jit(solution)/shard_map/ppermute | solution.py:183
  91.8 2.8 %collective-permute-done.19 = f32[8,72,512]{2,1,0:T(8,128)S(1)} collective-permute-done((f32[8,72,512]{2,1,0:T(8,128)S(1)}, f32[8,72,512]{2,1,0:T(8,128)S(1)}, u32[]{:S(2)}, u32[]{:S(2)}) %collective-permute-start.19) | collective-permute-done | bytes 1179680 | tf_op jit(solution)/shard_map/ppermute | solution.py:183
  94.9 21.9 %all_to_all.5.parts_ref = f32[8,72,512]{2,1,0:T(8,128)S(1)} all-to-all(f32[8,72,512]{2,1,0:T(8,128)S(1)} %fusion), channel_id=1, replica_groups={{0,64,128,192,256,320,384,448},{32,96,160,224,288,352,416,480},{1,65,12..., dimensions={0} | all-to-all | bytes 2359296 | tf_op jit(solution)/shard_map/all_to_all | solution.py:185
  116.9 3.9 %collective-permute-start.20 = (f32[72,128]{1,0:T(8,128)S(1)}, f32[72,128]{1,0:T(8,128)S(1)}, u32[]{:S(2)}, u32[]{:S(2)}) collective-permute-start(f32[72,128]{1,0:T(8,128)S(1)} %get-tuple-element.15), channel_id=1, source_target_pairs={{0,8},{1,9},{2,10},{3,11},{4,12},{5,13},{6,14},{7,15},{8,16},{9,17... | collective-permute-start | bytes 110600 | tf_op jit(solution)/shard_map/ppermute | solution.py:24
  120.8 2.9 %collective-permute-start.21 = (f32[72,128]{1,0:T(8,128)S(1)}, f32[72,128]{1,0:T(8,128)S(1)}, u32[]{:S(2)}, u32[]{:S(2)}) collective-permute-start(f32[72,128]{1,0:T(8,128)S(1)} %get-tuple-element.16), channel_id=1, source_target_pairs={{0,24},{1,25},{2,26},{3,27},{4,28},{5,29},{6,30},{7,31},{8,0},{9,1... | collective-permute-start | bytes 110600 | tf_op jit(solution)/shard_map/ppermute | solution.py:24
  123.7 5.3 %collective-permute-done.21.high_ref = f32[72,128]{1,0:T(8,128)S(1)} collective-permute-done((f32[72,128]{1,0:T(8,128)S(1)}, f32[72,128]{1,0:T(8,128)S(1)}, u32[]{:S(2)}, u32[]{:S(2)}) %collective-permute-start.21) | collective-permute-done | bytes 36896 | tf_op jit(solution)/shard_map/ppermute | solution.py:24
  129.0 1.4 %shard_map.58 = f32[64,256]{1,0:T(8,128)} custom-call(f32[72,256]{1,0:T(8,128)S(1)} %get-tuple-element.14.near_ref, f32[72,128]{1,0:T(8,128)S(1)} %collective-permute-done.20.low_ref, f32[72,128]{1,0:T(8,128)S(1)} %collective-permute-done.21.high_ref, s32[1,2]{1,0:T(1,128)S(1)} %copy-done, s32[1,2]{1,0:T(1,128)S(1)} %copy-done.1, f32[8]{0:T(128)S(1)} %copy-done.2), custom_call_target="tpu_custom_call" | custom-call | tf_op jit(solution)/shard_map/pallas_call | solution.py:196
  (32 shorter events, 1.1 us)
Async XLA Ops:
  1.0 33.5 %collective-permute-start.9 = (bf16[32,2048]{1,0:T(8,128)(2,1)S(1)}, bf16[32,2048]{1,0:T(8,128)(2,1)S(1)}, u32[]{:S(2)}, u32[]{:S(2)}) collective-permute-start(bf16[32,2048]{1,0:T(8,128)(2,1)S(1)} %get-tuple-element.22), channel_id=1, source_target_pairs={{0,24},{1,25},{2,26},{3,27},{4,28},{5,29},{6,30},{7,31},{8,0},{9,1... | collective-permute-start | bytes 393224 | tf_op jit(solution)/shard_map/ppermute | solution.py:24
  5.0 10.3 %collective-permute-start = (bf16[32,2048]{1,0:T(8,128)(2,1)S(1)}, bf16[32,2048]{1,0:T(8,128)(2,1)S(1)}, u32[]{:S(2)}, u32[]{:S(2)}) collective-permute-start(bf16[32,2048]{1,0:T(8,128)(2,1)S(1)} %get-tuple-element.22), channel_id=1, source_target_pairs={{0,8},{1,9},{2,10},{3,11},{4,12},{5,13},{6,14},{7,15},{8,16},{9,17... | collective-permute-start | bytes 393224 | tf_op jit(solution)/shard_map/ppermute | solution.py:24
  9.0 27.5 %collective-permute-start.10 = (bf16[32,2048]{1,0:T(8,128)(2,1)S(1)}, bf16[32,2048]{1,0:T(8,128)(2,1)S(1)}, u32[]{:S(2)}, u32[]{:S(2)}) collective-permute-start(bf16[32,2048]{1,0:T(8,128)(2,1)S(1)} %get-tuple-element.21), channel_id=1, source_target_pairs={{0,16},{1,17},{2,18},{3,19},{4,20},{5,21},{6,22},{7,23},{8,24},{9,... | collective-permute-start | bytes 393224 | tf_op jit(solution)/shard_map/ppermute | solution.py:24
  15.4 26.2 %collective-permute-start.6 = (bf16[64,2048]{1,0:T(8,128)(2,1)S(1)}, bf16[64,2048]{1,0:T(8,128)(2,1)S(1)}, u32[]{:S(2)}, u32[]{:S(2)}) collective-permute-start(bf16[64,2048]{1,0:T(8,128)(2,1)S(1)} %pad_maximum_fusion.1.refs_0_), channel_id=1, source_target_pairs={{0,7},{1,0},{2,1},{3,2},{4,3},{5,4},{6,5},{7,6},{8,15},{9,8},{10,9... | collective-permute-start | bytes 786440 | tf_op jit(solution)/shard_map/ppermute | solution.py:19
  27.5 16.1 %collective-permute-start.1 = (bf16[64,2048]{1,0:T(8,128)(2,1)S(1)}, bf16[64,2048]{1,0:T(8,128)(2,1)S(1)}, u32[]{:S(2)}, u32[]{:S(2)}) collective-permute-start(bf16[64,2048]{1,0:T(8,128)(2,1)S(1)} %pad_maximum_fusion.1.refs_0_), channel_id=1, source_target_pairs={{0,1},{1,2},{2,3},{3,4},{4,5},{5,6},{6,7},{7,0},{8,9},{9,10},{10,1... | collective-permute-start | bytes 786440 | tf_op jit(solution)/shard_map/ppermute | solution.py:19
  29.5 25.6 %collective-permute-start.3 = (bf16[2048,128]{1,0:T(8,128)(2,1)S(1)}, bf16[2048,128]{1,0:T(8,128)(2,1)S(1)}, u32[]{:S(2)}, u32[]{:S(2)}) collective-permute-start(bf16[2048,128]{1,0:T(8,128)(2,1)S(1)} %get-tuple-element.19), channel_id=1, source_target_pairs={{0,8},{1,9},{2,10},{3,11},{4,12},{5,13},{6,14},{7,15},{8,16},{9,17... | collective-permute-start | bytes 1572872 | tf_op jit(solution)/shard_map/ppermute | solution.py:24
  34.5 25.0 %collective-permute-start.4 = (bf16[2048,128]{1,0:T(8,128)(2,1)S(1)}, bf16[2048,128]{1,0:T(8,128)(2,1)S(1)}, u32[]{:S(2)}, u32[]{:S(2)}) collective-permute-start(bf16[2048,128]{1,0:T(8,128)(2,1)S(1)} %get-tuple-element.20), channel_id=1, source_target_pairs={{0,24},{1,25},{2,26},{3,27},{4,28},{5,29},{6,30},{7,31},{8,0},{9,1... | collective-permute-start | bytes 1572872 | tf_op jit(solution)/shard_map/ppermute | solution.py:24
  36.5 9.0 %collective-permute-start.14 = (bf16[64,2048]{1,0:T(8,128)(2,1)S(1)}, bf16[64,2048]{1,0:T(8,128)(2,1)S(1)}, u32[]{:S(2)}, u32[]{:S(2)}) collective-permute-start(bf16[64,2048]{1,0:T(8,128)(2,1)S(1)} %constant_dynamic-update-slice_fusion.refs_1_), channel_id=1, source_target_pairs={{0,7},{1,0},{2,1},{3,2},{4,3},{5,4},{6,5},{7,6},{8,15},{9,8},{10,9... | collective-permute-start | bytes 786440 | tf_op jit(solution)/shard_map/ppermute | solution.py:19
  41.6 11.6 %collective-permute-start.11 = (bf16[64,2048]{1,0:T(8,128)(2,1)S(1)}, bf16[64,2048]{1,0:T(8,128)(2,1)S(1)}, u32[]{:S(2)}, u32[]{:S(2)}) collective-permute-start(bf16[64,2048]{1,0:T(8,128)(2,1)S(1)} %constant_dynamic-update-slice_fusion.refs_1_), channel_id=1, source_target_pairs={{0,1},{1,2},{2,3},{3,4},{4,5},{5,6},{6,7},{7,0},{8,9},{9,10},{10,1... | collective-permute-start | bytes 786440 | tf_op jit(solution)/shard_map/ppermute | solution.py:19
  43.6 16.1 %collective-permute-start.2 = (bf16[64,2048]{1,0:T(8,128)(2,1)S(1)}, bf16[64,2048]{1,0:T(8,128)(2,1)S(1)}, u32[]{:S(2)}, u32[]{:S(2)}) collective-permute-start(bf16[64,2048]{1,0:T(8,128)(2,1)S(1)} %collective-permute-done.1.refs_2_), channel_id=1, source_target_pairs={{0,1},{1,2},{2,3},{3,4},{4,5},{5,6},{6,7},{7,0},{8,9},{9,10},{10,1... | collective-permute-start | bytes 786440 | tf_op jit(solution)/shard_map/ppermute | solution.py:19
  45.5 14.1 %collective-permute-start.15 = (bf16[64,2048]{1,0:T(8,128)(2,1)S(1)}, bf16[64,2048]{1,0:T(8,128)(2,1)S(1)}, u32[]{:S(2)}, u32[]{:S(2)}) collective-permute-start(bf16[64,2048]{1,0:T(8,128)(2,1)S(1)} %collective-permute-done.14.refs_5_), channel_id=1, source_target_pairs={{0,7},{1,0},{2,1},{3,2},{4,3},{5,4},{6,5},{7,6},{8,15},{9,8},{10,9... | collective-permute-start | bytes 786440 | tf_op jit(solution)/shard_map/ppermute | solution.py:19
  53.2 13.2 %collective-permute-start.7 = (bf16[64,2048]{1,0:T(8,128)(2,1)S(1)}, bf16[64,2048]{1,0:T(8,128)(2,1)S(1)}, u32[]{:S(2)}, u32[]{:S(2)}) collective-permute-start(bf16[64,2048]{1,0:T(8,128)(2,1)S(1)} %collective-permute-done.6.refs_3_), channel_id=1, source_target_pairs={{0,7},{1,0},{2,1},{3,2},{4,3},{5,4},{6,5},{7,6},{8,15},{9,8},{10,9... | collective-permute-start | bytes 786440 | tf_op jit(solution)/shard_map/ppermute | solution.py:19
  55.1 16.4 %collective-permute-start.12 = (bf16[64,2048]{1,0:T(8,128)(2,1)S(1)}, bf16[64,2048]{1,0:T(8,128)(2,1)S(1)}, u32[]{:S(2)}, u32[]{:S(2)}) collective-permute-start(bf16[64,2048]{1,0:T(8,128)(2,1)S(1)} %collective-permute-done.11.refs_4_), channel_id=1, source_target_pairs={{0,1},{1,2},{2,3},{3,4},{4,5},{5,6},{6,7},{7,0},{8,9},{9,10},{10,1... | collective-permute-start | bytes 786440 | tf_op jit(solution)/shard_map/ppermute | solution.py:19
  59.6 13.9 %collective-permute-start.16 = (bf16[64,2048]{1,0:T(8,128)(2,1)S(1)}, bf16[64,2048]{1,0:T(8,128)(2,1)S(1)}, u32[]{:S(2)}, u32[]{:S(2)}) collective-permute-start(bf16[64,2048]{1,0:T(8,128)(2,1)S(1)} %collective-permute-done.15.refs_9_), channel_id=1, source_target_pairs={{0,7},{1,0},{2,1},{3,2},{4,3},{5,4},{6,5},{7,6},{8,15},{9,8},{10,9... | collective-permute-start | bytes 786440 | tf_op jit(solution)/shard_map/ppermute | solution.py:19
  64.5 14.2 %collective-permute-start.5 = (bf16[64,2048]{1,0:T(8,128)(2,1)S(1)}, bf16[64,2048]{1,0:T(8,128)(2,1)S(1)}, u32[]{:S(2)}, u32[]{:S(2)}) collective-permute-start(bf16[64,2048]{1,0:T(8,128)(2,1)S(1)} %collective-permute-done.2.refs_6_), channel_id=1, source_target_pairs={{0,1},{1,2},{2,3},{3,4},{4,5},{5,6},{6,7},{7,0},{8,9},{9,10},{10,1... | collective-permute-start | bytes 786440 | tf_op jit(solution)/shard_map/ppermute | solution.py:19
  66.4 16.6 %collective-permute-start.8 = (bf16[64,2048]{1,0:T(8,128)(2,1)S(1)}, bf16[64,2048]{1,0:T(8,128)(2,1)S(1)}, u32[]{:S(2)}, u32[]{:S(2)}) collective-permute-start(bf16[64,2048]{1,0:T(8,128)(2,1)S(1)} %collective-permute-done.7.refs_7_), channel_id=1, source_target_pairs={{0,7},{1,0},{2,1},{3,2},{4,3},{5,4},{6,5},{7,6},{8,15},{9,8},{10,9... | collective-permute-start | bytes 786440 | tf_op jit(solution)/shard_map/ppermute | solution.py:19
  71.6 11.5 %collective-permute-start.13 = (bf16[64,2048]{1,0:T(8,128)(2,1)S(1)}, bf16[64,2048]{1,0:T(8,128)(2,1)S(1)}, u32[]{:S(2)}, u32[]{:S(2)}) collective-permute-start(bf16[64,2048]{1,0:T(8,128)(2,1)S(1)} %collective-permute-done.12.refs_8_), channel_id=1, source_target_pairs={{0,1},{1,2},{2,3},{3,4},{4,5},{5,6},{6,7},{7,0},{8,9},{9,10},{10,1... | collective-permute-start | bytes 786440 | tf_op jit(solution)/shard_map/ppermute | solution.py:19
  73.5 9.6 %collective-permute-start.18 = (bf16[64,2048]{1,0:T(8,128)(2,1)S(1)}, bf16[64,2048]{1,0:T(8,128)(2,1)S(1)}, u32[]{:S(2)}, u32[]{:S(2)}) collective-permute-start(bf16[64,2048]{1,0:T(8,128)(2,1)S(1)} %collective-permute-done.16.refs_3_), channel_id=1, source_target_pairs={{0,7},{1,0},{2,1},{3,2},{4,3},{5,4},{6,5},{7,6},{8,15},{9,8},{10,9... | collective-permute-start | bytes 786440 | tf_op jit(solution)/shard_map/ppermute | solution.py:19
  78.7 9.6 %collective-permute-start.17 = (bf16[64,2048]{1,0:T(8,128)(2,1)S(1)}, bf16[64,2048]{1,0:T(8,128)(2,1)S(1)}, u32[]{:S(2)}, u32[]{:S(2)}) collective-permute-start(bf16[64,2048]{1,0:T(8,128)(2,1)S(1)} %collective-permute-done.5.refs_0_), channel_id=1, source_target_pairs={{0,1},{1,2},{2,3},{3,4},{4,5},{5,6},{6,7},{7,0},{8,9},{9,10},{10,1... | collective-permute-start | bytes 786440 | tf_op jit(solution)/shard_map/ppermute | solution.py:19
  89.9 4.7 %collective-permute-start.19 = (f32[8,72,512]{2,1,0:T(8,128)S(1)}, f32[8,72,512]{2,1,0:T(8,128)S(1)}, u32[]{:S(2)}, u32[]{:S(2)}) collective-permute-start(f32[8,72,512]{2,1,0:T(8,128)S(1)} %slice_bitcast_fusion), channel_id=1, source_target_pairs={{0,32},{32,0},{64,96},{96,64},{128,160},{160,128},{192,224},{224,1... | collective-permute-start | bytes 3538952 | tf_op jit(solution)/shard_map/ppermute | solution.py:183
  94.9 34.2 %copy-start = (s32[1,2]{1,0:T(1,128)S(1)}, s32[1,2]{1,0:T(1,128)}, u32[]{:S(2)}) copy-start(s32[1,2]{1,0:T(1,128)} %cutoff_ref.1) | copy-start | bytes 28
  94.9 34.1 %copy-start.1 = (s32[1,2]{1,0:T(1,128)S(1)}, s32[1,2]{1,0:T(1,128)}, u32[]{:S(2)}) copy-start(s32[1,2]{1,0:T(1,128)} %index_ref.1) | copy-start | bytes 28
  94.9 34.1 %copy-start.2 = (f32[8]{0:T(128)S(1)}, f32[8]{0:T(128)}, u32[]{:S(2)}) copy-start(f32[8]{0:T(128)} %table_ref.1) | copy-start | bytes 100
  116.9 6.8 %collective-permute-start.20 = (f32[72,128]{1,0:T(8,128)S(1)}, f32[72,128]{1,0:T(8,128)S(1)}, u32[]{:S(2)}, u32[]{:S(2)}) collective-permute-start(f32[72,128]{1,0:T(8,128)S(1)} %get-tuple-element.15), channel_id=1, source_target_pairs={{0,8},{1,9},{2,10},{3,11},{4,12},{5,13},{6,14},{7,15},{8,16},{9,17... | collective-permute-start | bytes 110600 | tf_op jit(solution)/shard_map/ppermute | solution.py:24
  120.8 8.2 %collective-permute-start.21 = (f32[72,128]{1,0:T(8,128)S(1)}, f32[72,128]{1,0:T(8,128)S(1)}, u32[]{:S(2)}, u32[]{:S(2)}) collective-permute-start(f32[72,128]{1,0:T(8,128)S(1)} %get-tuple-element.16), channel_id=1, source_target_pairs={{0,24},{1,25},{2,26},{3,27},{4,28},{5,29},{6,30},{7,31},{8,0},{9,1... | collective-permute-start | bytes 110600 | tf_op jit(solution)/shard_map/ppermute | solution.py:24

commit v5 on v4

--- a/solution.py
+++ b/solution.py
@@ -170,8 +170,8 @@
     for s in (1, 2, 3):
         up_1, down_1 = z_shift(up_1, 1), z_shift(down_1, -1)
         up_2, down_2 = z_shift(up_2, 1), z_shift(down_2, -1)
-        if s == 2:
-            up_1, side = lax.optimization_barrier((up_1, side))
+        if s == 1:
+            down_1, side = lax.optimization_barrier((down_1, side))
         (early if s < 3 else late).extend(
             [(up_1, parts_1(-s)), (down_1, parts_1(s)), (up_2, parts_2(-s)), (down_2, parts_2(s))]
         )

time: 132 us -> 128 us (0.970)
  waiting for transfers between devices: 15.9 us -> 13.2 us
    ppermute x14, waiting for transfers between devices: 7.34 us -> 5.65 us  [z_shift(): return lax.ppermute(x, 'ocn', perm)]
  transfers between devices with their start and end apart: 22 -> 22, of which waited for: 5 -> 9; matrix products, arithmetic and copies ran while one was open for 1% -> 2% of each run, Pallas kernels for 2% -> 2%
where the time goes in v5:
time: 128 us; the launch traced here: 127 us
  starting transfers between devices  83 us (65%)
  blocking collectives  21.9 us (17%)
  waiting for transfers between devices  13.2 us (10%)
  Pallas kernels  5.44 us (4%)
  local copies, waits for them, and re-layouts  2.86 us (2%)
    ppermute x14, starting transfers between devices, z_shift(): return lax.ppermute(x, 'ocn', perm)  54.8 us
    ppermute x7, starting transfers between devices, y_shift(): return lax.ppermute(x, 'ocn', perm)  26.3 us
    all_to_all x1, blocking collectives, per_device(): lax.all_to_all(parts, 'mem', split_axis=0, concat_axis=0, axis_index_grou...  21.9 us
    ppermute x14, waiting for transfers between devices, z_shift(): return lax.ppermute(x, 'ocn', perm)  5.65 us
    ppermute x7, waiting for transfers between devices, y_shift(): return lax.ppermute(x, 'ocn', perm)  4.77 us
    pallas_call x2, Pallas kernels, cross(): pl.pallas_call(functools.partial(cross_kernel, groups, before is None), o...  3.98 us
    ppermute x1, waiting for transfers between devices, per_device(): lax.ppermute(parts[1], 'mem', [(m, m ^ 1) for m in range(n_mem)])  2.81 us
  transfers between devices with their start and end apart: 22, of which 9 were waited for; matrix products, arithmetic and copies ran while one was open for 2% of the time, Pallas kernels for 2%

profile of v5, /device:TPU:56, one launch (start us, length us, event | category | flops | bytes accessed | tf_op | source)
XLA Modules:
  0.0 127.2 jit_solution(5239351988416048126)
XLA Ops:
  0.0 1.0 dynamic-slice_bitcast_fusion.1
  1.0 4.0 %collective-permute-start.9 = (bf16[32,2048]{1,0:T(8,128)(2,1)S(1)}, bf16[32,2048]{1,0:T(8,128)(2,1)S(1)}, u32[]{:S(2)}, u32[]{:S(2)}) collective-permute-start(bf16[32,2048]{1,0:T(8,128)(2,1)S(1)} %get-tuple-element.22), channel_id=1, source_target_pairs={{0,24},{1,25},{2,26},{3,27},{4,28},{5,29},{6,30},{7,31},{8,0},{9,1... | collective-permute-start | bytes 393224 | tf_op jit(solution)/shard_map/ppermute | solution.py:24
  5.0 3.9 %collective-permute-start = (bf16[32,2048]{1,0:T(8,128)(2,1)S(1)}, bf16[32,2048]{1,0:T(8,128)(2,1)S(1)}, u32[]{:S(2)}, u32[]{:S(2)}) collective-permute-start(bf16[32,2048]{1,0:T(8,128)(2,1)S(1)} %get-tuple-element.22), channel_id=1, source_target_pairs={{0,8},{1,9},{2,10},{3,11},{4,12},{5,13},{6,14},{7,15},{8,16},{9,17... | collective-permute-start | bytes 393224 | tf_op jit(solution)/shard_map/ppermute | solution.py:24
  9.0 4.7 %collective-permute-start.10 = (bf16[32,2048]{1,0:T(8,128)(2,1)S(1)}, bf16[32,2048]{1,0:T(8,128)(2,1)S(1)}, u32[]{:S(2)}, u32[]{:S(2)}) collective-permute-start(bf16[32,2048]{1,0:T(8,128)(2,1)S(1)} %get-tuple-element.21), channel_id=1, source_target_pairs={{0,16},{1,17},{2,18},{3,19},{4,20},{5,21},{6,22},{7,23},{8,24},{9,... | collective-permute-start | bytes 393224 | tf_op jit(solution)/shard_map/ppermute | solution.py:24
  13.7 1.7 %constant_dynamic-slice_fusion = (bf16[2048,256]{1,0:T(8,128)(2,1)S(1)}, bf16[2048,256]{1,0:T(8,128)(2,1)S(1)}) fusion(bf16[4096,256]{1,0:T(8,128)(2,1)} %param.6, s32[]{:T(128)S(6)} %select_n.14, s32[]{:T(128)S(6)} %select_n.15), kind=kLoop, calls=%fused_computation.9 | loop fusion | bytes 4194312 | tf_op jit(solution)/shard_map/dynamic_slice | solution.py:154
  15.4 5.4 %collective-permute-start.1 = (bf16[64,2048]{1,0:T(8,128)(2,1)S(1)}, bf16[64,2048]{1,0:T(8,128)(2,1)S(1)}, u32[]{:S(2)}, u32[]{:S(2)}) collective-permute-start(bf16[64,2048]{1,0:T(8,128)(2,1)S(1)} %pad_maximum_fusion.1.refs_0_), channel_id=1, source_target_pairs={{0,1},{1,2},{2,3},{3,4},{4,5},{5,6},{6,7},{7,0},{8,9},{9,10},{10,1... | collective-permute-start | bytes 786440 | tf_op jit(solution)/shard_map/ppermute | solution.py:19
  20.9 5.0 %collective-permute-start.5 = (bf16[2048,128]{1,0:T(8,128)(2,1)S(1)}, bf16[2048,128]{1,0:T(8,128)(2,1)S(1)}, u32[]{:S(2)}, u32[]{:S(2)}) collective-permute-start(bf16[2048,128]{1,0:T(8,128)(2,1)S(1)} %get-tuple-element.19), channel_id=1, source_target_pairs={{0,8},{1,9},{2,10},{3,11},{4,12},{5,13},{6,14},{7,15},{8,16},{9,17... | collective-permute-start | bytes 1572872 | tf_op jit(solution)/shard_map/ppermute | solution.py:24
  25.9 1.9 %collective-permute-start.6 = (bf16[2048,128]{1,0:T(8,128)(2,1)S(1)}, bf16[2048,128]{1,0:T(8,128)(2,1)S(1)}, u32[]{:S(2)}, u32[]{:S(2)}) collective-permute-start(bf16[2048,128]{1,0:T(8,128)(2,1)S(1)} %get-tuple-element.20), channel_id=1, source_target_pairs={{0,24},{1,25},{2,26},{3,27},{4,28},{5,29},{6,30},{7,31},{8,0},{9,1... | collective-permute-start | bytes 1572872 | tf_op jit(solution)/shard_map/ppermute | solution.py:24
  27.9 8.6 %collective-permute-start.14 = (bf16[64,2048]{1,0:T(8,128)(2,1)S(1)}, bf16[64,2048]{1,0:T(8,128)(2,1)S(1)}, u32[]{:S(2)}, u32[]{:S(2)}) collective-permute-start(bf16[64,2048]{1,0:T(8,128)(2,1)S(1)} %constant_dynamic-update-slice_fusion.refs_1_), channel_id=1, source_target_pairs={{0,7},{1,0},{2,1},{3,2},{4,3},{5,4},{6,5},{7,6},{8,15},{9,8},{10,9... | collective-permute-start | bytes 786440 | tf_op jit(solution)/shard_map/ppermute | solution.py:19
  36.5 1.9 %collective-permute-start.11 = (bf16[64,2048]{1,0:T(8,128)(2,1)S(1)}, bf16[64,2048]{1,0:T(8,128)(2,1)S(1)}, u32[]{:S(2)}, u32[]{:S(2)}) collective-permute-start(bf16[64,2048]{1,0:T(8,128)(2,1)S(1)} %constant_dynamic-update-slice_fusion.refs_1_), channel_id=1, source_target_pairs={{0,1},{1,2},{2,3},{3,4},{4,5},{5,6},{6,7},{7,0},{8,9},{9,10},{10,1... | collective-permute-start | bytes 786440 | tf_op jit(solution)/shard_map/ppermute | solution.py:19
  38.4 5.1 %collective-permute-start.4 = (bf16[64,2048]{1,0:T(8,128)(2,1)S(1)}, bf16[64,2048]{1,0:T(8,128)(2,1)S(1)}, u32[]{:S(2)}, u32[]{:S(2)}) collective-permute-start(bf16[64,2048]{1,0:T(8,128)(2,1)S(1)} %pad_maximum_fusion.1.refs_0_), channel_id=1, source_target_pairs={{0,7},{1,0},{2,1},{3,2},{4,3},{5,4},{6,5},{7,6},{8,15},{9,8},{10,9... | collective-permute-start | bytes 786440 | tf_op jit(solution)/shard_map/ppermute | solution.py:19
  43.6 1.9 %collective-permute-start.2 = (bf16[64,2048]{1,0:T(8,128)(2,1)S(1)}, bf16[64,2048]{1,0:T(8,128)(2,1)S(1)}, u32[]{:S(2)}, u32[]{:S(2)}) collective-permute-start(bf16[64,2048]{1,0:T(8,128)(2,1)S(1)} %collective-permute-done.1.refs_2_), channel_id=1, source_target_pairs={{0,1},{1,2},{2,3},{3,4},{4,5},{5,6},{6,7},{7,0},{8,9},{9,10},{10,1... | collective-permute-start | bytes 786440 | tf_op jit(solution)/shard_map/ppermute | solution.py:19
  45.9 4.7 %collective-permute-start.15 = (bf16[64,2048]{1,0:T(8,128)(2,1)S(1)}, bf16[64,2048]{1,0:T(8,128)(2,1)S(1)}, u32[]{:S(2)}, u32[]{:S(2)}) collective-permute-start(bf16[64,2048]{1,0:T(8,128)(2,1)S(1)} %collective-permute-done.14.refs_5_), channel_id=1, source_target_pairs={{0,7},{1,0},{2,1},{3,2},{4,3},{5,4},{6,5},{7,6},{8,15},{9,8},{10,9... | collective-permute-start | bytes 786440 | tf_op jit(solution)/shard_map/ppermute | solution.py:19
  50.6 1.9 %collective-permute-start.12 = (bf16[64,2048]{1,0:T(8,128)(2,1)S(1)}, bf16[64,2048]{1,0:T(8,128)(2,1)S(1)}, u32[]{:S(2)}, u32[]{:S(2)}) collective-permute-start(bf16[64,2048]{1,0:T(8,128)(2,1)S(1)} %collective-permute-done.11.refs_4_), channel_id=1, source_target_pairs={{0,1},{1,2},{2,3},{3,4},{4,5},{5,6},{6,7},{7,0},{8,9},{9,10},{10,1... | collective-permute-start | bytes 786440 | tf_op jit(solution)/shard_map/ppermute | solution.py:19
  53.0 2.3 %collective-permute-start.3 = (bf16[64,2048]{1,0:T(8,128)(2,1)S(1)}, bf16[64,2048]{1,0:T(8,128)(2,1)S(1)}, u32[]{:S(2)}, u32[]{:S(2)}) collective-permute-start(bf16[64,2048]{1,0:T(8,128)(2,1)S(1)} %collective-permute-done.2.refs_6_), channel_id=1, source_target_pairs={{0,1},{1,2},{2,3},{3,4},{4,5},{5,6},{6,7},{7,0},{8,9},{9,10},{10,1... | collective-permute-start | bytes 786440 | tf_op jit(solution)/shard_map/ppermute | solution.py:19
  55.3 6.5 %collective-permute-start.16 = (bf16[64,2048]{1,0:T(8,128)(2,1)S(1)}, bf16[64,2048]{1,0:T(8,128)(2,1)S(1)}, u32[]{:S(2)}, u32[]{:S(2)}) collective-permute-start(bf16[64,2048]{1,0:T(8,128)(2,1)S(1)} %collective-permute-done.15.refs_9_), channel_id=1, source_target_pairs={{0,7},{1,0},{2,1},{3,2},{4,3},{5,4},{6,5},{7,6},{8,15},{9,8},{10,9... | collective-permute-start | bytes 786440 | tf_op jit(solution)/shard_map/ppermute | solution.py:19
  61.8 3.9 %collective-permute-start.7 = (bf16[64,2048]{1,0:T(8,128)(2,1)S(1)}, bf16[64,2048]{1,0:T(8,128)(2,1)S(1)}, u32[]{:S(2)}, u32[]{:S(2)}) collective-permute-start(bf16[64,2048]{1,0:T(8,128)(2,1)S(1)} %collective-permute-done.4.refs_3_), channel_id=1, source_target_pairs={{0,7},{1,0},{2,1},{3,2},{4,3},{5,4},{6,5},{7,6},{8,15},{9,8},{10,9... | collective-permute-start | bytes 786440 | tf_op jit(solution)/shard_map/ppermute | solution.py:19
  65.8 1.9 %collective-permute-start.13 = (bf16[64,2048]{1,0:T(8,128)(2,1)S(1)}, bf16[64,2048]{1,0:T(8,128)(2,1)S(1)}, u32[]{:S(2)}, u32[]{:S(2)}) collective-permute-start(bf16[64,2048]{1,0:T(8,128)(2,1)S(1)} %collective-permute-done.12.refs_8_), channel_id=1, source_target_pairs={{0,1},{1,2},{2,3},{3,4},{4,5},{5,6},{6,7},{7,0},{8,9},{9,10},{10,1... | collective-permute-start | bytes 786440 | tf_op jit(solution)/shard_map/ppermute | solution.py:19
  68.1 1.9 %collective-permute-start.17 = (bf16[64,2048]{1,0:T(8,128)(2,1)S(1)}, bf16[64,2048]{1,0:T(8,128)(2,1)S(1)}, u32[]{:S(2)}, u32[]{:S(2)}) collective-permute-start(bf16[64,2048]{1,0:T(8,128)(2,1)S(1)} %collective-permute-done.3.refs_0_), channel_id=1, source_target_pairs={{0,1},{1,2},{2,3},{3,4},{4,5},{5,6},{6,7},{7,0},{8,9},{9,10},{10,1... | collective-permute-start | bytes 786440 | tf_op jit(solution)/shard_map/ppermute | solution.py:19
  70.0 5.1 %collective-permute-start.18 = (bf16[64,2048]{1,0:T(8,128)(2,1)S(1)}, bf16[64,2048]{1,0:T(8,128)(2,1)S(1)}, u32[]{:S(2)}, u32[]{:S(2)}) collective-permute-start(bf16[64,2048]{1,0:T(8,128)(2,1)S(1)} %collective-permute-done.16.refs_3_), channel_id=1, source_target_pairs={{0,7},{1,0},{2,1},{3,2},{4,3},{5,4},{6,5},{7,6},{8,15},{9,8},{10,9... | collective-permute-start | bytes 786440 | tf_op jit(solution)/shard_map/ppermute | solution.py:19
  75.2 3.6 %collective-permute-start.8 = (bf16[64,2048]{1,0:T(8,128)(2,1)S(1)}, bf16[64,2048]{1,0:T(8,128)(2,1)S(1)}, u32[]{:S(2)}, u32[]{:S(2)}) collective-permute-start(bf16[64,2048]{1,0:T(8,128)(2,1)S(1)} %collective-permute-done.7.refs_7_), channel_id=1, source_target_pairs={{0,7},{1,0},{2,1},{3,2},{4,3},{5,4},{6,5},{7,6},{8,15},{9,8},{10,9... | collective-permute-start | bytes 786440 | tf_op jit(solution)/shard_map/ppermute | solution.py:19
  78.7 2.5 %shard_map.55.refs_8_ = f32[2,8,72,512]{3,2,1,0:T(8,128)S(1)} custom-call(bf16[64,2048]{1,0:T(8,128)(2,1)S(1)} %pad_maximum_fusion.1.refs_0_, bf16[64,2048]{1,0:T(8,128)(2,1)S(1)} %constant_dynamic-update-slice_fusion.refs_1_, bf16[64,2048]{1,0:T(8,128)(2,1)S(1)} %collective-permute-done.1.refs_2_, bf16[64,2048]{1,0:T(8,128)(2,1)S(1)} %collective-permute-done.4.refs_3_, ...), custom_call_target="tpu_custom_call" | custom-call | flops 1342177280 | bytes 4718592 | tf_op jit(solution)/shard_map/pallas_call | solution.py:96
  81.2 0.5 collective-permute-done.17.refs_4_
  81.9 3.8 %collective-permute-done.8.refs_1_ = bf16[64,2048]{1,0:T(8,128)(2,1)S(1)} collective-permute-done((bf16[64,2048]{1,0:T(8,128)(2,1)S(1)}, bf16[64,2048]{1,0:T(8,128)(2,1)S(1)}, u32[]{:S(2)}, u32[]{:S(2)}) %collective-permute-start.8) | collective-permute-done | bytes 262176 | tf_op jit(solution)/shard_map/ppermute | solution.py:19
  85.7 1.5 %shard_map.56 = f32[2,8,72,512]{3,2,1,0:T(8,128)S(1)} custom-call(bf16[64,2048]{1,0:T(8,128)(2,1)S(1)} %collective-permute-done.3.refs_0_, bf16[64,2048]{1,0:T(8,128)(2,1)S(1)} %collective-permute-done.8.refs_1_, bf16[64,2048]{1,0:T(8,128)(2,1)S(1)} %collective-permute-done.13.refs_2_, ...), custom_call_target="tpu_custom_call", output_to_operand_aliasing={{}: (8, {})} | custom-call | flops 805306368 | bytes 3670016 | tf_op jit(solution)/shard_map/pallas_call | solution.py:96
  87.3 1.9 %collective-permute-start.19 = (f32[8,72,512]{2,1,0:T(8,128)S(1)}, f32[8,72,512]{2,1,0:T(8,128)S(1)}, u32[]{:S(2)}, u32[]{:S(2)}) collective-permute-start(f32[8,72,512]{2,1,0:T(8,128)S(1)} %slice_bitcast_fusion), channel_id=1, source_target_pairs={{0,32},{32,0},{64,96},{96,64},{128,160},{160,128},{192,224},{224,1... | collective-permute-start | bytes 3538952 | tf_op jit(solution)/shard_map/ppermute | solution.py:183
  89.2 2.8 %collective-permute-done.19 = f32[8,72,512]{2,1,0:T(8,128)S(1)} collective-permute-done((f32[8,72,512]{2,1,0:T(8,128)S(1)}, f32[8,72,512]{2,1,0:T(8,128)S(1)}, u32[]{:S(2)}, u32[]{:S(2)}) %collective-permute-start.19) | collective-permute-done | bytes 1179680 | tf_op jit(solution)/shard_map/ppermute | solution.py:183
  92.3 21.9 %all_to_all.5.parts_ref = f32[8,72,512]{2,1,0:T(8,128)S(1)} all-to-all(f32[8,72,512]{2,1,0:T(8,128)S(1)} %fusion), channel_id=1, replica_groups={{0,64,128,192,256,320,384,448},{32,96,160,224,288,352,416,480},{1,65,12..., dimensions={0} | all-to-all | bytes 2359296 | tf_op jit(solution)/shard_map/all_to_all | solution.py:185
  114.3 3.4 %collective-permute-start.20 = (f32[72,128]{1,0:T(8,128)S(1)}, f32[72,128]{1,0:T(8,128)S(1)}, u32[]{:S(2)}, u32[]{:S(2)}) collective-permute-start(f32[72,128]{1,0:T(8,128)S(1)} %get-tuple-element.15), channel_id=1, source_target_pairs={{0,8},{1,9},{2,10},{3,11},{4,12},{5,13},{6,14},{7,15},{8,16},{9,17... | collective-permute-start | bytes 110600 | tf_op jit(solution)/shard_map/ppermute | solution.py:24
  117.8 3.3 %collective-permute-start.21 = (f32[72,128]{1,0:T(8,128)S(1)}, f32[72,128]{1,0:T(8,128)S(1)}, u32[]{:S(2)}, u32[]{:S(2)}) collective-permute-start(f32[72,128]{1,0:T(8,128)S(1)} %get-tuple-element.16), channel_id=1, source_target_pairs={{0,24},{1,25},{2,26},{3,27},{4,28},{5,29},{6,30},{7,31},{8,0},{9,1... | collective-permute-start | bytes 110600 | tf_op jit(solution)/shard_map/ppermute | solution.py:24
  121.2 4.7 %collective-permute-done.21.high_ref = f32[72,128]{1,0:T(8,128)S(1)} collective-permute-done((f32[72,128]{1,0:T(8,128)S(1)}, f32[72,128]{1,0:T(8,128)S(1)}, u32[]{:S(2)}, u32[]{:S(2)}) %collective-permute-start.21) | collective-permute-done | bytes 36896 | tf_op jit(solution)/shard_map/ppermute | solution.py:24
  125.9 1.4 %shard_map.58 = f32[64,256]{1,0:T(8,128)} custom-call(f32[72,256]{1,0:T(8,128)S(1)} %get-tuple-element.14.near_ref, f32[72,128]{1,0:T(8,128)S(1)} %collective-permute-done.20.low_ref, f32[72,128]{1,0:T(8,128)S(1)} %collective-permute-done.21.high_ref, s32[1,2]{1,0:T(1,128)S(1)} %copy-done, s32[1,2]{1,0:T(1,128)S(1)} %copy-done.1, f32[8]{0:T(128)S(1)} %copy-done.2), custom_call_target="tpu_custom_call" | custom-call | tf_op jit(solution)/shard_map/pallas_call | solution.py:196
  (32 shorter events, 2.1 us)
Async XLA Ops:
  1.0 26.8 %collective-permute-start.9 = (bf16[32,2048]{1,0:T(8,128)(2,1)S(1)}, bf16[32,2048]{1,0:T(8,128)(2,1)S(1)}, u32[]{:S(2)}, u32[]{:S(2)}) collective-permute-start(bf16[32,2048]{1,0:T(8,128)(2,1)S(1)} %get-tuple-element.22), channel_id=1, source_target_pairs={{0,24},{1,25},{2,26},{3,27},{4,28},{5,29},{6,30},{7,31},{8,0},{9,1... | collective-permute-start | bytes 393224 | tf_op jit(solution)/shard_map/ppermute | solution.py:24
  5.0 10.3 %collective-permute-start = (bf16[32,2048]{1,0:T(8,128)(2,1)S(1)}, bf16[32,2048]{1,0:T(8,128)(2,1)S(1)}, u32[]{:S(2)}, u32[]{:S(2)}) collective-permute-start(bf16[32,2048]{1,0:T(8,128)(2,1)S(1)} %get-tuple-element.22), channel_id=1, source_target_pairs={{0,8},{1,9},{2,10},{3,11},{4,12},{5,13},{6,14},{7,15},{8,16},{9,17... | collective-permute-start | bytes 393224 | tf_op jit(solution)/shard_map/ppermute | solution.py:24
  9.0 18.9 %collective-permute-start.10 = (bf16[32,2048]{1,0:T(8,128)(2,1)S(1)}, bf16[32,2048]{1,0:T(8,128)(2,1)S(1)}, u32[]{:S(2)}, u32[]{:S(2)}) collective-permute-start(bf16[32,2048]{1,0:T(8,128)(2,1)S(1)} %get-tuple-element.21), channel_id=1, source_target_pairs={{0,16},{1,17},{2,18},{3,19},{4,20},{5,21},{6,22},{7,23},{8,24},{9,... | collective-permute-start | bytes 393224 | tf_op jit(solution)/shard_map/ppermute | solution.py:24
  15.4 23.0 %collective-permute-start.1 = (bf16[64,2048]{1,0:T(8,128)(2,1)S(1)}, bf16[64,2048]{1,0:T(8,128)(2,1)S(1)}, u32[]{:S(2)}, u32[]{:S(2)}) collective-permute-start(bf16[64,2048]{1,0:T(8,128)(2,1)S(1)} %pad_maximum_fusion.1.refs_0_), channel_id=1, source_target_pairs={{0,1},{1,2},{2,3},{3,4},{4,5},{5,6},{6,7},{7,0},{8,9},{9,10},{10,1... | collective-permute-start | bytes 786440 | tf_op jit(solution)/shard_map/ppermute | solution.py:19
  20.9 29.7 %collective-permute-start.5 = (bf16[2048,128]{1,0:T(8,128)(2,1)S(1)}, bf16[2048,128]{1,0:T(8,128)(2,1)S(1)}, u32[]{:S(2)}, u32[]{:S(2)}) collective-permute-start(bf16[2048,128]{1,0:T(8,128)(2,1)S(1)} %get-tuple-element.19), channel_id=1, source_target_pairs={{0,8},{1,9},{2,10},{3,11},{4,12},{5,13},{6,14},{7,15},{8,16},{9,17... | collective-permute-start | bytes 1572872 | tf_op jit(solution)/shard_map/ppermute | solution.py:24
  25.9 26.7 %collective-permute-start.6 = (bf16[2048,128]{1,0:T(8,128)(2,1)S(1)}, bf16[2048,128]{1,0:T(8,128)(2,1)S(1)}, u32[]{:S(2)}, u32[]{:S(2)}) collective-permute-start(bf16[2048,128]{1,0:T(8,128)(2,1)S(1)} %get-tuple-element.20), channel_id=1, source_target_pairs={{0,24},{1,25},{2,26},{3,27},{4,28},{5,29},{6,30},{7,31},{8,0},{9,1... | collective-permute-start | bytes 1572872 | tf_op jit(solution)/shard_map/ppermute | solution.py:24
  27.9 15.7 %collective-permute-start.14 = (bf16[64,2048]{1,0:T(8,128)(2,1)S(1)}, bf16[64,2048]{1,0:T(8,128)(2,1)S(1)}, u32[]{:S(2)}, u32[]{:S(2)}) collective-permute-start(bf16[64,2048]{1,0:T(8,128)(2,1)S(1)} %constant_dynamic-update-slice_fusion.refs_1_), channel_id=1, source_target_pairs={{0,7},{1,0},{2,1},{3,2},{4,3},{5,4},{6,5},{7,6},{8,15},{9,8},{10,9... | collective-permute-start | bytes 786440 | tf_op jit(solution)/shard_map/ppermute | solution.py:19
  36.5 9.5 %collective-permute-start.11 = (bf16[64,2048]{1,0:T(8,128)(2,1)S(1)}, bf16[64,2048]{1,0:T(8,128)(2,1)S(1)}, u32[]{:S(2)}, u32[]{:S(2)}) collective-permute-start(bf16[64,2048]{1,0:T(8,128)(2,1)S(1)} %constant_dynamic-update-slice_fusion.refs_1_), channel_id=1, source_target_pairs={{0,1},{1,2},{2,3},{3,4},{4,5},{5,6},{6,7},{7,0},{8,9},{9,10},{10,1... | collective-permute-start | bytes 786440 | tf_op jit(solution)/shard_map/ppermute | solution.py:19
  38.4 14.3 %collective-permute-start.4 = (bf16[64,2048]{1,0:T(8,128)(2,1)S(1)}, bf16[64,2048]{1,0:T(8,128)(2,1)S(1)}, u32[]{:S(2)}, u32[]{:S(2)}) collective-permute-start(bf16[64,2048]{1,0:T(8,128)(2,1)S(1)} %pad_maximum_fusion.1.refs_0_), channel_id=1, source_target_pairs={{0,7},{1,0},{2,1},{3,2},{4,3},{5,4},{6,5},{7,6},{8,15},{9,8},{10,9... | collective-permute-start | bytes 786440 | tf_op jit(solution)/shard_map/ppermute | solution.py:19
  43.6 9.5 %collective-permute-start.2 = (bf16[64,2048]{1,0:T(8,128)(2,1)S(1)}, bf16[64,2048]{1,0:T(8,128)(2,1)S(1)}, u32[]{:S(2)}, u32[]{:S(2)}) collective-permute-start(bf16[64,2048]{1,0:T(8,128)(2,1)S(1)} %collective-permute-done.1.refs_2_), channel_id=1, source_target_pairs={{0,1},{1,2},{2,3},{3,4},{4,5},{5,6},{6,7},{7,0},{8,9},{9,10},{10,1... | collective-permute-start | bytes 786440 | tf_op jit(solution)/shard_map/ppermute | solution.py:19
  45.9 9.4 %collective-permute-start.15 = (bf16[64,2048]{1,0:T(8,128)(2,1)S(1)}, bf16[64,2048]{1,0:T(8,128)(2,1)S(1)}, u32[]{:S(2)}, u32[]{:S(2)}) collective-permute-start(bf16[64,2048]{1,0:T(8,128)(2,1)S(1)} %collective-permute-done.14.refs_5_), channel_id=1, source_target_pairs={{0,7},{1,0},{2,1},{3,2},{4,3},{5,4},{6,5},{7,6},{8,15},{9,8},{10,9... | collective-permute-start | bytes 786440 | tf_op jit(solution)/shard_map/ppermute | solution.py:19
  50.6 15.1 %collective-permute-start.12 = (bf16[64,2048]{1,0:T(8,128)(2,1)S(1)}, bf16[64,2048]{1,0:T(8,128)(2,1)S(1)}, u32[]{:S(2)}, u32[]{:S(2)}) collective-permute-start(bf16[64,2048]{1,0:T(8,128)(2,1)S(1)} %collective-permute-done.11.refs_4_), channel_id=1, source_target_pairs={{0,1},{1,2},{2,3},{3,4},{4,5},{5,6},{6,7},{7,0},{8,9},{9,10},{10,1... | collective-permute-start | bytes 786440 | tf_op jit(solution)/shard_map/ppermute | solution.py:19
  53.0 15.1 %collective-permute-start.3 = (bf16[64,2048]{1,0:T(8,128)(2,1)S(1)}, bf16[64,2048]{1,0:T(8,128)(2,1)S(1)}, u32[]{:S(2)}, u32[]{:S(2)}) collective-permute-start(bf16[64,2048]{1,0:T(8,128)(2,1)S(1)} %collective-permute-done.2.refs_6_), channel_id=1, source_target_pairs={{0,1},{1,2},{2,3},{3,4},{4,5},{5,6},{6,7},{7,0},{8,9},{9,10},{10,1... | collective-permute-start | bytes 786440 | tf_op jit(solution)/shard_map/ppermute | solution.py:19
  55.3 14.7 %collective-permute-start.16 = (bf16[64,2048]{1,0:T(8,128)(2,1)S(1)}, bf16[64,2048]{1,0:T(8,128)(2,1)S(1)}, u32[]{:S(2)}, u32[]{:S(2)}) collective-permute-start(bf16[64,2048]{1,0:T(8,128)(2,1)S(1)} %collective-permute-done.15.refs_9_), channel_id=1, source_target_pairs={{0,7},{1,0},{2,1},{3,2},{4,3},{5,4},{6,5},{7,6},{8,15},{9,8},{10,9... | collective-permute-start | bytes 786440 | tf_op jit(solution)/shard_map/ppermute | solution.py:19
  61.8 13.3 %collective-permute-start.7 = (bf16[64,2048]{1,0:T(8,128)(2,1)S(1)}, bf16[64,2048]{1,0:T(8,128)(2,1)S(1)}, u32[]{:S(2)}, u32[]{:S(2)}) collective-permute-start(bf16[64,2048]{1,0:T(8,128)(2,1)S(1)} %collective-permute-done.4.refs_3_), channel_id=1, source_target_pairs={{0,7},{1,0},{2,1},{3,2},{4,3},{5,4},{6,5},{7,6},{8,15},{9,8},{10,9... | collective-permute-start | bytes 786440 | tf_op jit(solution)/shard_map/ppermute | solution.py:19
  65.8 15.4 %collective-permute-start.13 = (bf16[64,2048]{1,0:T(8,128)(2,1)S(1)}, bf16[64,2048]{1,0:T(8,128)(2,1)S(1)}, u32[]{:S(2)}, u32[]{:S(2)}) collective-permute-start(bf16[64,2048]{1,0:T(8,128)(2,1)S(1)} %collective-permute-done.12.refs_8_), channel_id=1, source_target_pairs={{0,1},{1,2},{2,3},{3,4},{4,5},{5,6},{6,7},{7,0},{8,9},{9,10},{10,1... | collective-permute-start | bytes 786440 | tf_op jit(solution)/shard_map/ppermute | solution.py:19
  68.1 13.6 %collective-permute-start.17 = (bf16[64,2048]{1,0:T(8,128)(2,1)S(1)}, bf16[64,2048]{1,0:T(8,128)(2,1)S(1)}, u32[]{:S(2)}, u32[]{:S(2)}) collective-permute-start(bf16[64,2048]{1,0:T(8,128)(2,1)S(1)} %collective-permute-done.3.refs_0_), channel_id=1, source_target_pairs={{0,1},{1,2},{2,3},{3,4},{4,5},{5,6},{6,7},{7,0},{8,9},{9,10},{10,1... | collective-permute-start | bytes 786440 | tf_op jit(solution)/shard_map/ppermute | solution.py:19
  70.0 11.9 %collective-permute-start.18 = (bf16[64,2048]{1,0:T(8,128)(2,1)S(1)}, bf16[64,2048]{1,0:T(8,128)(2,1)S(1)}, u32[]{:S(2)}, u32[]{:S(2)}) collective-permute-start(bf16[64,2048]{1,0:T(8,128)(2,1)S(1)} %collective-permute-done.16.refs_3_), channel_id=1, source_target_pairs={{0,7},{1,0},{2,1},{3,2},{4,3},{5,4},{6,5},{7,6},{8,15},{9,8},{10,9... | collective-permute-start | bytes 786440 | tf_op jit(solution)/shard_map/ppermute | solution.py:19
  75.2 10.5 %collective-permute-start.8 = (bf16[64,2048]{1,0:T(8,128)(2,1)S(1)}, bf16[64,2048]{1,0:T(8,128)(2,1)S(1)}, u32[]{:S(2)}, u32[]{:S(2)}) collective-permute-start(bf16[64,2048]{1,0:T(8,128)(2,1)S(1)} %collective-permute-done.7.refs_7_), channel_id=1, source_target_pairs={{0,7},{1,0},{2,1},{3,2},{4,3},{5,4},{6,5},{7,6},{8,15},{9,8},{10,9... | collective-permute-start | bytes 786440 | tf_op jit(solution)/shard_map/ppermute | solution.py:19
  87.3 4.7 %collective-permute-start.19 = (f32[8,72,512]{2,1,0:T(8,128)S(1)}, f32[8,72,512]{2,1,0:T(8,128)S(1)}, u32[]{:S(2)}, u32[]{:S(2)}) collective-permute-start(f32[8,72,512]{2,1,0:T(8,128)S(1)} %slice_bitcast_fusion), channel_id=1, source_target_pairs={{0,32},{32,0},{64,96},{96,64},{128,160},{160,128},{192,224},{224,1... | collective-permute-start | bytes 3538952 | tf_op jit(solution)/shard_map/ppermute | solution.py:183
  92.3 33.6 %copy-start = (s32[1,2]{1,0:T(1,128)S(1)}, s32[1,2]{1,0:T(1,128)}, u32[]{:S(2)}) copy-start(s32[1,2]{1,0:T(1,128)} %cutoff_ref.1) | copy-start | bytes 28
  92.3 33.6 %copy-start.1 = (s32[1,2]{1,0:T(1,128)S(1)}, s32[1,2]{1,0:T(1,128)}, u32[]{:S(2)}) copy-start(s32[1,2]{1,0:T(1,128)} %index_ref.1) | copy-start | bytes 28
  92.3 33.5 %copy-start.2 = (f32[8]{0:T(128)S(1)}, f32[8]{0:T(128)}, u32[]{:S(2)}) copy-start(f32[8]{0:T(128)} %table_ref.1) | copy-start | bytes 100
  114.3 6.9 %collective-permute-start.20 = (f32[72,128]{1,0:T(8,128)S(1)}, f32[72,128]{1,0:T(8,128)S(1)}, u32[]{:S(2)}, u32[]{:S(2)}) collective-permute-start(f32[72,128]{1,0:T(8,128)S(1)} %get-tuple-element.15), channel_id=1, source_target_pairs={{0,8},{1,9},{2,10},{3,11},{4,12},{5,13},{6,14},{7,15},{8,16},{9,17... | collective-permute-start | bytes 110600 | tf_op jit(solution)/shard_map/ppermute | solution.py:24
  117.8 8.1 %collective-permute-start.21 = (f32[72,128]{1,0:T(8,128)S(1)}, f32[72,128]{1,0:T(8,128)S(1)}, u32[]{:S(2)}, u32[]{:S(2)}) collective-permute-start(f32[72,128]{1,0:T(8,128)S(1)} %get-tuple-element.16), channel_id=1, source_target_pairs={{0,24},{1,25},{2,26},{3,27},{4,28},{5,29},{6,30},{7,31},{8,0},{9,1... | collective-permute-start | bytes 110600 | tf_op jit(solution)/shard_map/ppermute | solution.py:24

commit v6 on v5

--- a/solution.py
+++ b/solution.py
@@ -39,7 +39,7 @@
     n = len(groups)
     blocks, near_ref, side_ref = refs[:n], refs[n], refs[n + 1]
     out_ref, rows_ref, cov_ref, sq_ref, sem = refs[-5:]
-    own = out_ref.shape[2] - EXTRA
+    own = out_ref.shape[3] - EXTRA
     per = own // 2
     cols = near_ref.shape[1]
     copies, placed = [], []
@@ -54,8 +54,8 @@
         for i, ref in enumerate((near_ref, side_ref)):
             ocean_f = ref[...].astype(jnp.float32)
             lines = jnp.where(line == 2, jnp.sum(ocean_f * ocean_f, axis=0, keepdims=True), 0.0)
-            for m in range(2 * out_ref.shape[1]):
-                out_ref[m % 2, m // 2, own:, i * cols : (i + 1) * cols] = lines
+            for m in range(2 * out_ref.shape[2]):
+                out_ref[m % 2, i, m // 2, own:, :] = lines
     for c in copies:
         c.wait()
     tile = rows_ref.shape[0] // 2
@@ -75,12 +75,13 @@
     for i, (dy, dz) in enumerate(placed):
         origin = lax.rem(y + (dy + NY), NY) * NZ + lax.rem(z + (dz + NZ), NZ)
         owner, side = origin // 2, lax.rem(origin, 2)
-        to = (lax.rem(owner + core, 2), owner // 2)
+        whose, chip = lax.rem(owner + core, 2), owner // 2
         at = slice(i * per, (i + 1) * per)
-        out_ref[(*to, pl.ds(pl.multiple_of(side * per, per), per))] = cov_ref[at, :]
+        to = pl.ds(pl.multiple_of(side * per, per), per)
         lines = jnp.where(line == side, along_lanes(sq_ref[at, :]), 0.0)
-        out_ref[(*to, slice(own, None), slice(0, 128))] += lines
-        out_ref[(*to, slice(own, None), slice(cols, cols + 128))] += lines
+        for j in range(2):
+            out_ref[whose, j, chip, to, :] = cov_ref[at, j * cols : (j + 1) * cols]
+            out_ref[whose, j, chip, own:, :128] += lines
 
 
 def cross(pieces, near, side, sums_shape, before=None):
@@ -112,19 +113,19 @@
     )(*args)
 
 
-def sum_kernel(parts_ref, near_ref, left_ref, right_ref):
+def sides_kernel(parts_ref, left_ref, right_ref):
     total = jnp.sum(parts_ref[...], axis=0)
-    cols = near_ref.shape[1]
-    near_ref[...] = total[:, :cols]
-    left_ref[...] = total[:, cols : cols + cols // 2]
-    right_ref[...] = total[:, cols + cols // 2 :]
-
-
-def finish_kernel(members, near_ref, low_ref, high_ref, cutoff_ref, index_ref, table_ref, out_ref):
+    cols = total.shape[1] // 2
+    left_ref[...] = total[:, :cols]
+    right_ref[...] = total[:, cols:]
+
+
+def finish_kernel(members, parts_ref, low_ref, high_ref, cutoff_ref, index_ref, table_ref, out_ref):
     own, cols = out_ref.shape
     half = own // 2
-    total = near_ref[...] + jnp.concatenate([low_ref[...], high_ref[...]], axis=1)
-    squares = near_ref[own:, :128] + high_ref[own:, :]
+    near = jnp.sum(parts_ref[...], axis=0)
+    total = near + jnp.concatenate([low_ref[...], high_ref[...]], axis=1)
+    squares = near[own:, :128] + high_ref[own:, :]
     eye = lax.broadcasted_iota(jnp.int32, (own, own), 0) == lax.broadcasted_iota(jnp.int32, (own, own), 1)
     across = jnp.concatenate([squares[:1, :half], squares[1:2, :half]], axis=1)
     rowsq = jnp.sum(jnp.where(eye, across, 0.0), axis=1, keepdims=True)
@@ -177,21 +178,25 @@
         )
     late += [(z_shift(up_1, 1), parts_1(-4)), (z_shift(down_2, -1), parts_2(4))]
 
-    sums_shape = (2, n_mem // 2, own_rows + EXTRA, 2 * cols)
+    sums_shape = (2, 2, n_mem // 2, own_rows + EXTRA, cols)
     parts = cross(early, near, side, sums_shape)
     parts = cross(late, near, side, sums_shape, parts)
-    parts = parts[0] + lax.ppermute(parts[1], "mem", [(m, m ^ 1) for m in range(n_mem)])
+    received = lax.ppermute(parts[1], "mem", [(m, m ^ 1) for m in range(n_mem)])
     groups = [list(range(c, n_mem, 2)) for c in range(2)]
-    parts = lax.all_to_all(parts, "mem", split_axis=0, concat_axis=0, axis_index_groups=groups, tiled=True)
+    exchange = functools.partial(
+        lax.all_to_all, axis_name="mem", split_axis=0, concat_axis=0, axis_index_groups=groups, tiled=True
+    )
+    side_parts = exchange(parts[0, 1] + received[1])
+    near_parts = exchange(parts[0, 0] + received[0])
     vmem, smem = pl.BlockSpec(memory_space=pltpu.VMEM), pl.BlockSpec(memory_space=pltpu.SMEM)
     compiler_params = pltpu.CompilerParams(vmem_limit_bytes=16 * 1024 * 1024)
-    here, to_left, to_right = pl.pallas_call(
-        sum_kernel,
-        out_shape=[jax.ShapeDtypeStruct((own_rows + EXTRA, n), jnp.float32) for n in (cols, cols // 2, cols // 2)],
+    to_left, to_right = pl.pallas_call(
+        sides_kernel,
+        out_shape=[jax.ShapeDtypeStruct((own_rows + EXTRA, cols // 2), jnp.float32)] * 2,
         in_specs=[vmem],
-        out_specs=[vmem] * 3,
+        out_specs=[vmem] * 2,
         compiler_params=compiler_params,
-    )(parts)
+    )(side_parts)
     low, high = y_shift(to_right, 1), y_shift(to_left, -1)
     return pl.pallas_call(
         functools.partial(finish_kernel, members),
@@ -199,7 +204,7 @@
         in_specs=[vmem] * 3 + [smem] * 3,
         out_specs=vmem,
         compiler_params=compiler_params,
-    )(here, low, high, cutoff, factor_index, factor_table)
+    )(near_parts, low, high, cutoff, factor_index, factor_table)
 
 
 def solution(mesh):

time: 128 us -> 127 us (level)
  blocking collectives: 21.9 us -> 15.6 us
  starting transfers between devices: 83 us -> 87.7 us
    all_to_all x1, blocking collectives: 21.9 us -> 15.6 us  [per_device(): side_parts = exchange(parts[0, 1] + received[1])]
    all_to_all x0 -> x1, starting transfers between devices: none -> 4.72 us  [per_device(): near_parts = exchange(parts[0, 0] + received[0])]
    ppermute x7, waiting for transfers between devices: 4.77 us -> 2.06 us  [y_shift(): return lax.ppermute(x, 'ocn', perm)]
    all_to_all x0 -> x1, waiting for transfers between devices: none -> 2.59 us  [per_device(): near_parts = exchange(parts[0, 0] + received[0])]
  transfers between devices with their start and end apart: 22 -> 23, of which waited for: 9 -> 9; matrix products, arithmetic and copies ran while one was open for 2% -> 2% of each run, Pallas kernels for 2% -> 2%
where the time goes in v6:
time: 127 us; the launch traced here: 126 us
  starting transfers between devices  87.7 us (69%)
  blocking collectives  15.6 us (12%)
  waiting for transfers between devices  13.1 us (10%)
  Pallas kernels  5.44 us (4%)
  local copies, waits for them, and re-layouts  2.86 us (2%)
    ppermute x14, starting transfers between devices, z_shift(): return lax.ppermute(x, 'ocn', perm)  54.8 us
    ppermute x7, starting transfers between devices, y_shift(): return lax.ppermute(x, 'ocn', perm)  26.3 us
    all_to_all x1, blocking collectives, per_device(): side_parts = exchange(parts[0, 1] + received[1])  15.6 us
    ppermute x14, waiting for transfers between devices, z_shift(): return lax.ppermute(x, 'ocn', perm)  5.62 us
    all_to_all x1, starting transfers between devices, per_device(): near_parts = exchange(parts[0, 0] + received[0])  4.72 us
    pallas_call x2, Pallas kernels, cross(): pl.pallas_call(functools.partial(cross_kernel, groups, before is None), o...  4.02 us
    ppermute x1, waiting for transfers between devices, per_device(): received = lax.ppermute(parts[1], 'mem', [(m, m ^ 1) for m in range(n_mem)])  2.81 us
    all_to_all x1, waiting for transfers between devices, per_device(): near_parts = exchange(parts[0, 0] + received[0])  2.59 us
  transfers between devices with their start and end apart: 23, of which 9 were waited for; matrix products, arithmetic and copies ran while one was open for 2% of the time, Pallas kernels for 2%

profile of v6, /device:TPU:56, one launch (start us, length us, event | category | flops | bytes accessed | tf_op | source)
XLA Modules:
  0.0 126.2 jit_solution(12161782275406655118)
XLA Ops:
  1.0 4.0 %collective-permute-start.9 = (bf16[32,2048]{1,0:T(8,128)(2,1)S(1)}, bf16[32,2048]{1,0:T(8,128)(2,1)S(1)}, u32[]{:S(2)}, u32[]{:S(2)}) collective-permute-start(bf16[32,2048]{1,0:T(8,128)(2,1)S(1)} %get-tuple-element.22), channel_id=1, source_target_pairs={{0,24},{1,25},{2,26},{3,27},{4,28},{5,29},{6,30},{7,31},{8,0},{9,1... | collective-permute-start | bytes 393224 | tf_op jit(solution)/shard_map/ppermute | solution.py:24
  5.0 3.9 %collective-permute-start = (bf16[32,2048]{1,0:T(8,128)(2,1)S(1)}, bf16[32,2048]{1,0:T(8,128)(2,1)S(1)}, u32[]{:S(2)}, u32[]{:S(2)}) collective-permute-start(bf16[32,2048]{1,0:T(8,128)(2,1)S(1)} %get-tuple-element.22), channel_id=1, source_target_pairs={{0,8},{1,9},{2,10},{3,11},{4,12},{5,13},{6,14},{7,15},{8,16},{9,17... | collective-permute-start | bytes 393224 | tf_op jit(solution)/shard_map/ppermute | solution.py:24
  9.0 4.7 %collective-permute-start.10 = (bf16[32,2048]{1,0:T(8,128)(2,1)S(1)}, bf16[32,2048]{1,0:T(8,128)(2,1)S(1)}, u32[]{:S(2)}, u32[]{:S(2)}) collective-permute-start(bf16[32,2048]{1,0:T(8,128)(2,1)S(1)} %get-tuple-element.21), channel_id=1, source_target_pairs={{0,16},{1,17},{2,18},{3,19},{4,20},{5,21},{6,22},{7,23},{8,24},{9,... | collective-permute-start | bytes 393224 | tf_op jit(solution)/shard_map/ppermute | solution.py:24
  13.7 1.7 %constant_dynamic-slice_fusion = (bf16[2048,256]{1,0:T(8,128)(2,1)S(1)}, bf16[2048,256]{1,0:T(8,128)(2,1)S(1)}) fusion(bf16[4096,256]{1,0:T(8,128)(2,1)} %param.6, s32[]{:T(128)S(6)} %select_n.14, s32[]{:T(128)S(6)} %select_n.15), kind=kLoop, calls=%fused_computation.13 | loop fusion | bytes 4194312 | tf_op jit(solution)/shard_map/dynamic_slice | solution.py:155
  15.4 5.4 %collective-permute-start.1 = (bf16[64,2048]{1,0:T(8,128)(2,1)S(1)}, bf16[64,2048]{1,0:T(8,128)(2,1)S(1)}, u32[]{:S(2)}, u32[]{:S(2)}) collective-permute-start(bf16[64,2048]{1,0:T(8,128)(2,1)S(1)} %pad_maximum_fusion.1.refs_0_), channel_id=1, source_target_pairs={{0,1},{1,2},{2,3},{3,4},{4,5},{5,6},{6,7},{7,0},{8,9},{9,10},{10,1... | collective-permute-start | bytes 786440 | tf_op jit(solution)/shard_map/ppermute | solution.py:19
  20.9 5.0 %collective-permute-start.5 = (bf16[2048,128]{1,0:T(8,128)(2,1)S(1)}, bf16[2048,128]{1,0:T(8,128)(2,1)S(1)}, u32[]{:S(2)}, u32[]{:S(2)}) collective-permute-start(bf16[2048,128]{1,0:T(8,128)(2,1)S(1)} %get-tuple-element.19), channel_id=1, source_target_pairs={{0,8},{1,9},{2,10},{3,11},{4,12},{5,13},{6,14},{7,15},{8,16},{9,17... | collective-permute-start | bytes 1572872 | tf_op jit(solution)/shard_map/ppermute | solution.py:24
  25.9 1.9 %collective-permute-start.6 = (bf16[2048,128]{1,0:T(8,128)(2,1)S(1)}, bf16[2048,128]{1,0:T(8,128)(2,1)S(1)}, u32[]{:S(2)}, u32[]{:S(2)}) collective-permute-start(bf16[2048,128]{1,0:T(8,128)(2,1)S(1)} %get-tuple-element.20), channel_id=1, source_target_pairs={{0,24},{1,25},{2,26},{3,27},{4,28},{5,29},{6,30},{7,31},{8,0},{9,1... | collective-permute-start | bytes 1572872 | tf_op jit(solution)/shard_map/ppermute | solution.py:24
  27.9 8.6 %collective-permute-start.14 = (bf16[64,2048]{1,0:T(8,128)(2,1)S(1)}, bf16[64,2048]{1,0:T(8,128)(2,1)S(1)}, u32[]{:S(2)}, u32[]{:S(2)}) collective-permute-start(bf16[64,2048]{1,0:T(8,128)(2,1)S(1)} %constant_dynamic-update-slice_fusion.refs_1_), channel_id=1, source_target_pairs={{0,7},{1,0},{2,1},{3,2},{4,3},{5,4},{6,5},{7,6},{8,15},{9,8},{10,9... | collective-permute-start | bytes 786440 | tf_op jit(solution)/shard_map/ppermute | solution.py:19
  36.5 1.9 %collective-permute-start.11 = (bf16[64,2048]{1,0:T(8,128)(2,1)S(1)}, bf16[64,2048]{1,0:T(8,128)(2,1)S(1)}, u32[]{:S(2)}, u32[]{:S(2)}) collective-permute-start(bf16[64,2048]{1,0:T(8,128)(2,1)S(1)} %constant_dynamic-update-slice_fusion.refs_1_), channel_id=1, source_target_pairs={{0,1},{1,2},{2,3},{3,4},{4,5},{5,6},{6,7},{7,0},{8,9},{9,10},{10,1... | collective-permute-start | bytes 786440 | tf_op jit(solution)/shard_map/ppermute | solution.py:19
  38.4 5.1 %collective-permute-start.4 = (bf16[64,2048]{1,0:T(8,128)(2,1)S(1)}, bf16[64,2048]{1,0:T(8,128)(2,1)S(1)}, u32[]{:S(2)}, u32[]{:S(2)}) collective-permute-start(bf16[64,2048]{1,0:T(8,128)(2,1)S(1)} %pad_maximum_fusion.1.refs_0_), channel_id=1, source_target_pairs={{0,7},{1,0},{2,1},{3,2},{4,3},{5,4},{6,5},{7,6},{8,15},{9,8},{10,9... | collective-permute-start | bytes 786440 | tf_op jit(solution)/shard_map/ppermute | solution.py:19
  43.6 1.9 %collective-permute-start.2 = (bf16[64,2048]{1,0:T(8,128)(2,1)S(1)}, bf16[64,2048]{1,0:T(8,128)(2,1)S(1)}, u32[]{:S(2)}, u32[]{:S(2)}) collective-permute-start(bf16[64,2048]{1,0:T(8,128)(2,1)S(1)} %collective-permute-done.1.refs_2_), channel_id=1, source_target_pairs={{0,1},{1,2},{2,3},{3,4},{4,5},{5,6},{6,7},{7,0},{8,9},{9,10},{10,1... | collective-permute-start | bytes 786440 | tf_op jit(solution)/shard_map/ppermute | solution.py:19
  45.9 4.7 %collective-permute-start.15 = (bf16[64,2048]{1,0:T(8,128)(2,1)S(1)}, bf16[64,2048]{1,0:T(8,128)(2,1)S(1)}, u32[]{:S(2)}, u32[]{:S(2)}) collective-permute-start(bf16[64,2048]{1,0:T(8,128)(2,1)S(1)} %collective-permute-done.14.refs_5_), channel_id=1, source_target_pairs={{0,7},{1,0},{2,1},{3,2},{4,3},{5,4},{6,5},{7,6},{8,15},{9,8},{10,9... | collective-permute-start | bytes 786440 | tf_op jit(solution)/shard_map/ppermute | solution.py:19
  50.6 1.9 %collective-permute-start.12 = (bf16[64,2048]{1,0:T(8,128)(2,1)S(1)}, bf16[64,2048]{1,0:T(8,128)(2,1)S(1)}, u32[]{:S(2)}, u32[]{:S(2)}) collective-permute-start(bf16[64,2048]{1,0:T(8,128)(2,1)S(1)} %collective-permute-done.11.refs_4_), channel_id=1, source_target_pairs={{0,1},{1,2},{2,3},{3,4},{4,5},{5,6},{6,7},{7,0},{8,9},{9,10},{10,1... | collective-permute-start | bytes 786440 | tf_op jit(solution)/shard_map/ppermute | solution.py:19
  53.0 2.3 %collective-permute-start.3 = (bf16[64,2048]{1,0:T(8,128)(2,1)S(1)}, bf16[64,2048]{1,0:T(8,128)(2,1)S(1)}, u32[]{:S(2)}, u32[]{:S(2)}) collective-permute-start(bf16[64,2048]{1,0:T(8,128)(2,1)S(1)} %collective-permute-done.2.refs_6_), channel_id=1, source_target_pairs={{0,1},{1,2},{2,3},{3,4},{4,5},{5,6},{6,7},{7,0},{8,9},{9,10},{10,1... | collective-permute-start | bytes 786440 | tf_op jit(solution)/shard_map/ppermute | solution.py:19
  55.3 6.5 %collective-permute-start.16 = (bf16[64,2048]{1,0:T(8,128)(2,1)S(1)}, bf16[64,2048]{1,0:T(8,128)(2,1)S(1)}, u32[]{:S(2)}, u32[]{:S(2)}) collective-permute-start(bf16[64,2048]{1,0:T(8,128)(2,1)S(1)} %collective-permute-done.15.refs_9_), channel_id=1, source_target_pairs={{0,7},{1,0},{2,1},{3,2},{4,3},{5,4},{6,5},{7,6},{8,15},{9,8},{10,9... | collective-permute-start | bytes 786440 | tf_op jit(solution)/shard_map/ppermute | solution.py:19
  61.8 3.9 %collective-permute-start.7 = (bf16[64,2048]{1,0:T(8,128)(2,1)S(1)}, bf16[64,2048]{1,0:T(8,128)(2,1)S(1)}, u32[]{:S(2)}, u32[]{:S(2)}) collective-permute-start(bf16[64,2048]{1,0:T(8,128)(2,1)S(1)} %collective-permute-done.4.refs_3_), channel_id=1, source_target_pairs={{0,7},{1,0},{2,1},{3,2},{4,3},{5,4},{6,5},{7,6},{8,15},{9,8},{10,9... | collective-permute-start | bytes 786440 | tf_op jit(solution)/shard_map/ppermute | solution.py:19
  65.8 1.9 %collective-permute-start.13 = (bf16[64,2048]{1,0:T(8,128)(2,1)S(1)}, bf16[64,2048]{1,0:T(8,128)(2,1)S(1)}, u32[]{:S(2)}, u32[]{:S(2)}) collective-permute-start(bf16[64,2048]{1,0:T(8,128)(2,1)S(1)} %collective-permute-done.12.refs_8_), channel_id=1, source_target_pairs={{0,1},{1,2},{2,3},{3,4},{4,5},{5,6},{6,7},{7,0},{8,9},{9,10},{10,1... | collective-permute-start | bytes 786440 | tf_op jit(solution)/shard_map/ppermute | solution.py:19
  68.1 1.9 %collective-permute-start.17 = (bf16[64,2048]{1,0:T(8,128)(2,1)S(1)}, bf16[64,2048]{1,0:T(8,128)(2,1)S(1)}, u32[]{:S(2)}, u32[]{:S(2)}) collective-permute-start(bf16[64,2048]{1,0:T(8,128)(2,1)S(1)} %collective-permute-done.3.refs_0_), channel_id=1, source_target_pairs={{0,1},{1,2},{2,3},{3,4},{4,5},{5,6},{6,7},{7,0},{8,9},{9,10},{10,1... | collective-permute-start | bytes 786440 | tf_op jit(solution)/shard_map/ppermute | solution.py:19
  70.0 5.1 %collective-permute-start.18 = (bf16[64,2048]{1,0:T(8,128)(2,1)S(1)}, bf16[64,2048]{1,0:T(8,128)(2,1)S(1)}, u32[]{:S(2)}, u32[]{:S(2)}) collective-permute-start(bf16[64,2048]{1,0:T(8,128)(2,1)S(1)} %collective-permute-done.16.refs_3_), channel_id=1, source_target_pairs={{0,7},{1,0},{2,1},{3,2},{4,3},{5,4},{6,5},{7,6},{8,15},{9,8},{10,9... | collective-permute-start | bytes 786440 | tf_op jit(solution)/shard_map/ppermute | solution.py:19
  75.2 3.6 %collective-permute-start.8 = (bf16[64,2048]{1,0:T(8,128)(2,1)S(1)}, bf16[64,2048]{1,0:T(8,128)(2,1)S(1)}, u32[]{:S(2)}, u32[]{:S(2)}) collective-permute-start(bf16[64,2048]{1,0:T(8,128)(2,1)S(1)} %collective-permute-done.7.refs_7_), channel_id=1, source_target_pairs={{0,7},{1,0},{2,1},{3,2},{4,3},{5,4},{6,5},{7,6},{8,15},{9,8},{10,9... | collective-permute-start | bytes 786440 | tf_op jit(solution)/shard_map/ppermute | solution.py:19
  78.7 2.5 %shard_map.55.refs_8_ = f32[2,2,8,72,256]{4,3,2,1,0:T(8,128)S(1)} custom-call(bf16[64,2048]{1,0:T(8,128)(2,1)S(1)} %pad_maximum_fusion.1.refs_0_, bf16[64,2048]{1,0:T(8,128)(2,1)S(1)} %constant_dynamic-update-slice_fusion.refs_1_, bf16[64,2048]{1,0:T(8,128)(2,1)S(1)} %collective-permute-done.1.refs_2_, bf16[64,2048]{1,0:T(8,128)(2,1)S(1)} %collective-permute-done.4.refs_3_, ...), custom_call_target="tpu_custom_call" | custom-call | flops 1342177280 | bytes 4718592 | tf_op jit(solution)/shard_map/pallas_call | solution.py:97
  81.9 3.8 %collective-permute-done.8.refs_1_ = bf16[64,2048]{1,0:T(8,128)(2,1)S(1)} collective-permute-done((bf16[64,2048]{1,0:T(8,128)(2,1)S(1)}, bf16[64,2048]{1,0:T(8,128)(2,1)S(1)}, u32[]{:S(2)}, u32[]{:S(2)}) %collective-permute-start.8) | collective-permute-done | bytes 262176 | tf_op jit(solution)/shard_map/ppermute | solution.py:19
  85.7 1.5 %shard_map.56 = f32[2,2,8,72,256]{4,3,2,1,0:T(8,128)S(1)} custom-call(bf16[64,2048]{1,0:T(8,128)(2,1)S(1)} %collective-permute-done.3.refs_0_, bf16[64,2048]{1,0:T(8,128)(2,1)S(1)} %collective-permute-done.8.refs_1_, bf16[64,2048]{1,0:T(8,128)(2,1)S(1)} %collective-permute-done.13.refs_2_, ...), custom_call_target="tpu_custom_call", output_to_operand_aliasing={{}: (8, {})} | custom-call | flops 805306368 | bytes 3670016 | tf_op jit(solution)/shard_map/pallas_call | solution.py:97
  87.3 1.9 %collective-permute-start.19 = (f32[2,8,72,256]{3,2,1,0:T(8,128)S(1)}, f32[2,8,72,256]{3,2,1,0:T(8,128)S(1)}, u32[]{:S(2)}, u32[]{:S(2)}) collective-permute-start(f32[2,8,72,256]{3,2,1,0:T(8,128)S(1)} %slice_bitcast_fusion), channel_id=1, source_target_pairs={{0,32},{32,0},{64,96},{96,64},{128,160},{160,128},{192,224},{224,1... | collective-permute-start | bytes 3538952 | tf_op jit(solution)/shard_map/ppermute | solution.py:184
  89.3 2.8 %collective-permute-done.19 = f32[2,8,72,256]{3,2,1,0:T(8,128)S(1)} collective-permute-done((f32[2,8,72,256]{3,2,1,0:T(8,128)S(1)}, f32[2,8,72,256]{3,2,1,0:T(8,128)S(1)}, u32[]{:S(2)}, u32[]{:S(2)}) %collective-permute-start.19) | collective-permute-done | bytes 1179680 | tf_op jit(solution)/shard_map/ppermute | solution.py:184
  93.0 15.6 %all_to_all.10.parts_ref = f32[8,72,256]{2,1,0:T(8,128)S(1)} all-to-all(f32[8,72,256]{2,1,0:T(8,128)S(1)} %get-tuple-element.15), channel_id=1, replica_groups={{0,64,128,192,256,320,384,448},{32,96,160,224,288,352,416,480},{1,65,12..., dimensions={0} | all-to-all | bytes 1179648 | tf_op jit(solution)/shard_map/all_to_all | solution.py:189
  108.6 4.7 %all-to-all-start = ((f32[8,72,256]{2,1,0:T(8,128)}), f32[8,72,256]{2,1,0:T(8,128)S(1)}, u32[]{:S(2)}, u32[]{:S(2)}) async-start(f32[8,72,256]{2,1,0:T(8,128)} %get-tuple-element.16), calls=%async_computation | async-start | bytes 1179648 | tf_op jit(solution)/shard_map/all_to_all | solution.py:190
  113.4 3.4 %collective-permute-start.20 = (f32[72,128]{1,0:T(8,128)S(1)}, f32[72,128]{1,0:T(8,128)S(1)}, u32[]{:S(2)}, u32[]{:S(2)}) collective-permute-start(f32[72,128]{1,0:T(8,128)S(1)} %get-tuple-element.13), channel_id=1, source_target_pairs={{0,8},{1,9},{2,10},{3,11},{4,12},{5,13},{6,14},{7,15},{8,16},{9,17... | collective-permute-start | bytes 110600 | tf_op jit(solution)/shard_map/ppermute | solution.py:24
  116.8 3.3 %collective-permute-start.21 = (f32[72,128]{1,0:T(8,128)S(1)}, f32[72,128]{1,0:T(8,128)S(1)}, u32[]{:S(2)}, u32[]{:S(2)}) collective-permute-start(f32[72,128]{1,0:T(8,128)S(1)} %get-tuple-element.14), channel_id=1, source_target_pairs={{0,24},{1,25},{2,26},{3,27},{4,28},{5,29},{6,30},{7,31},{8,0},{9,1... | collective-permute-start | bytes 110600 | tf_op jit(solution)/shard_map/ppermute | solution.py:24
  120.2 2.6 %all-to-all-done.parts_ref = f32[8,72,256]{2,1,0:T(8,128)S(1)} async-done(((f32[8,72,256]{2,1,0:T(8,128)}), f32[8,72,256]{2,1,0:T(8,128)S(1)}, u32[]{:S(2)}, u32[]{:S(2)}) %all-to-all-start) | async-done | bytes 589856 | tf_op jit(solution)/shard_map/all_to_all | solution.py:190
  122.7 2.0 %collective-permute-done.21.high_ref = f32[72,128]{1,0:T(8,128)S(1)} collective-permute-done((f32[72,128]{1,0:T(8,128)S(1)}, f32[72,128]{1,0:T(8,128)S(1)}, u32[]{:S(2)}, u32[]{:S(2)}) %collective-permute-start.21) | collective-permute-done | bytes 36896 | tf_op jit(solution)/shard_map/ppermute | solution.py:24
  124.8 1.4 %shard_map.58 = f32[64,256]{1,0:T(8,128)} custom-call(f32[8,72,256]{2,1,0:T(8,128)S(1)} %all-to-all-done.parts_ref, f32[72,128]{1,0:T(8,128)S(1)} %collective-permute-done.20.low_ref, f32[72,128]{1,0:T(8,128)S(1)} %collective-permute-done.21.high_ref, s32[1,2]{1,0:T(1,128)S(1)} %copy-done, s32[1,2]{1,0:T(1,128)S(1)} %copy-done.1, f32[8]{0:T(128)S(1)} %copy-done.2), custom_call_target="tpu_custom_call" | custom-call | tf_op jit(solution)/shard_map/pallas_call | solution.py:201
  (34 shorter events, 4.2 us)
Async XLA Ops:
  1.0 26.8 %collective-permute-start.9 = (bf16[32,2048]{1,0:T(8,128)(2,1)S(1)}, bf16[32,2048]{1,0:T(8,128)(2,1)S(1)}, u32[]{:S(2)}, u32[]{:S(2)}) collective-permute-start(bf16[32,2048]{1,0:T(8,128)(2,1)S(1)} %get-tuple-element.22), channel_id=1, source_target_pairs={{0,24},{1,25},{2,26},{3,27},{4,28},{5,29},{6,30},{7,31},{8,0},{9,1... | collective-permute-start | bytes 393224 | tf_op jit(solution)/shard_map/ppermute | solution.py:24
  5.0 10.3 %collective-permute-start = (bf16[32,2048]{1,0:T(8,128)(2,1)S(1)}, bf16[32,2048]{1,0:T(8,128)(2,1)S(1)}, u32[]{:S(2)}, u32[]{:S(2)}) collective-permute-start(bf16[32,2048]{1,0:T(8,128)(2,1)S(1)} %get-tuple-element.22), channel_id=1, source_target_pairs={{0,8},{1,9},{2,10},{3,11},{4,12},{5,13},{6,14},{7,15},{8,16},{9,17... | collective-permute-start | bytes 393224 | tf_op jit(solution)/shard_map/ppermute | solution.py:24
  9.0 18.9 %collective-permute-start.10 = (bf16[32,2048]{1,0:T(8,128)(2,1)S(1)}, bf16[32,2048]{1,0:T(8,128)(2,1)S(1)}, u32[]{:S(2)}, u32[]{:S(2)}) collective-permute-start(bf16[32,2048]{1,0:T(8,128)(2,1)S(1)} %get-tuple-element.21), channel_id=1, source_target_pairs={{0,16},{1,17},{2,18},{3,19},{4,20},{5,21},{6,22},{7,23},{8,24},{9,... | collective-permute-start | bytes 393224 | tf_op jit(solution)/shard_map/ppermute | solution.py:24
  15.4 23.0 %collective-permute-start.1 = (bf16[64,2048]{1,0:T(8,128)(2,1)S(1)}, bf16[64,2048]{1,0:T(8,128)(2,1)S(1)}, u32[]{:S(2)}, u32[]{:S(2)}) collective-permute-start(bf16[64,2048]{1,0:T(8,128)(2,1)S(1)} %pad_maximum_fusion.1.refs_0_), channel_id=1, source_target_pairs={{0,1},{1,2},{2,3},{3,4},{4,5},{5,6},{6,7},{7,0},{8,9},{9,10},{10,1... | collective-permute-start | bytes 786440 | tf_op jit(solution)/shard_map/ppermute | solution.py:19
  20.9 29.7 %collective-permute-start.5 = (bf16[2048,128]{1,0:T(8,128)(2,1)S(1)}, bf16[2048,128]{1,0:T(8,128)(2,1)S(1)}, u32[]{:S(2)}, u32[]{:S(2)}) collective-permute-start(bf16[2048,128]{1,0:T(8,128)(2,1)S(1)} %get-tuple-element.19), channel_id=1, source_target_pairs={{0,8},{1,9},{2,10},{3,11},{4,12},{5,13},{6,14},{7,15},{8,16},{9,17... | collective-permute-start | bytes 1572872 | tf_op jit(solution)/shard_map/ppermute | solution.py:24
  25.9 26.7 %collective-permute-start.6 = (bf16[2048,128]{1,0:T(8,128)(2,1)S(1)}, bf16[2048,128]{1,0:T(8,128)(2,1)S(1)}, u32[]{:S(2)}, u32[]{:S(2)}) collective-permute-start(bf16[2048,128]{1,0:T(8,128)(2,1)S(1)} %get-tuple-element.20), channel_id=1, source_target_pairs={{0,24},{1,25},{2,26},{3,27},{4,28},{5,29},{6,30},{7,31},{8,0},{9,1... | collective-permute-start | bytes 1572872 | tf_op jit(solution)/shard_map/ppermute | solution.py:24
  27.9 15.7 %collective-permute-start.14 = (bf16[64,2048]{1,0:T(8,128)(2,1)S(1)}, bf16[64,2048]{1,0:T(8,128)(2,1)S(1)}, u32[]{:S(2)}, u32[]{:S(2)}) collective-permute-start(bf16[64,2048]{1,0:T(8,128)(2,1)S(1)} %constant_dynamic-update-slice_fusion.refs_1_), channel_id=1, source_target_pairs={{0,7},{1,0},{2,1},{3,2},{4,3},{5,4},{6,5},{7,6},{8,15},{9,8},{10,9... | collective-permute-start | bytes 786440 | tf_op jit(solution)/shard_map/ppermute | solution.py:19
  36.5 9.5 %collective-permute-start.11 = (bf16[64,2048]{1,0:T(8,128)(2,1)S(1)}, bf16[64,2048]{1,0:T(8,128)(2,1)S(1)}, u32[]{:S(2)}, u32[]{:S(2)}) collective-permute-start(bf16[64,2048]{1,0:T(8,128)(2,1)S(1)} %constant_dynamic-update-slice_fusion.refs_1_), channel_id=1, source_target_pairs={{0,1},{1,2},{2,3},{3,4},{4,5},{5,6},{6,7},{7,0},{8,9},{9,10},{10,1... | collective-permute-start | bytes 786440 | tf_op jit(solution)/shard_map/ppermute | solution.py:19
  38.4 14.3 %collective-permute-start.4 = (bf16[64,2048]{1,0:T(8,128)(2,1)S(1)}, bf16[64,2048]{1,0:T(8,128)(2,1)S(1)}, u32[]{:S(2)}, u32[]{:S(2)}) collective-permute-start(bf16[64,2048]{1,0:T(8,128)(2,1)S(1)} %pad_maximum_fusion.1.refs_0_), channel_id=1, source_target_pairs={{0,7},{1,0},{2,1},{3,2},{4,3},{5,4},{6,5},{7,6},{8,15},{9,8},{10,9... | collective-permute-start | bytes 786440 | tf_op jit(solution)/shard_map/ppermute | solution.py:19
  43.6 9.5 %collective-permute-start.2 = (bf16[64,2048]{1,0:T(8,128)(2,1)S(1)}, bf16[64,2048]{1,0:T(8,128)(2,1)S(1)}, u32[]{:S(2)}, u32[]{:S(2)}) collective-permute-start(bf16[64,2048]{1,0:T(8,128)(2,1)S(1)} %collective-permute-done.1.refs_2_), channel_id=1, source_target_pairs={{0,1},{1,2},{2,3},{3,4},{4,5},{5,6},{6,7},{7,0},{8,9},{9,10},{10,1... | collective-permute-start | bytes 786440 | tf_op jit(solution)/shard_map/ppermute | solution.py:19
  45.9 9.4 %collective-permute-start.15 = (bf16[64,2048]{1,0:T(8,128)(2,1)S(1)}, bf16[64,2048]{1,0:T(8,128)(2,1)S(1)}, u32[]{:S(2)}, u32[]{:S(2)}) collective-permute-start(bf16[64,2048]{1,0:T(8,128)(2,1)S(1)} %collective-permute-done.14.refs_5_), channel_id=1, source_target_pairs={{0,7},{1,0},{2,1},{3,2},{4,3},{5,4},{6,5},{7,6},{8,15},{9,8},{10,9... | collective-permute-start | bytes 786440 | tf_op jit(solution)/shard_map/ppermute | solution.py:19
  50.6 15.1 %collective-permute-start.12 = (bf16[64,2048]{1,0:T(8,128)(2,1)S(1)}, bf16[64,2048]{1,0:T(8,128)(2,1)S(1)}, u32[]{:S(2)}, u32[]{:S(2)}) collective-permute-start(bf16[64,2048]{1,0:T(8,128)(2,1)S(1)} %collective-permute-done.11.refs_4_), channel_id=1, source_target_pairs={{0,1},{1,2},{2,3},{3,4},{4,5},{5,6},{6,7},{7,0},{8,9},{9,10},{10,1... | collective-permute-start | bytes 786440 | tf_op jit(solution)/shard_map/ppermute | solution.py:19
  53.0 15.1 %collective-permute-start.3 = (bf16[64,2048]{1,0:T(8,128)(2,1)S(1)}, bf16[64,2048]{1,0:T(8,128)(2,1)S(1)}, u32[]{:S(2)}, u32[]{:S(2)}) collective-permute-start(bf16[64,2048]{1,0:T(8,128)(2,1)S(1)} %collective-permute-done.2.refs_6_), channel_id=1, source_target_pairs={{0,1},{1,2},{2,3},{3,4},{4,5},{5,6},{6,7},{7,0},{8,9},{9,10},{10,1... | collective-permute-start | bytes 786440 | tf_op jit(solution)/shard_map/ppermute | solution.py:19
  55.3 14.7 %collective-permute-start.16 = (bf16[64,2048]{1,0:T(8,128)(2,1)S(1)}, bf16[64,2048]{1,0:T(8,128)(2,1)S(1)}, u32[]{:S(2)}, u32[]{:S(2)}) collective-permute-start(bf16[64,2048]{1,0:T(8,128)(2,1)S(1)} %collective-permute-done.15.refs_9_), channel_id=1, source_target_pairs={{0,7},{1,0},{2,1},{3,2},{4,3},{5,4},{6,5},{7,6},{8,15},{9,8},{10,9... | collective-permute-start | bytes 786440 | tf_op jit(solution)/shard_map/ppermute | solution.py:19
  61.8 13.3 %collective-permute-start.7 = (bf16[64,2048]{1,0:T(8,128)(2,1)S(1)}, bf16[64,2048]{1,0:T(8,128)(2,1)S(1)}, u32[]{:S(2)}, u32[]{:S(2)}) collective-permute-start(bf16[64,2048]{1,0:T(8,128)(2,1)S(1)} %collective-permute-done.4.refs_3_), channel_id=1, source_target_pairs={{0,7},{1,0},{2,1},{3,2},{4,3},{5,4},{6,5},{7,6},{8,15},{9,8},{10,9... | collective-permute-start | bytes 786440 | tf_op jit(solution)/shard_map/ppermute | solution.py:19
  65.8 15.5 %collective-permute-start.13 = (bf16[64,2048]{1,0:T(8,128)(2,1)S(1)}, bf16[64,2048]{1,0:T(8,128)(2,1)S(1)}, u32[]{:S(2)}, u32[]{:S(2)}) collective-permute-start(bf16[64,2048]{1,0:T(8,128)(2,1)S(1)} %collective-permute-done.12.refs_8_), channel_id=1, source_target_pairs={{0,1},{1,2},{2,3},{3,4},{4,5},{5,6},{6,7},{7,0},{8,9},{9,10},{10,1... | collective-permute-start | bytes 786440 | tf_op jit(solution)/shard_map/ppermute | solution.py:19
  68.1 13.6 %collective-permute-start.17 = (bf16[64,2048]{1,0:T(8,128)(2,1)S(1)}, bf16[64,2048]{1,0:T(8,128)(2,1)S(1)}, u32[]{:S(2)}, u32[]{:S(2)}) collective-permute-start(bf16[64,2048]{1,0:T(8,128)(2,1)S(1)} %collective-permute-done.3.refs_0_), channel_id=1, source_target_pairs={{0,1},{1,2},{2,3},{3,4},{4,5},{5,6},{6,7},{7,0},{8,9},{9,10},{10,1... | collective-permute-start | bytes 786440 | tf_op jit(solution)/shard_map/ppermute | solution.py:19
  70.0 11.9 %collective-permute-start.18 = (bf16[64,2048]{1,0:T(8,128)(2,1)S(1)}, bf16[64,2048]{1,0:T(8,128)(2,1)S(1)}, u32[]{:S(2)}, u32[]{:S(2)}) collective-permute-start(bf16[64,2048]{1,0:T(8,128)(2,1)S(1)} %collective-permute-done.16.refs_3_), channel_id=1, source_target_pairs={{0,7},{1,0},{2,1},{3,2},{4,3},{5,4},{6,5},{7,6},{8,15},{9,8},{10,9... | collective-permute-start | bytes 786440 | tf_op jit(solution)/shard_map/ppermute | solution.py:19
  75.2 10.5 %collective-permute-start.8 = (bf16[64,2048]{1,0:T(8,128)(2,1)S(1)}, bf16[64,2048]{1,0:T(8,128)(2,1)S(1)}, u32[]{:S(2)}, u32[]{:S(2)}) collective-permute-start(bf16[64,2048]{1,0:T(8,128)(2,1)S(1)} %collective-permute-done.7.refs_7_), channel_id=1, source_target_pairs={{0,7},{1,0},{2,1},{3,2},{4,3},{5,4},{6,5},{7,6},{8,15},{9,8},{10,9... | collective-permute-start | bytes 786440 | tf_op jit(solution)/shard_map/ppermute | solution.py:19
  87.3 4.7 %collective-permute-start.19 = (f32[2,8,72,256]{3,2,1,0:T(8,128)S(1)}, f32[2,8,72,256]{3,2,1,0:T(8,128)S(1)}, u32[]{:S(2)}, u32[]{:S(2)}) collective-permute-start(f32[2,8,72,256]{3,2,1,0:T(8,128)S(1)} %slice_bitcast_fusion), channel_id=1, source_target_pairs={{0,32},{32,0},{64,96},{96,64},{128,160},{160,128},{192,224},{224,1... | collective-permute-start | bytes 3538952 | tf_op jit(solution)/shard_map/ppermute | solution.py:184
  93.0 31.8 %copy-start = (s32[1,2]{1,0:T(1,128)S(1)}, s32[1,2]{1,0:T(1,128)}, u32[]{:S(2)}) copy-start(s32[1,2]{1,0:T(1,128)} %cutoff_ref.1) | copy-start | bytes 28
  93.0 31.8 %copy-start.1 = (s32[1,2]{1,0:T(1,128)S(1)}, s32[1,2]{1,0:T(1,128)}, u32[]{:S(2)}) copy-start(s32[1,2]{1,0:T(1,128)} %index_ref.1) | copy-start | bytes 28
  93.0 31.8 %copy-start.2 = (f32[8]{0:T(128)S(1)}, f32[8]{0:T(128)}, u32[]{:S(2)}) copy-start(f32[8]{0:T(128)} %table_ref.1) | copy-start | bytes 100
  108.6 14.1 %all-to-all-start = ((f32[8,72,256]{2,1,0:T(8,128)}), f32[8,72,256]{2,1,0:T(8,128)S(1)}, u32[]{:S(2)}, u32[]{:S(2)}) async-start(f32[8,72,256]{2,1,0:T(8,128)} %get-tuple-element.16), calls=%async_computation | async-start | bytes 1179648 | tf_op jit(solution)/shard_map/all_to_all | solution.py:190
  113.4 9.3 %collective-permute-start.20 = (f32[72,128]{1,0:T(8,128)S(1)}, f32[72,128]{1,0:T(8,128)S(1)}, u32[]{:S(2)}, u32[]{:S(2)}) collective-permute-start(f32[72,128]{1,0:T(8,128)S(1)} %get-tuple-element.13), channel_id=1, source_target_pairs={{0,8},{1,9},{2,10},{3,11},{4,12},{5,13},{6,14},{7,15},{8,16},{9,17... | collective-permute-start | bytes 110600 | tf_op jit(solution)/shard_map/ppermute | solution.py:24
  116.8 8.0 %collective-permute-start.21 = (f32[72,128]{1,0:T(8,128)S(1)}, f32[72,128]{1,0:T(8,128)S(1)}, u32[]{:S(2)}, u32[]{:S(2)}) collective-permute-start(f32[72,128]{1,0:T(8,128)S(1)} %get-tuple-element.14), channel_id=1, source_target_pairs={{0,24},{1,25},{2,26},{3,27},{4,28},{5,29},{6,30},{7,31},{8,0},{9,1... | collective-permute-start | bytes 110600 | tf_op jit(solution)/shard_map/ppermute | solution.py:24

commit v7 on v6

--- a/solution.py
+++ b/solution.py
@@ -181,13 +181,17 @@
     sums_shape = (2, 2, n_mem // 2, own_rows + EXTRA, cols)
     parts = cross(early, near, side, sums_shape)
     parts = cross(late, near, side, sums_shape, parts)
-    received = lax.ppermute(parts[1], "mem", [(m, m ^ 1) for m in range(n_mem)])
+    def from_other_core(x):
+        return lax.ppermute(x, "mem", [(m, m ^ 1) for m in range(n_mem)])
+
+    side_received = from_other_core(parts[1, 1])
+    near_received = from_other_core(parts[1, 0])
     groups = [list(range(c, n_mem, 2)) for c in range(2)]
     exchange = functools.partial(
         lax.all_to_all, axis_name="mem", split_axis=0, concat_axis=0, axis_index_groups=groups, tiled=True
     )
-    side_parts = exchange(parts[0, 1] + received[1])
-    near_parts = exchange(parts[0, 0] + received[0])
+    side_parts = exchange(parts[0, 1] + side_received)
+    near_parts = exchange(parts[0, 0] + near_received)
     vmem, smem = pl.BlockSpec(memory_space=pltpu.VMEM), pl.BlockSpec(memory_space=pltpu.SMEM)
     compiler_params = pltpu.CompilerParams(vmem_limit_bytes=16 * 1024 * 1024)
     to_left, to_right = pl.pallas_call(

time: 127 us -> 129 us (1.016)
  starting transfers between devices: 87.7 us -> 90.2 us
    ppermute x1 -> x2, starting transfers between devices: 1.92 us -> 4.33 us  [from_other_core(): return lax.ppermute(x, 'mem', [(m, m ^ 1) for m in range(n_mem)])]
    ppermute x1 -> x2, waiting for transfers between devices: 2.81 us -> 1.6 us  [from_other_core(): return lax.ppermute(x, 'mem', [(m, m ^ 1) for m in range(n_mem)])]
  transfers between devices with their start and end apart: 23 -> 24, of which waited for: 9 -> 9; matrix products, arithmetic and copies ran while one was open for 2% -> 1% of each run, Pallas kernels for 2% -> 2%
where the time goes in v7:
time: 129 us; the launch traced here: 128 us
  starting transfers between devices  90.2 us (70%)
  blocking collectives  15.8 us (12%)
  waiting for transfers between devices  11.9 us (9%)
  Pallas kernels  5.44 us (4%)
  local copies, waits for them, and re-layouts  2.86 us (2%)
    ppermute x14, starting transfers between devices, z_shift(): return lax.ppermute(x, 'ocn', perm)  54.8 us
    ppermute x7, starting transfers between devices, y_shift(): return lax.ppermute(x, 'ocn', perm)  26.3 us
    all_to_all x1, blocking collectives, per_device(): side_parts = exchange(parts[0, 1] + side_received)  15.8 us
    ppermute x14, waiting for transfers between devices, z_shift(): return lax.ppermute(x, 'ocn', perm)  5.62 us
    all_to_all x1, starting transfers between devices, per_device(): near_parts = exchange(parts[0, 0] + near_received)  4.72 us
    ppermute x2, starting transfers between devices, from_other_core(): return lax.ppermute(x, 'mem', [(m, m ^ 1) for m in range(n_mem)])  4.33 us
    pallas_call x2, Pallas kernels, cross(): pl.pallas_call(functools.partial(cross_kernel, groups, before is None), o...  4.02 us
    all_to_all x1, waiting for transfers between devices, per_device(): near_parts = exchange(parts[0, 0] + near_received)  2.78 us
  transfers between devices with their start and end apart: 24, of which 9 were waited for; matrix products, arithmetic and copies ran while one was open for 1% of the time, Pallas kernels for 2%

profile of v7, /device:TPU:56, one launch (start us, length us, event | category | flops | bytes accessed | tf_op | source)
XLA Modules:
  0.0 127.6 jit_solution(14052571761748928395)
XLA Ops:
  1.0 4.0 %collective-permute-start.9 = (bf16[32,2048]{1,0:T(8,128)(2,1)S(1)}, bf16[32,2048]{1,0:T(8,128)(2,1)S(1)}, u32[]{:S(2)}, u32[]{:S(2)}) collective-permute-start(bf16[32,2048]{1,0:T(8,128)(2,1)S(1)} %get-tuple-element.24), channel_id=1, source_target_pairs={{0,24},{1,25},{2,26},{3,27},{4,28},{5,29},{6,30},{7,31},{8,0},{9,1... | collective-permute-start | bytes 393224 | tf_op jit(solution)/shard_map/ppermute | solution.py:24
  5.0 3.9 %collective-permute-start = (bf16[32,2048]{1,0:T(8,128)(2,1)S(1)}, bf16[32,2048]{1,0:T(8,128)(2,1)S(1)}, u32[]{:S(2)}, u32[]{:S(2)}) collective-permute-start(bf16[32,2048]{1,0:T(8,128)(2,1)S(1)} %get-tuple-element.24), channel_id=1, source_target_pairs={{0,8},{1,9},{2,10},{3,11},{4,12},{5,13},{6,14},{7,15},{8,16},{9,17... | collective-permute-start | bytes 393224 | tf_op jit(solution)/shard_map/ppermute | solution.py:24
  9.0 4.7 %collective-permute-start.10 = (bf16[32,2048]{1,0:T(8,128)(2,1)S(1)}, bf16[32,2048]{1,0:T(8,128)(2,1)S(1)}, u32[]{:S(2)}, u32[]{:S(2)}) collective-permute-start(bf16[32,2048]{1,0:T(8,128)(2,1)S(1)} %get-tuple-element.23), channel_id=1, source_target_pairs={{0,16},{1,17},{2,18},{3,19},{4,20},{5,21},{6,22},{7,23},{8,24},{9,... | collective-permute-start | bytes 393224 | tf_op jit(solution)/shard_map/ppermute | solution.py:24
  13.7 1.7 %constant_dynamic-slice_fusion = (bf16[2048,256]{1,0:T(8,128)(2,1)S(1)}, bf16[2048,256]{1,0:T(8,128)(2,1)S(1)}) fusion(bf16[4096,256]{1,0:T(8,128)(2,1)} %param.6, s32[]{:T(128)S(6)} %select_n.14, s32[]{:T(128)S(6)} %select_n.15), kind=kLoop, calls=%fused_computation.12 | loop fusion | bytes 4194312 | tf_op jit(solution)/shard_map/dynamic_slice | solution.py:155
  15.4 5.4 %collective-permute-start.1 = (bf16[64,2048]{1,0:T(8,128)(2,1)S(1)}, bf16[64,2048]{1,0:T(8,128)(2,1)S(1)}, u32[]{:S(2)}, u32[]{:S(2)}) collective-permute-start(bf16[64,2048]{1,0:T(8,128)(2,1)S(1)} %pad_maximum_fusion.1.refs_0_), channel_id=1, source_target_pairs={{0,1},{1,2},{2,3},{3,4},{4,5},{5,6},{6,7},{7,0},{8,9},{9,10},{10,1... | collective-permute-start | bytes 786440 | tf_op jit(solution)/shard_map/ppermute | solution.py:19
  20.9 5.0 %collective-permute-start.5 = (bf16[2048,128]{1,0:T(8,128)(2,1)S(1)}, bf16[2048,128]{1,0:T(8,128)(2,1)S(1)}, u32[]{:S(2)}, u32[]{:S(2)}) collective-permute-start(bf16[2048,128]{1,0:T(8,128)(2,1)S(1)} %get-tuple-element.21), channel_id=1, source_target_pairs={{0,8},{1,9},{2,10},{3,11},{4,12},{5,13},{6,14},{7,15},{8,16},{9,17... | collective-permute-start | bytes 1572872 | tf_op jit(solution)/shard_map/ppermute | solution.py:24
  25.9 1.9 %collective-permute-start.6 = (bf16[2048,128]{1,0:T(8,128)(2,1)S(1)}, bf16[2048,128]{1,0:T(8,128)(2,1)S(1)}, u32[]{:S(2)}, u32[]{:S(2)}) collective-permute-start(bf16[2048,128]{1,0:T(8,128)(2,1)S(1)} %get-tuple-element.22), channel_id=1, source_target_pairs={{0,24},{1,25},{2,26},{3,27},{4,28},{5,29},{6,30},{7,31},{8,0},{9,1... | collective-permute-start | bytes 1572872 | tf_op jit(solution)/shard_map/ppermute | solution.py:24
  27.9 8.6 %collective-permute-start.14 = (bf16[64,2048]{1,0:T(8,128)(2,1)S(1)}, bf16[64,2048]{1,0:T(8,128)(2,1)S(1)}, u32[]{:S(2)}, u32[]{:S(2)}) collective-permute-start(bf16[64,2048]{1,0:T(8,128)(2,1)S(1)} %constant_dynamic-update-slice_fusion.refs_1_), channel_id=1, source_target_pairs={{0,7},{1,0},{2,1},{3,2},{4,3},{5,4},{6,5},{7,6},{8,15},{9,8},{10,9... | collective-permute-start | bytes 786440 | tf_op jit(solution)/shard_map/ppermute | solution.py:19
  36.5 1.9 %collective-permute-start.11 = (bf16[64,2048]{1,0:T(8,128)(2,1)S(1)}, bf16[64,2048]{1,0:T(8,128)(2,1)S(1)}, u32[]{:S(2)}, u32[]{:S(2)}) collective-permute-start(bf16[64,2048]{1,0:T(8,128)(2,1)S(1)} %constant_dynamic-update-slice_fusion.refs_1_), channel_id=1, source_target_pairs={{0,1},{1,2},{2,3},{3,4},{4,5},{5,6},{6,7},{7,0},{8,9},{9,10},{10,1... | collective-permute-start | bytes 786440 | tf_op jit(solution)/shard_map/ppermute | solution.py:19
  38.4 5.1 %collective-permute-start.4 = (bf16[64,2048]{1,0:T(8,128)(2,1)S(1)}, bf16[64,2048]{1,0:T(8,128)(2,1)S(1)}, u32[]{:S(2)}, u32[]{:S(2)}) collective-permute-start(bf16[64,2048]{1,0:T(8,128)(2,1)S(1)} %pad_maximum_fusion.1.refs_0_), channel_id=1, source_target_pairs={{0,7},{1,0},{2,1},{3,2},{4,3},{5,4},{6,5},{7,6},{8,15},{9,8},{10,9... | collective-permute-start | bytes 786440 | tf_op jit(solution)/shard_map/ppermute | solution.py:19
  43.6 1.9 %collective-permute-start.2 = (bf16[64,2048]{1,0:T(8,128)(2,1)S(1)}, bf16[64,2048]{1,0:T(8,128)(2,1)S(1)}, u32[]{:S(2)}, u32[]{:S(2)}) collective-permute-start(bf16[64,2048]{1,0:T(8,128)(2,1)S(1)} %collective-permute-done.1.refs_2_), channel_id=1, source_target_pairs={{0,1},{1,2},{2,3},{3,4},{4,5},{5,6},{6,7},{7,0},{8,9},{9,10},{10,1... | collective-permute-start | bytes 786440 | tf_op jit(solution)/shard_map/ppermute | solution.py:19
  45.9 4.7 %collective-permute-start.15 = (bf16[64,2048]{1,0:T(8,128)(2,1)S(1)}, bf16[64,2048]{1,0:T(8,128)(2,1)S(1)}, u32[]{:S(2)}, u32[]{:S(2)}) collective-permute-start(bf16[64,2048]{1,0:T(8,128)(2,1)S(1)} %collective-permute-done.14.refs_5_), channel_id=1, source_target_pairs={{0,7},{1,0},{2,1},{3,2},{4,3},{5,4},{6,5},{7,6},{8,15},{9,8},{10,9... | collective-permute-start | bytes 786440 | tf_op jit(solution)/shard_map/ppermute | solution.py:19
  50.6 1.9 %collective-permute-start.12 = (bf16[64,2048]{1,0:T(8,128)(2,1)S(1)}, bf16[64,2048]{1,0:T(8,128)(2,1)S(1)}, u32[]{:S(2)}, u32[]{:S(2)}) collective-permute-start(bf16[64,2048]{1,0:T(8,128)(2,1)S(1)} %collective-permute-done.11.refs_4_), channel_id=1, source_target_pairs={{0,1},{1,2},{2,3},{3,4},{4,5},{5,6},{6,7},{7,0},{8,9},{9,10},{10,1... | collective-permute-start | bytes 786440 | tf_op jit(solution)/shard_map/ppermute | solution.py:19
  53.0 2.3 %collective-permute-start.3 = (bf16[64,2048]{1,0:T(8,128)(2,1)S(1)}, bf16[64,2048]{1,0:T(8,128)(2,1)S(1)}, u32[]{:S(2)}, u32[]{:S(2)}) collective-permute-start(bf16[64,2048]{1,0:T(8,128)(2,1)S(1)} %collective-permute-done.2.refs_6_), channel_id=1, source_target_pairs={{0,1},{1,2},{2,3},{3,4},{4,5},{5,6},{6,7},{7,0},{8,9},{9,10},{10,1... | collective-permute-start | bytes 786440 | tf_op jit(solution)/shard_map/ppermute | solution.py:19
  55.3 6.5 %collective-permute-start.16 = (bf16[64,2048]{1,0:T(8,128)(2,1)S(1)}, bf16[64,2048]{1,0:T(8,128)(2,1)S(1)}, u32[]{:S(2)}, u32[]{:S(2)}) collective-permute-start(bf16[64,2048]{1,0:T(8,128)(2,1)S(1)} %collective-permute-done.15.refs_9_), channel_id=1, source_target_pairs={{0,7},{1,0},{2,1},{3,2},{4,3},{5,4},{6,5},{7,6},{8,15},{9,8},{10,9... | collective-permute-start | bytes 786440 | tf_op jit(solution)/shard_map/ppermute | solution.py:19
  61.8 3.9 %collective-permute-start.7 = (bf16[64,2048]{1,0:T(8,128)(2,1)S(1)}, bf16[64,2048]{1,0:T(8,128)(2,1)S(1)}, u32[]{:S(2)}, u32[]{:S(2)}) collective-permute-start(bf16[64,2048]{1,0:T(8,128)(2,1)S(1)} %collective-permute-done.4.refs_3_), channel_id=1, source_target_pairs={{0,7},{1,0},{2,1},{3,2},{4,3},{5,4},{6,5},{7,6},{8,15},{9,8},{10,9... | collective-permute-start | bytes 786440 | tf_op jit(solution)/shard_map/ppermute | solution.py:19
  65.8 1.9 %collective-permute-start.13 = (bf16[64,2048]{1,0:T(8,128)(2,1)S(1)}, bf16[64,2048]{1,0:T(8,128)(2,1)S(1)}, u32[]{:S(2)}, u32[]{:S(2)}) collective-permute-start(bf16[64,2048]{1,0:T(8,128)(2,1)S(1)} %collective-permute-done.12.refs_8_), channel_id=1, source_target_pairs={{0,1},{1,2},{2,3},{3,4},{4,5},{5,6},{6,7},{7,0},{8,9},{9,10},{10,1... | collective-permute-start | bytes 786440 | tf_op jit(solution)/shard_map/ppermute | solution.py:19
  68.1 1.9 %collective-permute-start.17 = (bf16[64,2048]{1,0:T(8,128)(2,1)S(1)}, bf16[64,2048]{1,0:T(8,128)(2,1)S(1)}, u32[]{:S(2)}, u32[]{:S(2)}) collective-permute-start(bf16[64,2048]{1,0:T(8,128)(2,1)S(1)} %collective-permute-done.3.refs_0_), channel_id=1, source_target_pairs={{0,1},{1,2},{2,3},{3,4},{4,5},{5,6},{6,7},{7,0},{8,9},{9,10},{10,1... | collective-permute-start | bytes 786440 | tf_op jit(solution)/shard_map/ppermute | solution.py:19
  70.0 5.1 %collective-permute-start.18 = (bf16[64,2048]{1,0:T(8,128)(2,1)S(1)}, bf16[64,2048]{1,0:T(8,128)(2,1)S(1)}, u32[]{:S(2)}, u32[]{:S(2)}) collective-permute-start(bf16[64,2048]{1,0:T(8,128)(2,1)S(1)} %collective-permute-done.16.refs_3_), channel_id=1, source_target_pairs={{0,7},{1,0},{2,1},{3,2},{4,3},{5,4},{6,5},{7,6},{8,15},{9,8},{10,9... | collective-permute-start | bytes 786440 | tf_op jit(solution)/shard_map/ppermute | solution.py:19
  75.2 3.6 %collective-permute-start.8 = (bf16[64,2048]{1,0:T(8,128)(2,1)S(1)}, bf16[64,2048]{1,0:T(8,128)(2,1)S(1)}, u32[]{:S(2)}, u32[]{:S(2)}) collective-permute-start(bf16[64,2048]{1,0:T(8,128)(2,1)S(1)} %collective-permute-done.7.refs_7_), channel_id=1, source_target_pairs={{0,7},{1,0},{2,1},{3,2},{4,3},{5,4},{6,5},{7,6},{8,15},{9,8},{10,9... | collective-permute-start | bytes 786440 | tf_op jit(solution)/shard_map/ppermute | solution.py:19
  78.7 2.5 %shard_map.55.refs_8_ = f32[2,2,8,72,256]{4,3,2,1,0:T(8,128)S(1)} custom-call(bf16[64,2048]{1,0:T(8,128)(2,1)S(1)} %pad_maximum_fusion.1.refs_0_, bf16[64,2048]{1,0:T(8,128)(2,1)S(1)} %constant_dynamic-update-slice_fusion.refs_1_, bf16[64,2048]{1,0:T(8,128)(2,1)S(1)} %collective-permute-done.1.refs_2_, bf16[64,2048]{1,0:T(8,128)(2,1)S(1)} %collective-permute-done.4.refs_3_, ...), custom_call_target="tpu_custom_call" | custom-call | flops 1342177280 | bytes 4718592 | tf_op jit(solution)/shard_map/pallas_call | solution.py:97
  81.9 3.8 %collective-permute-done.8.refs_1_ = bf16[64,2048]{1,0:T(8,128)(2,1)S(1)} collective-permute-done((bf16[64,2048]{1,0:T(8,128)(2,1)S(1)}, bf16[64,2048]{1,0:T(8,128)(2,1)S(1)}, u32[]{:S(2)}, u32[]{:S(2)}) %collective-permute-start.8) | collective-permute-done | bytes 262176 | tf_op jit(solution)/shard_map/ppermute | solution.py:19
  85.7 1.5 %shard_map.56 = f32[2,2,8,72,256]{4,3,2,1,0:T(8,128)S(1)} custom-call(bf16[64,2048]{1,0:T(8,128)(2,1)S(1)} %collective-permute-done.3.refs_0_, bf16[64,2048]{1,0:T(8,128)(2,1)S(1)} %collective-permute-done.8.refs_1_, bf16[64,2048]{1,0:T(8,128)(2,1)S(1)} %collective-permute-done.13.refs_2_, ...), custom_call_target="tpu_custom_call", output_to_operand_aliasing={{}: (8, {})} | custom-call | flops 805306368 | bytes 3670016 | tf_op jit(solution)/shard_map/pallas_call | solution.py:97
  87.3 1.9 %collective-permute-start.20 = (f32[8,72,256]{2,1,0:T(8,128)S(1)}, f32[8,72,256]{2,1,0:T(8,128)S(1)}, u32[]{:S(2)}, u32[]{:S(2)}) collective-permute-start(f32[8,72,256]{2,1,0:T(8,128)S(1)} %get-tuple-element.17), channel_id=1, source_target_pairs={{0,32},{32,0},{64,96},{96,64},{128,160},{160,128},{192,224},{224,1... | collective-permute-start | bytes 1769480 | tf_op jit(solution)/shard_map/ppermute | solution.py:185
  89.3 2.4 %collective-permute-start.19 = (f32[8,72,256]{2,1,0:T(8,128)S(1)}, f32[8,72,256]{2,1,0:T(8,128)S(1)}, u32[]{:S(2)}, u32[]{:S(2)}) collective-permute-start(f32[8,72,256]{2,1,0:T(8,128)S(1)} %get-tuple-element.18), channel_id=1, source_target_pairs={{0,32},{32,0},{64,96},{96,64},{128,160},{160,128},{192,224},{224,1... | collective-permute-start | bytes 1769480 | tf_op jit(solution)/shard_map/ppermute | solution.py:185
  91.7 1.6 %collective-permute-done.19 = f32[8,72,256]{2,1,0:T(8,128)S(1)} collective-permute-done((f32[8,72,256]{2,1,0:T(8,128)S(1)}, f32[8,72,256]{2,1,0:T(8,128)S(1)}, u32[]{:S(2)}, u32[]{:S(2)}) %collective-permute-start.19) | collective-permute-done | bytes 589856 | tf_op jit(solution)/shard_map/ppermute | solution.py:185
  94.3 15.8 %all_to_all.10.parts_ref = f32[8,72,256]{2,1,0:T(8,128)S(1)} all-to-all(f32[8,72,256]{2,1,0:T(8,128)S(1)} %get-tuple-element.15), channel_id=1, replica_groups={{0,64,128,192,256,320,384,448},{32,96,160,224,288,352,416,480},{1,65,12..., dimensions={0} | all-to-all | bytes 1179648 | tf_op jit(solution)/shard_map/all_to_all | solution.py:193
  110.1 4.7 %all-to-all-start = ((f32[8,72,256]{2,1,0:T(8,128)}), f32[8,72,256]{2,1,0:T(8,128)S(1)}, u32[]{:S(2)}, u32[]{:S(2)}) async-start(f32[8,72,256]{2,1,0:T(8,128)} %get-tuple-element.16), calls=%async_computation | async-start | bytes 1179648 | tf_op jit(solution)/shard_map/all_to_all | solution.py:194
  114.8 3.4 %collective-permute-start.21 = (f32[72,128]{1,0:T(8,128)S(1)}, f32[72,128]{1,0:T(8,128)S(1)}, u32[]{:S(2)}, u32[]{:S(2)}) collective-permute-start(f32[72,128]{1,0:T(8,128)S(1)} %get-tuple-element.13), channel_id=1, source_target_pairs={{0,8},{1,9},{2,10},{3,11},{4,12},{5,13},{6,14},{7,15},{8,16},{9,17... | collective-permute-start | bytes 110600 | tf_op jit(solution)/shard_map/ppermute | solution.py:24
  118.3 3.3 %collective-permute-start.22 = (f32[72,128]{1,0:T(8,128)S(1)}, f32[72,128]{1,0:T(8,128)S(1)}, u32[]{:S(2)}, u32[]{:S(2)}) collective-permute-start(f32[72,128]{1,0:T(8,128)S(1)} %get-tuple-element.14), channel_id=1, source_target_pairs={{0,24},{1,25},{2,26},{3,27},{4,28},{5,29},{6,30},{7,31},{8,0},{9,1... | collective-permute-start | bytes 110600 | tf_op jit(solution)/shard_map/ppermute | solution.py:24
  121.6 2.8 %all-to-all-done.parts_ref = f32[8,72,256]{2,1,0:T(8,128)S(1)} async-done(((f32[8,72,256]{2,1,0:T(8,128)}), f32[8,72,256]{2,1,0:T(8,128)S(1)}, u32[]{:S(2)}, u32[]{:S(2)}) %all-to-all-start) | async-done | bytes 589856 | tf_op jit(solution)/shard_map/all_to_all | solution.py:194
  124.4 1.9 %collective-permute-done.22.high_ref = f32[72,128]{1,0:T(8,128)S(1)} collective-permute-done((f32[72,128]{1,0:T(8,128)S(1)}, f32[72,128]{1,0:T(8,128)S(1)}, u32[]{:S(2)}, u32[]{:S(2)}) %collective-permute-start.22) | collective-permute-done | bytes 36896 | tf_op jit(solution)/shard_map/ppermute | solution.py:24
  (36 shorter events, 5.5 us)
Async XLA Ops:
  1.0 26.8 %collective-permute-start.9 = (bf16[32,2048]{1,0:T(8,128)(2,1)S(1)}, bf16[32,2048]{1,0:T(8,128)(2,1)S(1)}, u32[]{:S(2)}, u32[]{:S(2)}) collective-permute-start(bf16[32,2048]{1,0:T(8,128)(2,1)S(1)} %get-tuple-element.24), channel_id=1, source_target_pairs={{0,24},{1,25},{2,26},{3,27},{4,28},{5,29},{6,30},{7,31},{8,0},{9,1... | collective-permute-start | bytes 393224 | tf_op jit(solution)/shard_map/ppermute | solution.py:24
  5.0 10.3 %collective-permute-start = (bf16[32,2048]{1,0:T(8,128)(2,1)S(1)}, bf16[32,2048]{1,0:T(8,128)(2,1)S(1)}, u32[]{:S(2)}, u32[]{:S(2)}) collective-permute-start(bf16[32,2048]{1,0:T(8,128)(2,1)S(1)} %get-tuple-element.24), channel_id=1, source_target_pairs={{0,8},{1,9},{2,10},{3,11},{4,12},{5,13},{6,14},{7,15},{8,16},{9,17... | collective-permute-start | bytes 393224 | tf_op jit(solution)/shard_map/ppermute | solution.py:24
  9.0 18.9 %collective-permute-start.10 = (bf16[32,2048]{1,0:T(8,128)(2,1)S(1)}, bf16[32,2048]{1,0:T(8,128)(2,1)S(1)}, u32[]{:S(2)}, u32[]{:S(2)}) collective-permute-start(bf16[32,2048]{1,0:T(8,128)(2,1)S(1)} %get-tuple-element.23), channel_id=1, source_target_pairs={{0,16},{1,17},{2,18},{3,19},{4,20},{5,21},{6,22},{7,23},{8,24},{9,... | collective-permute-start | bytes 393224 | tf_op jit(solution)/shard_map/ppermute | solution.py:24
  15.4 23.0 %collective-permute-start.1 = (bf16[64,2048]{1,0:T(8,128)(2,1)S(1)}, bf16[64,2048]{1,0:T(8,128)(2,1)S(1)}, u32[]{:S(2)}, u32[]{:S(2)}) collective-permute-start(bf16[64,2048]{1,0:T(8,128)(2,1)S(1)} %pad_maximum_fusion.1.refs_0_), channel_id=1, source_target_pairs={{0,1},{1,2},{2,3},{3,4},{4,5},{5,6},{6,7},{7,0},{8,9},{9,10},{10,1... | collective-permute-start | bytes 786440 | tf_op jit(solution)/shard_map/ppermute | solution.py:19
  20.9 29.7 %collective-permute-start.5 = (bf16[2048,128]{1,0:T(8,128)(2,1)S(1)}, bf16[2048,128]{1,0:T(8,128)(2,1)S(1)}, u32[]{:S(2)}, u32[]{:S(2)}) collective-permute-start(bf16[2048,128]{1,0:T(8,128)(2,1)S(1)} %get-tuple-element.21), channel_id=1, source_target_pairs={{0,8},{1,9},{2,10},{3,11},{4,12},{5,13},{6,14},{7,15},{8,16},{9,17... | collective-permute-start | bytes 1572872 | tf_op jit(solution)/shard_map/ppermute | solution.py:24
  25.9 26.7 %collective-permute-start.6 = (bf16[2048,128]{1,0:T(8,128)(2,1)S(1)}, bf16[2048,128]{1,0:T(8,128)(2,1)S(1)}, u32[]{:S(2)}, u32[]{:S(2)}) collective-permute-start(bf16[2048,128]{1,0:T(8,128)(2,1)S(1)} %get-tuple-element.22), channel_id=1, source_target_pairs={{0,24},{1,25},{2,26},{3,27},{4,28},{5,29},{6,30},{7,31},{8,0},{9,1... | collective-permute-start | bytes 1572872 | tf_op jit(solution)/shard_map/ppermute | solution.py:24
  27.9 15.7 %collective-permute-start.14 = (bf16[64,2048]{1,0:T(8,128)(2,1)S(1)}, bf16[64,2048]{1,0:T(8,128)(2,1)S(1)}, u32[]{:S(2)}, u32[]{:S(2)}) collective-permute-start(bf16[64,2048]{1,0:T(8,128)(2,1)S(1)} %constant_dynamic-update-slice_fusion.refs_1_), channel_id=1, source_target_pairs={{0,7},{1,0},{2,1},{3,2},{4,3},{5,4},{6,5},{7,6},{8,15},{9,8},{10,9... | collective-permute-start | bytes 786440 | tf_op jit(solution)/shard_map/ppermute | solution.py:19
  36.5 9.5 %collective-permute-start.11 = (bf16[64,2048]{1,0:T(8,128)(2,1)S(1)}, bf16[64,2048]{1,0:T(8,128)(2,1)S(1)}, u32[]{:S(2)}, u32[]{:S(2)}) collective-permute-start(bf16[64,2048]{1,0:T(8,128)(2,1)S(1)} %constant_dynamic-update-slice_fusion.refs_1_), channel_id=1, source_target_pairs={{0,1},{1,2},{2,3},{3,4},{4,5},{5,6},{6,7},{7,0},{8,9},{9,10},{10,1... | collective-permute-start | bytes 786440 | tf_op jit(solution)/shard_map/ppermute | solution.py:19
  38.4 14.3 %collective-permute-start.4 = (bf16[64,2048]{1,0:T(8,128)(2,1)S(1)}, bf16[64,2048]{1,0:T(8,128)(2,1)S(1)}, u32[]{:S(2)}, u32[]{:S(2)}) collective-permute-start(bf16[64,2048]{1,0:T(8,128)(2,1)S(1)} %pad_maximum_fusion.1.refs_0_), channel_id=1, source_target_pairs={{0,7},{1,0},{2,1},{3,2},{4,3},{5,4},{6,5},{7,6},{8,15},{9,8},{10,9... | collective-permute-start | bytes 786440 | tf_op jit(solution)/shard_map/ppermute | solution.py:19
  43.6 9.5 %collective-permute-start.2 = (bf16[64,2048]{1,0:T(8,128)(2,1)S(1)}, bf16[64,2048]{1,0:T(8,128)(2,1)S(1)}, u32[]{:S(2)}, u32[]{:S(2)}) collective-permute-start(bf16[64,2048]{1,0:T(8,128)(2,1)S(1)} %collective-permute-done.1.refs_2_), channel_id=1, source_target_pairs={{0,1},{1,2},{2,3},{3,4},{4,5},{5,6},{6,7},{7,0},{8,9},{9,10},{10,1... | collective-permute-start | bytes 786440 | tf_op jit(solution)/shard_map/ppermute | solution.py:19
  45.9 9.4 %collective-permute-start.15 = (bf16[64,2048]{1,0:T(8,128)(2,1)S(1)}, bf16[64,2048]{1,0:T(8,128)(2,1)S(1)}, u32[]{:S(2)}, u32[]{:S(2)}) collective-permute-start(bf16[64,2048]{1,0:T(8,128)(2,1)S(1)} %collective-permute-done.14.refs_5_), channel_id=1, source_target_pairs={{0,7},{1,0},{2,1},{3,2},{4,3},{5,4},{6,5},{7,6},{8,15},{9,8},{10,9... | collective-permute-start | bytes 786440 | tf_op jit(solution)/shard_map/ppermute | solution.py:19
  50.6 15.1 %collective-permute-start.12 = (bf16[64,2048]{1,0:T(8,128)(2,1)S(1)}, bf16[64,2048]{1,0:T(8,128)(2,1)S(1)}, u32[]{:S(2)}, u32[]{:S(2)}) collective-permute-start(bf16[64,2048]{1,0:T(8,128)(2,1)S(1)} %collective-permute-done.11.refs_4_), channel_id=1, source_target_pairs={{0,1},{1,2},{2,3},{3,4},{4,5},{5,6},{6,7},{7,0},{8,9},{9,10},{10,1... | collective-permute-start | bytes 786440 | tf_op jit(solution)/shard_map/ppermute | solution.py:19
  53.0 15.1 %collective-permute-start.3 = (bf16[64,2048]{1,0:T(8,128)(2,1)S(1)}, bf16[64,2048]{1,0:T(8,128)(2,1)S(1)}, u32[]{:S(2)}, u32[]{:S(2)}) collective-permute-start(bf16[64,2048]{1,0:T(8,128)(2,1)S(1)} %collective-permute-done.2.refs_6_), channel_id=1, source_target_pairs={{0,1},{1,2},{2,3},{3,4},{4,5},{5,6},{6,7},{7,0},{8,9},{9,10},{10,1... | collective-permute-start | bytes 786440 | tf_op jit(solution)/shard_map/ppermute | solution.py:19
  55.3 14.7 %collective-permute-start.16 = (bf16[64,2048]{1,0:T(8,128)(2,1)S(1)}, bf16[64,2048]{1,0:T(8,128)(2,1)S(1)}, u32[]{:S(2)}, u32[]{:S(2)}) collective-permute-start(bf16[64,2048]{1,0:T(8,128)(2,1)S(1)} %collective-permute-done.15.refs_9_), channel_id=1, source_target_pairs={{0,7},{1,0},{2,1},{3,2},{4,3},{5,4},{6,5},{7,6},{8,15},{9,8},{10,9... | collective-permute-start | bytes 786440 | tf_op jit(solution)/shard_map/ppermute | solution.py:19
  61.8 13.3 %collective-permute-start.7 = (bf16[64,2048]{1,0:T(8,128)(2,1)S(1)}, bf16[64,2048]{1,0:T(8,128)(2,1)S(1)}, u32[]{:S(2)}, u32[]{:S(2)}) collective-permute-start(bf16[64,2048]{1,0:T(8,128)(2,1)S(1)} %collective-permute-done.4.refs_3_), channel_id=1, source_target_pairs={{0,7},{1,0},{2,1},{3,2},{4,3},{5,4},{6,5},{7,6},{8,15},{9,8},{10,9... | collective-permute-start | bytes 786440 | tf_op jit(solution)/shard_map/ppermute | solution.py:19
  65.8 15.5 %collective-permute-start.13 = (bf16[64,2048]{1,0:T(8,128)(2,1)S(1)}, bf16[64,2048]{1,0:T(8,128)(2,1)S(1)}, u32[]{:S(2)}, u32[]{:S(2)}) collective-permute-start(bf16[64,2048]{1,0:T(8,128)(2,1)S(1)} %collective-permute-done.12.refs_8_), channel_id=1, source_target_pairs={{0,1},{1,2},{2,3},{3,4},{4,5},{5,6},{6,7},{7,0},{8,9},{9,10},{10,1... | collective-permute-start | bytes 786440 | tf_op jit(solution)/shard_map/ppermute | solution.py:19
  68.1 13.6 %collective-permute-start.17 = (bf16[64,2048]{1,0:T(8,128)(2,1)S(1)}, bf16[64,2048]{1,0:T(8,128)(2,1)S(1)}, u32[]{:S(2)}, u32[]{:S(2)}) collective-permute-start(bf16[64,2048]{1,0:T(8,128)(2,1)S(1)} %collective-permute-done.3.refs_0_), channel_id=1, source_target_pairs={{0,1},{1,2},{2,3},{3,4},{4,5},{5,6},{6,7},{7,0},{8,9},{9,10},{10,1... | collective-permute-start | bytes 786440 | tf_op jit(solution)/shard_map/ppermute | solution.py:19
  70.0 11.9 %collective-permute-start.18 = (bf16[64,2048]{1,0:T(8,128)(2,1)S(1)}, bf16[64,2048]{1,0:T(8,128)(2,1)S(1)}, u32[]{:S(2)}, u32[]{:S(2)}) collective-permute-start(bf16[64,2048]{1,0:T(8,128)(2,1)S(1)} %collective-permute-done.16.refs_3_), channel_id=1, source_target_pairs={{0,7},{1,0},{2,1},{3,2},{4,3},{5,4},{6,5},{7,6},{8,15},{9,8},{10,9... | collective-permute-start | bytes 786440 | tf_op jit(solution)/shard_map/ppermute | solution.py:19
  75.2 10.5 %collective-permute-start.8 = (bf16[64,2048]{1,0:T(8,128)(2,1)S(1)}, bf16[64,2048]{1,0:T(8,128)(2,1)S(1)}, u32[]{:S(2)}, u32[]{:S(2)}) collective-permute-start(bf16[64,2048]{1,0:T(8,128)(2,1)S(1)} %collective-permute-done.7.refs_7_), channel_id=1, source_target_pairs={{0,7},{1,0},{2,1},{3,2},{4,3},{5,4},{6,5},{7,6},{8,15},{9,8},{10,9... | collective-permute-start | bytes 786440 | tf_op jit(solution)/shard_map/ppermute | solution.py:19
  87.3 4.3 %collective-permute-start.20 = (f32[8,72,256]{2,1,0:T(8,128)S(1)}, f32[8,72,256]{2,1,0:T(8,128)S(1)}, u32[]{:S(2)}, u32[]{:S(2)}) collective-permute-start(f32[8,72,256]{2,1,0:T(8,128)S(1)} %get-tuple-element.17), channel_id=1, source_target_pairs={{0,32},{32,0},{64,96},{96,64},{128,160},{160,128},{192,224},{224,1... | collective-permute-start | bytes 1769480 | tf_op jit(solution)/shard_map/ppermute | solution.py:185
  89.3 4.0 %collective-permute-start.19 = (f32[8,72,256]{2,1,0:T(8,128)S(1)}, f32[8,72,256]{2,1,0:T(8,128)S(1)}, u32[]{:S(2)}, u32[]{:S(2)}) collective-permute-start(f32[8,72,256]{2,1,0:T(8,128)S(1)} %get-tuple-element.18), channel_id=1, source_target_pairs={{0,32},{32,0},{64,96},{96,64},{128,160},{160,128},{192,224},{224,1... | collective-permute-start | bytes 1769480 | tf_op jit(solution)/shard_map/ppermute | solution.py:185
  94.2 32.0 %copy-start = (s32[1,2]{1,0:T(1,128)S(1)}, s32[1,2]{1,0:T(1,128)}, u32[]{:S(2)}) copy-start(s32[1,2]{1,0:T(1,128)} %cutoff_ref.1) | copy-start | bytes 28
  94.2 32.0 %copy-start.1 = (s32[1,2]{1,0:T(1,128)S(1)}, s32[1,2]{1,0:T(1,128)}, u32[]{:S(2)}) copy-start(s32[1,2]{1,0:T(1,128)} %index_ref.1) | copy-start | bytes 28
  94.2 32.0 %copy-start.2 = (f32[8]{0:T(128)S(1)}, f32[8]{0:T(128)}, u32[]{:S(2)}) copy-start(f32[8]{0:T(128)} %table_ref.1) | copy-start | bytes 100
  110.1 14.3 %all-to-all-start = ((f32[8,72,256]{2,1,0:T(8,128)}), f32[8,72,256]{2,1,0:T(8,128)S(1)}, u32[]{:S(2)}, u32[]{:S(2)}) async-start(f32[8,72,256]{2,1,0:T(8,128)} %get-tuple-element.16), calls=%async_computation | async-start | bytes 1179648 | tf_op jit(solution)/shard_map/all_to_all | solution.py:194
  114.8 9.5 %collective-permute-start.21 = (f32[72,128]{1,0:T(8,128)S(1)}, f32[72,128]{1,0:T(8,128)S(1)}, u32[]{:S(2)}, u32[]{:S(2)}) collective-permute-start(f32[72,128]{1,0:T(8,128)S(1)} %get-tuple-element.13), channel_id=1, source_target_pairs={{0,8},{1,9},{2,10},{3,11},{4,12},{5,13},{6,14},{7,15},{8,16},{9,17... | collective-permute-start | bytes 110600 | tf_op jit(solution)/shard_map/ppermute | solution.py:24
  118.3 8.0 %collective-permute-start.22 = (f32[72,128]{1,0:T(8,128)S(1)}, f32[72,128]{1,0:T(8,128)S(1)}, u32[]{:S(2)}, u32[]{:S(2)}) collective-permute-start(f32[72,128]{1,0:T(8,128)S(1)} %get-tuple-element.14), channel_id=1, source_target_pairs={{0,24},{1,25},{2,26},{3,27},{4,28},{5,29},{6,30},{7,31},{8,0},{9,1... | collective-permute-start | bytes 110600 | tf_op jit(solution)/shard_map/ppermute | solution.py:24
